TPU v7x, 32 devices: a whole 2x2x4 slice. The times are simulated.
32 devices in a mesh: fsdp: 16 (over z, y, x), rep: 2 (over core).
Axes of the slice: x: 2, y: 2, z: 4, core: 2. Of those that a mesh axis runs over, the one named last changes fastest.
Arguments:
- tokens: bfloat16 [2, 64, 512, 768], P(None, ('fsdp', 'rep')), may hold values from -6 to 6
- masked: int32 [2, 64, 512], P(None, ('fsdp', 'rep')), may hold values from 0 to 1, as said below
- cotangent: bfloat16 [2, 64, 512, 768], P(None, ('fsdp', 'rep')), may hold values from -6 to 6
- mask_vector: bfloat16 [768], P('fsdp'), may hold values from -6 to 6
- heads_weight: bfloat16 [768, 2304], P('fsdp'), may hold values from -0.21875 to 0.21875
- query_bias: bfloat16 [768], P('fsdp'), may hold values from -3 to 3
- value_bias: bfloat16 [768], P('fsdp'), may hold values from -3 to 3
- output_weight: bfloat16 [768, 768], P('fsdp'), may hold values from -0.875 to 0.875
- output_bias: bfloat16 [768], P('fsdp'), may hold values from -3 to 3
- first_gain: bfloat16 [768], P('fsdp'), may hold values from 0.5 to 1.5
- first_shift: bfloat16 [768], P('fsdp'), may hold values from -3 to 3
- expand_weight: bfloat16 [768, 3072], P('fsdp'), may hold values from -0.21875 to 0.21875
- expand_bias: bfloat16 [3072], P('fsdp'), may hold values from -3 to 3
- reduce_weight: bfloat16 [3072, 768], P('fsdp'), may hold values from -0.109375 to 0.109375
- reduce_bias: bfloat16 [768], P('fsdp'), may hold values from -3 to 3
- second_gain: bfloat16 [768], P('fsdp'), may hold values from 0.5 to 1.5
- second_shift: bfloat16 [768], P('fsdp'), may hold values from -3 to 3
Outputs:
- outputs: bfloat16 [2, 64, 512, 768], P(None, ('fsdp', 'rep'))
- grad_tokens: bfloat16 [2, 64, 512, 768], P(None, ('fsdp', 'rep'))
- grad_mask_vector: float32 [768], P('fsdp')
- grad_heads_weight: float32 [768, 2304], P('fsdp')
- grad_query_bias: float32 [768], P('fsdp')
- grad_value_bias: float32 [768], P('fsdp')
- grad_output_weight: float32 [768, 768], P('fsdp')
- grad_output_bias: float32 [768], P('fsdp')
- grad_first_gain: float32 [768], P('fsdp')
- grad_first_shift: float32 [768], P('fsdp')
- grad_expand_weight: float32 [768, 3072], P('fsdp')
- grad_expand_bias: float32 [3072], P('fsdp')
- grad_reduce_weight: float32 [3072, 768], P('fsdp')
- grad_reduce_bias: float32 [768], P('fsdp')
- grad_second_gain: float32 [768], P('fsdp')
- grad_second_shift: float32 [768], P('fsdp')
Inputs may be any that keep to these rules, and one draw needn't show every extreme that they name: 1 marks a masked position; masked positions come in runs of consecutive positions, and the share of masked positions differs from sequence to sequence.
All inputs are finite; a program needn't handle non-finite values.
Results may differ from a plain program's by a relative error of at most 0.022.
Values may be sent and summed in bfloat16 or wider, within the bound.
No kernel may reach another device: no remote copies, remote signals or barrier semaphores. Data moves between devices by JAX's collectives and lax.ppermute only.
A program may use at most 256 MiB of HBM per device.

v0:
```python
import jax
import jax.numpy as jnp
from jax import lax
from jax.sharding import PartitionSpec as P

HEADS = 12


epsilon = 1e-06


def layer_norm(values, scaling, offset):
    centred = values - jnp.mean(values, axis=-1, keepdims=True)
    spread = jnp.mean(centred * centred, axis=-1, keepdims=True)
    return centred * lax.rsqrt(spread + epsilon) * scaling + offset


def exact_gelu(values):
    return jax.nn.gelu(values, approximate=False)


def norm_back(values, scaling, incoming):

    def scaled(inner_values, weight):
        return layer_norm(inner_values, weight, 0.0)

    _, pullback = jax.vjp(scaled, values, scaling.astype(jnp.float32))
    grad_values, grad_scaling = pullback(incoming)
    return (grad_values, grad_scaling, jnp.sum(incoming, axis=0))


def split_heads(block):
    length, features = block.shape
    return block.reshape(length, HEADS, features // HEADS)


def attend_one(triple):
    queries, key_rows, value_rows = triple
    factor = (queries.shape[-1] // HEADS) ** (-0.5)
    scores = (
        jnp.einsum(
            "qhd,khd->hqk",
            split_heads(queries),
            split_heads(key_rows),
            preferred_element_type=jnp.float32,
        )
        * factor
    )
    row_max = jnp.max(scores, axis=-1, keepdims=True)
    raised = jnp.exp(scores - row_max)
    row_total = jnp.sum(raised, axis=-1, keepdims=True)
    probs_low = (raised / row_total).astype(jnp.bfloat16)
    context = jnp.einsum(
        "hqk,khd->qhd", probs_low, split_heads(value_rows), preferred_element_type=jnp.float32
    )
    return (context.reshape(queries.shape).astype(jnp.bfloat16), row_max + jnp.log(row_total))


def attend_back(quintet):
    queries, key_rows, value_rows, summit, grad_context = quintet
    factor = (queries.shape[-1] // HEADS) ** (-0.5)
    heads_query = split_heads(queries)
    heads_keys = split_heads(key_rows)
    scores = (
        jnp.einsum("qhd,khd->hqk", heads_query, heads_keys, preferred_element_type=jnp.float32)
        * factor
    )
    probs = jnp.exp(scores - summit)
    probs_low = probs.astype(jnp.bfloat16)
    grad_heads = split_heads(grad_context)
    grad_values = jnp.einsum(
        "hqk,qhd->khd", probs_low, grad_heads, preferred_element_type=jnp.float32
    )
    grad_probs = jnp.einsum(
        "qhd,khd->hqk", grad_heads, split_heads(value_rows), preferred_element_type=jnp.float32
    )
    inner_sum = jnp.sum(grad_probs * probs, axis=-1, keepdims=True)
    grad_scores = (probs * (grad_probs - inner_sum)).astype(jnp.bfloat16)
    grad_queries = (
        jnp.einsum("hqk,khd->qhd", grad_scores, heads_keys, preferred_element_type=jnp.float32)
        * factor
    )
    grad_keys = (
        jnp.einsum("hqk,qhd->khd", grad_scores, heads_query, preferred_element_type=jnp.float32)
        * factor
    )
    layout = queries.shape
    return jnp.concatenate(
        [
            grad_queries.reshape(layout).astype(jnp.bfloat16),
            grad_keys.reshape(layout).astype(jnp.bfloat16),
            grad_values.reshape(layout).astype(jnp.bfloat16),
        ],
        axis=-1,
    )


def forward_pass(gathered, tokens, masked):
    (
        mask_vector,
        heads_weight,
        query_bias,
        value_bias,
        output_weight,
        output_bias,
        first_gain,
        first_shift,
        expand_weight,
        expand_bias,
        reduce_weight,
        reduce_bias,
        second_gain,
        second_shift,
    ) = gathered
    sequences, length, features = tokens.shape
    chosen = masked.reshape(-1, 1) == 1
    inputs = jnp.where(chosen, mask_vector[None, :], tokens.reshape(-1, features))
    projected = jnp.dot(inputs, heads_weight, preferred_element_type=jnp.float32)
    queries = (projected[:, :features] + query_bias.astype(jnp.float32)).astype(jnp.bfloat16)
    key_rows = projected[:, features : 2 * features].astype(jnp.bfloat16)
    value_rows = (projected[:, 2 * features :] + value_bias.astype(jnp.float32)).astype(
        jnp.bfloat16
    )
    layout = (sequences, length, features)
    folded = (queries.reshape(layout), key_rows.reshape(layout), value_rows.reshape(layout))
    context, summit = lax.map(attend_one, folded)
    context = context.reshape(-1, features)
    branch = jnp.dot(
        context, output_weight, preferred_element_type=jnp.float32
    ) + output_bias.astype(jnp.float32)
    first_sum = inputs.astype(jnp.float32) + branch
    normed = layer_norm(first_sum, first_gain.astype(jnp.float32), first_shift.astype(jnp.float32))
    normed_low = normed.astype(jnp.bfloat16)
    hidden = jnp.dot(
        normed_low, expand_weight, preferred_element_type=jnp.float32
    ) + expand_bias.astype(jnp.float32)
    active = exact_gelu(hidden).astype(jnp.bfloat16)
    second_sum = normed + (
        jnp.dot(active, reduce_weight, preferred_element_type=jnp.float32)
        + reduce_bias.astype(jnp.float32)
    )
    outputs = layer_norm(
        second_sum, second_gain.astype(jnp.float32), second_shift.astype(jnp.float32)
    )
    stored = (
        chosen,
        inputs,
        folded,
        summit,
        context,
        first_sum,
        normed_low,
        hidden,
        active,
        second_sum,
    )
    return (outputs.astype(jnp.bfloat16).reshape(tokens.shape), stored)


def backward_pass(needed, stored, cotangent):
    heads_weight, output_weight, first_gain, expand_weight, reduce_weight, second_gain = needed
    chosen, inputs, folded, summit, context, first_sum, normed_low, hidden, active, second_sum = (
        stored
    )
    sequences, length, features = folded[0].shape
    upstream = jnp.where(chosen, cotangent.reshape(-1, features).astype(jnp.float32), 0.0)
    grad_outer, grad_second_gain, grad_second_shift = norm_back(second_sum, second_gain, upstream)
    grad_second = grad_outer.astype(jnp.bfloat16)
    grad_reduce_bias = jnp.sum(grad_second.astype(jnp.float32), axis=0)
    grad_reduce_weight = jnp.dot(active.T, grad_second, preferred_element_type=jnp.float32)
    _, gelu_pull = jax.vjp(exact_gelu, hidden)
    grad_active = jnp.dot(grad_second, reduce_weight.T, preferred_element_type=jnp.float32)
    grad_hidden = gelu_pull(grad_active)[0].astype(jnp.bfloat16)
    grad_expand_bias = jnp.sum(grad_hidden.astype(jnp.float32), axis=0)
    grad_expand_weight = jnp.dot(normed_low.T, grad_hidden, preferred_element_type=jnp.float32)
    grad_normed = grad_outer + jnp.dot(
        grad_hidden, expand_weight.T, preferred_element_type=jnp.float32
    )
    grad_inner, grad_first_gain, grad_first_shift = norm_back(first_sum, first_gain, grad_normed)
    grad_branch = grad_inner.astype(jnp.bfloat16)
    grad_output_bias = jnp.sum(grad_branch.astype(jnp.float32), axis=0)
    grad_output_weight = jnp.dot(context.T, grad_branch, preferred_element_type=jnp.float32)
    grad_context = jnp.dot(grad_branch, output_weight.T, preferred_element_type=jnp.float32).astype(
        jnp.bfloat16
    )
    quintet = (
        folded[0],
        folded[1],
        folded[2],
        summit,
        grad_context.reshape(sequences, length, features),
    )
    grad_mixed = lax.map(attend_back, quintet).reshape(-1, 3 * features)
    column_sums = jnp.sum(grad_mixed.astype(jnp.float32), axis=0)
    grad_query_bias = column_sums[:features]
    grad_value_bias = column_sums[2 * features :]
    grad_heads_weight = jnp.dot(inputs.T, grad_mixed, preferred_element_type=jnp.float32)
    grad_rows = grad_inner + jnp.dot(grad_mixed, heads_weight.T, preferred_element_type=jnp.float32)
    grad_mask_vector = jnp.sum(jnp.where(chosen, grad_rows, 0.0), axis=0)
    grad_input = (
        jnp.where(chosen, 0.0, grad_rows).astype(jnp.bfloat16).reshape(sequences, length, features)
    )
    terms = (
        grad_mask_vector,
        grad_heads_weight,
        grad_query_bias,
        grad_value_bias,
        grad_output_weight,
        grad_output_bias,
        grad_first_gain,
        grad_first_shift,
        grad_expand_weight,
        grad_expand_bias,
        grad_reduce_weight,
        grad_reduce_bias,
        grad_second_gain,
        grad_second_shift,
    )
    return (grad_input, terms)


def local(
    tokens,
    masked,
    cotangent,
    mask_vector,
    heads_weight,
    query_bias,
    value_bias,
    output_weight,
    output_bias,
    first_gain,
    first_shift,
    expand_weight,
    expand_bias,
    reduce_weight,
    reduce_bias,
    second_gain,
    second_shift,
):
    totals = None
    results = []
    grad_inputs = []
    for batch_index in range(tokens.shape[0]):
        gathered = (
            lax.all_gather(mask_vector, "fsdp", axis=0, tiled=True),
            lax.all_gather(heads_weight, "fsdp", axis=0, tiled=True),
            lax.all_gather(query_bias, "fsdp", axis=0, tiled=True),
            lax.all_gather(value_bias, "fsdp", axis=0, tiled=True),
            lax.all_gather(output_weight, "fsdp", axis=0, tiled=True),
            lax.all_gather(output_bias, "fsdp", axis=0, tiled=True),
            lax.all_gather(first_gain, "fsdp", axis=0, tiled=True),
            lax.all_gather(first_shift, "fsdp", axis=0, tiled=True),
            lax.all_gather(expand_weight, "fsdp", axis=0, tiled=True),
            lax.all_gather(expand_bias, "fsdp", axis=0, tiled=True),
            lax.all_gather(reduce_weight, "fsdp", axis=0, tiled=True),
            lax.all_gather(reduce_bias, "fsdp", axis=0, tiled=True),
            lax.all_gather(second_gain, "fsdp", axis=0, tiled=True),
            lax.all_gather(second_shift, "fsdp", axis=0, tiled=True),
        )
        outputs, stored = forward_pass(gathered, tokens[batch_index], masked[batch_index])
        needed = (
            lax.all_gather(heads_weight, "fsdp", axis=0, tiled=True),
            lax.all_gather(output_weight, "fsdp", axis=0, tiled=True),
            lax.all_gather(first_gain, "fsdp", axis=0, tiled=True),
            lax.all_gather(expand_weight, "fsdp", axis=0, tiled=True),
            lax.all_gather(reduce_weight, "fsdp", axis=0, tiled=True),
            lax.all_gather(second_gain, "fsdp", axis=0, tiled=True),
        )
        grad_input, terms = backward_pass(needed, stored, cotangent[batch_index])
        totals = terms if totals is None else jax.tree.map(jnp.add, totals, terms)
        results.append(outputs)
        grad_inputs.append(grad_input)
    summed = (
        lax.psum_scatter(totals[0], "fsdp", scatter_dimension=0, tiled=True),
        lax.psum_scatter(totals[1], "fsdp", scatter_dimension=0, tiled=True),
        lax.psum_scatter(totals[2], "fsdp", scatter_dimension=0, tiled=True),
        lax.psum_scatter(totals[3], "fsdp", scatter_dimension=0, tiled=True),
        lax.psum_scatter(totals[4], "fsdp", scatter_dimension=0, tiled=True),
        lax.psum_scatter(totals[5], "fsdp", scatter_dimension=0, tiled=True),
        lax.psum_scatter(totals[6], "fsdp", scatter_dimension=0, tiled=True),
        lax.psum_scatter(totals[7], "fsdp", scatter_dimension=0, tiled=True),
        lax.psum_scatter(totals[8], "fsdp", scatter_dimension=0, tiled=True),
        lax.psum_scatter(totals[9], "fsdp", scatter_dimension=0, tiled=True),
        lax.psum_scatter(totals[10], "fsdp", scatter_dimension=0, tiled=True),
        lax.psum_scatter(totals[11], "fsdp", scatter_dimension=0, tiled=True),
        lax.psum_scatter(totals[12], "fsdp", scatter_dimension=0, tiled=True),
        lax.psum_scatter(totals[13], "fsdp", scatter_dimension=0, tiled=True),
    )
    shares = (
        lax.psum(summed[0].astype(jnp.bfloat16), "rep").astype(jnp.float32),
        lax.psum(summed[1].astype(jnp.bfloat16), "rep").astype(jnp.float32),
        lax.psum(summed[2].astype(jnp.bfloat16), "rep").astype(jnp.float32),
        lax.psum(summed[3].astype(jnp.bfloat16), "rep").astype(jnp.float32),
        lax.psum(summed[4].astype(jnp.bfloat16), "rep").astype(jnp.float32),
        lax.psum(summed[5].astype(jnp.bfloat16), "rep").astype(jnp.float32),
        lax.psum(summed[6].astype(jnp.bfloat16), "rep").astype(jnp.float32),
        lax.psum(summed[7].astype(jnp.bfloat16), "rep").astype(jnp.float32),
        lax.psum(summed[8].astype(jnp.bfloat16), "rep").astype(jnp.float32),
        lax.psum(summed[9].astype(jnp.bfloat16), "rep").astype(jnp.float32),
        lax.psum(summed[10].astype(jnp.bfloat16), "rep").astype(jnp.float32),
        lax.psum(summed[11].astype(jnp.bfloat16), "rep").astype(jnp.float32),
        lax.psum(summed[12].astype(jnp.bfloat16), "rep").astype(jnp.float32),
        lax.psum(summed[13].astype(jnp.bfloat16), "rep").astype(jnp.float32),
    )
    return (
        jnp.stack(results),
        jnp.stack(grad_inputs),
        shares[0],
        shares[1],
        shares[2],
        shares[3],
        shares[4],
        shares[5],
        shares[6],
        shares[7],
        shares[8],
        shares[9],
        shares[10],
        shares[11],
        shares[12],
        shares[13],
    )


def solution(mesh):
    in_specs = (
        P(None, ("fsdp", "rep"), None, None),
        P(None, ("fsdp", "rep"), None),
        P(None, ("fsdp", "rep"), None, None),
        P("fsdp"),
        P("fsdp", None),
        P("fsdp"),
        P("fsdp"),
        P("fsdp", None),
        P("fsdp"),
        P("fsdp"),
        P("fsdp"),
        P("fsdp", None),
        P("fsdp"),
        P("fsdp", None),
        P("fsdp"),
        P("fsdp"),
        P("fsdp"),
    )
    out_specs = (
        P(None, ("fsdp", "rep"), None, None),
        P(None, ("fsdp", "rep"), None, None),
        P("fsdp"),
        P("fsdp", None),
        P("fsdp"),
        P("fsdp"),
        P("fsdp", None),
        P("fsdp"),
        P("fsdp"),
        P("fsdp"),
        P("fsdp", None),
        P("fsdp"),
        P("fsdp", None),
        P("fsdp"),
        P("fsdp"),
        P("fsdp"),
    )
    return jax.shard_map(local, mesh=mesh, in_specs=in_specs, out_specs=out_specs, check_vma=False)
```

profile of v0, /device:TPU:0, one launch (start us, length us, event | category | flops | bytes accessed | tf_op | source)
XLA Modules:
  0.0 1207.9 jit_solution(13710309623490252691)
XLA Ops:
  21.8 79.3 %all-reduce.21 = (bf16[768]{0:T(1024)(128)(2,1)S(1)}, bf16[768]{0:T(1024)(128)(2,1)S(1)}, bf16[768]{0:T(1024)(128)(2,1)S(1)}, bf16[768]{0:T(1024)(128)(2,1)S(1)}...) all-reduce(bf16[768]{0:T(1024)(128)(2,1)S(1)} %dynamic-update-slice, ...), channel_id=1, replica_groups=mesh['fsdp'=16,'rep'=2] {'fsdp'}, use_global_device_ids=true, to_apply=%add | all-reduce | flops 9984 | bytes 39936
  104.7 3.3 broadcast_select_fusion
  109.1 7.0 fusion.72
  117.4 3.8 fusion.73
  122.5 3.0 fusion.40
  127.3 2.6 copy.90
  130.0 2.6 copy.91
  133.8 19.4 %while.44 = (s32[]{:T(128)}, bf16[2,512,768]{2,1,0:T(8,128)(2,1)}, f32[2,12,512,1]{2,1,3,0:T(8,128)S(1)}, bf16[2,512,768]{1,2,0:T(8,128)(2,1)S(1)}, bf16[2,512,7...) while((s32[]{:T(128)}, bf16[2,512,768]{2,1,0:T(8,128)(2,1)}, ...), condition=%wide.region_3.4_spmd, body=%wide.region_0.3_spmd.sunk | while | flops 834004992 | bytes 48980568 | solution.py:126
  139.5 2.8 fusion.186
  149.1 2.8 fusion.186
  153.1 4.4 fusion.66
  161.0 2.6 copy.94
  163.6 2.6 copy.95
  167.5 19.6 %while.45 = (s32[]{:T(128)}, bf16[2,512,768]{2,1,0:T(8,128)(2,1)}, f32[2,12,512,1]{2,1,3,0:T(8,128)S(1)}, bf16[2,512,768]{1,2,0:T(8,128)(2,1)S(1)}, bf16[2,512,7...) while((s32[]{:T(128)}, bf16[2,512,768]{2,1,0:T(8,128)(2,1)}, ...), condition=%wide.region_11.12_spmd, body=%wide.region_8.11_spmd.sunk | while | flops 834004992 | bytes 48980568 | solution.py:126
  173.4 2.8 fusion.191
  183.0 2.8 fusion.191
  187.0 4.4 fusion.67
  193.1 32.3 %all-gather.9.cloned.1.call-done = bf16[768,3072]{1,0:T(8,128)(2,1)} async-done(((bf16[48,3072]{1,0:T(8,128)(2,1)}), bf16[768,3072]{1,0:T(8,128)(2,1)}) %all-gather.9.cloned.1.call-update) | async-done | bytes 4718608 | tf_op jit(solution)/shard_map/all_gather | solution.py:254
  225.5 8.3 fusion.53
  233.8 4.5 copy-done.86
  238.3 63.3 %multiply_convert_fusion.7 = (bf16[1024,3072]{1,0:T(8,128)(2,1)}, f32[1024,3072]{1,0:T(8,128)}, bf16[1024,3072]{1,0:T(8,128)(2,1)}, f32[1024,3072]{1,0:T(8,128)}, f32[1024,3072]{1,0:T(8,128)}) fusion(f32[3072]{0:T(1024)S(1)} %copy-done.74, f32[1024,3072]{1,0:T(8,128)S(1)} %fusion.53, bf16[768,3072]{1,0:T(8,128)(2,1)S(1)} %copy-done.82, ...), kind=kOutput, calls=%fused_computation.81 | convolution fusion | flops 5251006464 | bytes 70805504 | tf_op jit(solution)/shard_map/dot_general | solution.py:134
  301.7 5.6 all-gather.11.cloned.1.call-done
  307.3 9.7 fusion.69
  317.6 5.4 fusion.68
  324.9 3.6 multiply_reduce_fusion.5
  328.5 4.7 fusion.62
  337.5 18.8 %convert_reduce_fusion = (f32[3072]{0:T(1024)}, bf16[1024,3072]{1,0:T(8,128)(2,1)}) fusion(f32[1024,3072]{1,0:T(8,128)} %get-tuple-element.392, bf16[1024,768]{1,0:T(8,128)(2,1)} %get-tuple-element.341, bf16[3072,768]{1,0:T(8,128)(2,1)} %all-gather.11.cloned.1.call-done, f32[1024,3072]{1,0:T(8,128)} %copy-done.86, f32[3072]{0:T(1024)S(1)} %copy-done.74), kind=kOutput, calls=%fused_computation.64 | convolution fusion | flops 4885312512 | bytes 37773312 | tf_op jit(solution)/shard_map/dot_general | solution.py:172
  356.3 10.1 add_add_fusion.9
  366.4 18.9 %convert_reduce_fusion.1 = (f32[3072]{0:T(1024)}, bf16[1024,3072]{1,0:T(8,128)(2,1)}) fusion(f32[1024,3072]{1,0:T(8,128)} %get-tuple-element.357, bf16[1024,768]{1,0:T(8,128)(2,1)} %get-tuple-element.343, bf16[3072,768]{1,0:T(8,128)(2,1)} %all-gather.11.cloned.1.call-done, f32[1024,3072]{1,0:T(8,128)} %get-tuple-element.410, f32[3072]{0:T(1024)S(1)} %copy-done.74), kind=kOutput, calls=%fused_computation.65 | convolution fusion | flops 4885312512 | bytes 37773312 | tf_op jit(solution)/shard_map/dot_general | solution.py:172
  385.3 12.2 %multiply_reduce_fusion.7 = (f32[768]{0:T(1024)}, f32[1024]{0:T(1024)S(1)}, f32[768]{0:T(1024)}, f32[768]{0:T(1024)}, f32[1024]{0:T(1024)S(1)}, /*index=5*/f32[768]{0:T(1024)}, f32[1024,768]{1,0:T(8,128)S(1)}) fusion(f32[1024,768]{1,0:T(8,128)S(1)} %copy-done.5, f32[1024]{0:T(1024)S(1)} %fusion.48, f32[1024]{0:T(1024)S(1)} %broadcast_multiply_fusion.3, ...), kind=kOutput, calls=%fused_computation.126 | convolution fusion | flops 4845987840 | bytes 26782720 | tf_op jit(solution)/shard_map/dot_general | solution.py:176
  397.6 2.9 fusion.59
  406.7 2.9 convolution_add_fusion.3
  409.7 2.6 convolution_convert_fusion.1
  414.8 75.2 %while.46 = (s32[]{:T(128)}, bf16[2,512,2304]{1,2,0:T(8,128)(2,1)}, bf16[2,512,768]{1,2,0:T(8,128)(2,1)}, bf16[2,512,768]{1,2,0:T(8,128)(2,1)}, f32[2,12,512,1]{...) while((s32[]{:T(128)}, bf16[2,512,2304]{1,2,0:T(8,128)(2,1)}, ...), condition=%wide.region_22.23_spmd, body=%wide.region_20.22_spmd.sunk | while | flops 2060052480 | bytes 165323504 | solution.py:193
  416.8 6.4 fusion.202
  425.6 10.7 multiply_reduce_fusion.22
  438.4 6.9 multiply_convert_fusion.14
  454.5 6.4 fusion.202
  463.3 10.6 multiply_reduce_fusion.22
  475.9 6.9 multiply_convert_fusion.14
  489.9 4.3 convolution_convert_fusion
  494.3 2.5 broadcast.361.clone
  496.8 75.1 %while.47 = (s32[]{:T(128)}, bf16[2,512,2304]{1,2,0:T(8,128)(2,1)}, bf16[2,512,768]{1,2,0:T(8,128)(2,1)}, bf16[2,512,768]{1,2,0:T(8,128)(2,1)}, f32[2,12,512,1]{...) while((s32[]{:T(128)}, bf16[2,512,2304]{1,2,0:T(8,128)(2,1)}, ...), condition=%wide.region_29.30_spmd, body=%wide.region_27.29_spmd.sunk | while | flops 2060052480 | bytes 165323504 | solution.py:193
  498.9 6.4 fusion.215
  507.7 10.7 multiply_reduce_fusion.23
  520.4 6.9 multiply_convert_fusion.17
  536.4 6.4 fusion.215
  545.2 10.6 multiply_reduce_fusion.23
  557.8 6.9 multiply_convert_fusion.17
  571.9 6.7 copy.101
  578.6 7.1 copy.106
  585.7 6.5 fusion.74
  592.3 6.2 convolution_add_fusion
  599.9 7.4 fusion.76
  607.3 10.7 convolution_add_fusion.1
  620.0 8.4 fusion.55
  628.5 11.2 convolution_add_fusion.2
  642.7 8.8 select_convert_fusion.1
  653.5 3.9 select_convert_fusion
  660.0 88.6 %reduce-scatter.5.cloned.1.call-done = f32[48,2304]{1,0:T(8,128)} async-done(((f32[768,2304]{1,0:T(8,128)}), f32[48,2304]{1,0:T(8,128)}) %reduce-scatter.5.cloned.1.call-update) | async-done | bytes 442384 | tf_op jit(solution)/shard_map/reduce_scatter | solution.py:276
  750.4 174.9 %reduce-scatter.11.cloned.1.call-done = f32[192,768]{1,0:T(8,128)} async-done(((f32[3072,768]{1,0:T(8,128)}), f32[192,768]{1,0:T(8,128)}) %reduce-scatter.11.cloned.1.call-update) | async-done | bytes 589840 | tf_op jit(solution)/shard_map/reduce_scatter | solution.py:285
  927.1 173.9 %reduce-scatter.9.cloned.1.call-done = f32[48,3072]{1,0:T(8,128)} async-done(((f32[768,3072]{1,0:T(8,128)}), f32[48,3072]{1,0:T(8,128)}) %reduce-scatter.9.cloned.1.call-update) | async-done | bytes 589840 | tf_op jit(solution)/shard_map/reduce_scatter | solution.py:283
  1102.8 3.0 convert_reduce_fusion.2
  1105.9 75.0 %all-reduce.20 = (bf16[768]{0:T(1024)(128)(2,1)S(1)}, bf16[768]{0:T(1024)(128)(2,1)S(1)}, bf16[768]{0:T(1024)(128)(2,1)S(1)}, bf16[768]{0:T(1024)(128)(2,1)S(1)}...) all-reduce(f32[768]{0:T(1024)S(1)} %add.339, ...), channel_id=2, replica_groups=mesh['fsdp'=16,'rep'=2] {'fsdp'}, use_global_device_ids=true, to_apply=%region_32.33.clone | all-reduce | flops 9984 | bytes 59904
  (431 shorter events, 160.9 us)
Async XLA Ops:
  7.2 101.9 %all-gather.5.cloned.1.call-start = ((), (), s32[]{:S(2)}) async-start(), calls=%async_computation.4 | async-start | bytes 3760128 | tf_op jit(solution)/shard_map/all_gather | solution.py:247
  7.9 145.2 %all-gather.7.cloned.1.call-start = ((), (), s32[]{:S(2)}) async-start(), calls=%async_computation.5 | async-start | bytes 1253376 | tf_op jit(solution)/shard_map/all_gather | solution.py:250
  8.7 216.8 %all-gather.9.cloned.1.call-start = ((), (), s32[]{:S(2)}) async-start(), calls=%async_computation.6 | async-start | bytes 5013504 | tf_op jit(solution)/shard_map/all_gather | solution.py:254
  9.4 297.9 %all-gather.11.cloned.1.call-start = ((), (), s32[]{:S(2)}) async-start(), calls=%async_computation.7 | async-start | bytes 5013504 | tf_op jit(solution)/shard_map/all_gather | solution.py:256
  10.0 648.5 %reduce-scatter.7.cloned.1.call-start = ((), (), s32[]{:S(2)}) async-start(), calls=%async_computation.9 | async-start | bytes 2506752 | tf_op jit(solution)/shard_map/reduce_scatter | solution.py:279
  13.4 94.6 %copy-start.53 = (pred[1,2,512]{2,1,0:T(4,128)(4,1)}, pred[1,2,512]{2,1,0:T(4,128)(4,1)S(1)}, u32[]{:S(2)}) copy-start(pred[1,2,512]{2,1,0:T(4,128)(4,1)S(1)} %get-tuple-element.395) | copy-start | bytes 3076
  13.4 94.6 %copy-start.55 = (pred[1,2,512]{2,1,0:T(4,128)(4,1)}, pred[1,2,512]{2,1,0:T(4,128)(4,1)S(1)}, u32[]{:S(2)}) copy-start(pred[1,2,512]{2,1,0:T(4,128)(4,1)S(1)} %get-tuple-element.396) | copy-start | bytes 3076
  13.4 94.6 %copy-start.60 = (pred[1024]{0:T(1024)(128)(4,1)}, pred[1024]{0:T(1024)(128)(4,1)S(1)}, u32[]{:S(2)}) copy-start(pred[1024]{0:T(1024)(128)(4,1)S(1)} %eq.31) | copy-start | bytes 3076
  13.4 94.6 %copy-start.57 = (pred[1024]{0:T(1024)(128)(4,1)}, pred[1024]{0:T(1024)(128)(4,1)S(1)}, u32[]{:S(2)}) copy-start(pred[1024]{0:T(1024)(128)(4,1)S(1)} %eq.33) | copy-start | bytes 3076
  109.0 7.0 copy-start.28
  109.0 8.4 copy-start.27
  109.0 8.3 copy-start.83
  157.6 239.9 %copy-start.38 = (f32[1024]{0:T(1024)}, f32[1024]{0:T(1024)S(1)}, u32[]{:S(2)}) copy-start(f32[1024]{0:T(1024)S(1)} %broadcast_multiply_fusion.3) | copy-start | bytes 12292
  158.2 239.4 %copy-start.43 = (f32[1024]{0:T(1024)}, f32[1024]{0:T(1024)S(1)}, u32[]{:S(2)}) copy-start(f32[1024]{0:T(1024)S(1)} %fusion.48) | copy-start | bytes 12292
  191.4 34.0 %copy-start.34 = (f32[768]{0:T(1024)S(1)}, f32[768]{0:T(1024)}, u32[]{:S(2)}) copy-start(f32[768]{0:T(1024)} %convert_element_type.346) | copy-start | bytes 9220
  191.4 34.0 %copy-start.36 = (f32[768]{0:T(1024)S(1)}, f32[768]{0:T(1024)}, u32[]{:S(2)}) copy-start(f32[768]{0:T(1024)} %convert_element_type.347) | copy-start | bytes 9220
  191.5 42.3 %copy-start.40 = (f32[1024]{0:T(1024)}, f32[1024]{0:T(1024)S(1)}, u32[]{:S(2)}) copy-start(f32[1024]{0:T(1024)S(1)} %broadcast_multiply_fusion.1) | copy-start | bytes 12292
  193.1 40.7 %copy-start.51 = (f32[1024]{0:T(1024)}, f32[1024]{0:T(1024)S(1)}, u32[]{:S(2)}) copy-start(f32[1024]{0:T(1024)S(1)} %multiply_reduce_fusion.13) | copy-start | bytes 12292
  193.1 40.7 %copy-start.45 = (f32[1024]{0:T(1024)}, f32[1024]{0:T(1024)S(1)}, u32[]{:S(2)}) copy-start(f32[1024]{0:T(1024)S(1)} %fusion.50) | copy-start | bytes 12292
  193.1 45.2 %copy-start.5 = (f32[1024,768]{1,0:T(8,128)S(1)}, f32[1024,768]{1,0:T(8,128)}, u32[]{:S(2)}) copy-start(f32[1024,768]{1,0:T(8,128)} %copy-done.4) | copy-start | bytes 9437188
  193.1 45.2 %copy-start.74 = (f32[3072]{0:T(1024)S(1)}, f32[3072]{0:T(1024)}, u32[]{:S(2)}) copy-start(f32[3072]{0:T(1024)} %convert_element_type.349) | copy-start | bytes 36868
  225.5 12.8 %copy-start.82 = (bf16[768,3072]{1,0:T(8,128)(2,1)S(1)}, bf16[768,3072]{1,0:T(8,128)(2,1)}, u32[]{:S(2)}) copy-start(bf16[768,3072]{1,0:T(8,128)(2,1)} %all-gather.9.cloned.1.call-done) | copy-start | bytes 14155780
  238.3 68.9 %copy-start.81 = (f32[768]{0:T(1024)S(1)}, f32[768]{0:T(1024)}, u32[]{:S(2)}) copy-start(f32[768]{0:T(1024)} %convert_element_type.351) | copy-start | bytes 9220
  307.3 10.2 slice-start.12
  307.3 10.3 slice-start.14
  307.3 10.3 slice-start.13
  307.3 10.3 slice-start.15
  366.4 18.9 %copy-start.10 = (f32[1024,768]{1,0:T(8,128)S(1)}, f32[1024,768]{1,0:T(8,128)}, u32[]{:S(2)}) copy-start(f32[1024,768]{1,0:T(8,128)} %copy-done.9) | copy-start | bytes 9437188
  366.4 18.9 %copy-start.41 = (f32[1024]{0:T(1024)S(1)}, f32[1024]{0:T(1024)}, u32[]{:S(2)}) copy-start(f32[1024]{0:T(1024)} %copy-done.40) | copy-start | bytes 12292
  366.4 18.9 %copy-start.46 = (f32[1024]{0:T(1024)S(1)}, f32[1024]{0:T(1024)}, u32[]{:S(2)}) copy-start(f32[1024]{0:T(1024)} %copy-done.45) | copy-start | bytes 12292
  385.3 12.2 %copy-start.52 = (f32[1024]{0:T(1024)S(1)}, f32[1024]{0:T(1024)}, u32[]{:S(2)}) copy-start(f32[1024]{0:T(1024)} %copy-done.51) | copy-start | bytes 12292
  385.3 12.2 %copy-start.50 = (f32[1024]{0:T(1024)S(1)}, f32[1024]{0:T(1024)}, u32[]{:S(2)}) copy-start(f32[1024]{0:T(1024)} %copy-done.49) | copy-start | bytes 12292
  385.3 12.2 %copy-start.21 = (f32[1024,768]{1,0:T(8,128)S(1)}, f32[1024,768]{1,0:T(8,128)}, u32[]{:S(2)}) copy-start(f32[1024,768]{1,0:T(8,128)} %add_add_fusion.9) | copy-start | bytes 9437188
  409.6 339.0 %reduce-scatter.5.cloned.1.call-start = ((), (), s32[]{:S(2)}) async-start(), calls=%async_computation.8 | async-start | bytes 7520256 | tf_op jit(solution)/shard_map/reduce_scatter | solution.py:276
  416.8 6.4 copy-start.17
  425.5 10.7 slice-start
  425.5 11.4 slice-start.1
  425.5 12.8 %slice-start.2 = ((s8[12582912]{0:T(1024)(128)(4,1)}), s8[4194304]{0:T(1024)(128)(4,1)S(1)}, s32[]{:S(2)}) async-start(s8[12582912]{0:T(1024)(128)(4,1)} %bitcast.276), calls=%async_computation.15 | async-start | bytes 8388608 | tf_op jit(solution)/shard_map/while
  454.5 6.4 copy-start.17
  463.2 10.6 slice-start
  463.2 11.0 slice-start.1
  463.2 12.7 %slice-start.2 = ((s8[12582912]{0:T(1024)(128)(4,1)}), s8[4194304]{0:T(1024)(128)(4,1)S(1)}, s32[]{:S(2)}) async-start(s8[12582912]{0:T(1024)(128)(4,1)} %bitcast.276), calls=%async_computation.15 | async-start | bytes 8388608 | tf_op jit(solution)/shard_map/while
  498.9 6.4 copy-start.16
  507.6 10.7 slice-start.3
  507.7 11.1 slice-start.4
  507.7 12.7 %slice-start.5 = ((s8[12582912]{0:T(1024)(128)(4,1)}), s8[4194304]{0:T(1024)(128)(4,1)S(1)}, s32[]{:S(2)}) async-start(s8[12582912]{0:T(1024)(128)(4,1)} %bitcast.278), calls=%async_computation.18 | async-start | bytes 8388608 | tf_op jit(solution)/shard_map/while
  536.4 6.4 copy-start.16
  545.1 10.7 slice-start.3
  545.1 10.9 slice-start.4
  545.2 12.6 %slice-start.5 = ((s8[12582912]{0:T(1024)(128)(4,1)}), s8[4194304]{0:T(1024)(128)(4,1)S(1)}, s32[]{:S(2)}) async-start(s8[12582912]{0:T(1024)(128)(4,1)} %bitcast.278), calls=%async_computation.18 | async-start | bytes 8388608 | tf_op jit(solution)/shard_map/while
  578.5 7.2 copy-start.22
  585.7 6.5 slice-start.8
  585.7 6.5 slice-start.9
  585.7 6.5 copy-start.18
  598.5 8.8 copy-start.26
  598.5 326.8 %reduce-scatter.11.cloned.1.call-start = ((), (), s32[]{:S(2)}) async-start(), calls=%async_computation.11 | async-start | bytes 10027008 | tf_op jit(solution)/shard_map/reduce_scatter | solution.py:285
  618.0 10.4 copy-start.42
  618.1 10.4 copy-start.47
  618.1 482.9 %reduce-scatter.9.cloned.1.call-start = ((), (), s32[]{:S(2)}) async-start(), calls=%async_computation.10 | async-start | bytes 10027008 | tf_op jit(solution)/shard_map/reduce_scatter | solution.py:283
  620.0 8.5 copy-start.11
  639.9 554.4 %all-reduce.26.cloned.1.call-start = ((), (), s32[]{:S(2)}) async-start(), calls=%async_computation.12 | async-start | bytes 1769472 | tf_op jit(solution)/shard_map/psum | solution.py:292
  641.6 10.2 slice-start.10
  642.7 9.2 slice-start.11
  642.7 9.2 copy-start.84
  (58 other events, 154.5 us)
Sparse Core Ops, SparseCore 0:
  10.8 74.6 all-gather.4
  88.3 54.8 all-gather.6
  146.0 79.4 all-gather.8
  228.1 79.0 all-gather.10
  409.8 127.0 reduce-scatter.6
  598.6 149.9 reduce-scatter.4
  755.3 169.9 reduce-scatter.10
  931.0 169.9 reduce-scatter.8
  1104.9 18.3 all-reduce.25
where the time goes:
time: 1220 us; the launch traced here: 1210 us
  waiting for transfers between devices  478 us (39%)
  matrix products  350 us (29%)
  blocking collectives  157 us (13%)
  local copies, waits for them, and re-layouts  102 us (8%)
  other arithmetic  102 us (8%)
  between operations  18.2 us (1%)
    reduce_scatter x1, waiting for transfers between devices, local(): lax.psum_scatter(totals[10], 'fsdp', scatter_dimension=0, tiled=True)  175 us
    reduce_scatter x1, waiting for transfers between devices, local(): lax.psum_scatter(totals[8], 'fsdp', scatter_dimension=0, tiled=True)  174 us
    unnamed x2, blocking collectives  154 us
    reduce_scatter x1, waiting for transfers between devices, local(): lax.psum_scatter(totals[1], 'fsdp', scatter_dimension=0, tiled=True)  88.6 us
    dot_general x2, matrix products, forward_pass(): jnp.dot(normed_low, expand_weight, preferred_element_type=jnp.float32)  71.6 us
    dot_general x4, matrix products, attend_back(): jnp.einsum('qhd,khd->hqk', grad_heads, split_heads(value_rows), preferred...  42.6 us
    dot_general x2, matrix products, backward_pass(): jnp.dot(grad_second, reduce_weight.T, preferred_element_type=jnp.float32)  37.6 us
    all_gather x1, waiting for transfers between devices, local(): lax.all_gather(expand_weight, 'fsdp', axis=0, tiled=True)  32.3 us
  transfers between devices with their start and end apart: 9, of which 5 were waited for; matrix products, arithmetic and copies ran while one was open for 35% of the time, Pallas kernels for 0%

commit v1 on v0

v1 whole, which is shorter than its diff:
```python
import functools

import jax
import jax.numpy as jnp
import numpy as np
from jax import lax
from jax.experimental import pallas as pl
from jax.experimental.pallas import tpu as pltpu
from jax.sharding import PartitionSpec as P

D = 768
HEADS = 12
HEAD_DIM = 64
FF = 3072
L = 512
QKV = 3 * D
LANES = 128
BLOCKS = 16
EPSILON = 1e-06
ALL = ("fsdp", "rep")
VECTORS = 13

bf16 = jnp.bfloat16
f32 = jnp.float32

NN = ((1,), (0,))
NT = ((1,), (1,))
TN = ((0,), (0,))


def dot(left, right, dims):
    return lax.dot_general(left, right, (dims, ((), ())), preferred_element_type=f32)


def params():
    return pltpu.CompilerParams(vmem_limit_bytes=60 << 20)


def shaped(shape, dtype):
    return jax.ShapeDtypeStruct(shape, dtype)


def rows(size, width, shift=0):
    return pl.BlockSpec((size, width), lambda i: (i + shift, 0))


def whole(shape):
    return pl.BlockSpec(shape, lambda i: (0,) * len(shape), pipeline_mode=pl.Buffered(1))


SMEM = pl.BlockSpec(memory_space=pltpu.SMEM)
ANY = pl.BlockSpec(memory_space=pl.ANY)


def fetch_copies(table, mine, other, target, sems, height, source_column, width):
    core = table[64]
    copies = []
    for half, source in ((0, mine), (1, other)):
        place = core if half == 0 else 1 - core
        column = pl.multiple_of(place * width, LANES)
        for block in range(BLOCKS):
            owner = table[16 * half + block]
            copies.append(
                pltpu.make_async_copy(
                    source.at[pl.ds(block * height, height), pl.ds(source_column, width)],
                    target.at[pl.ds(pl.multiple_of(owner * height, 16), height), pl.ds(column, width)],
                    sems.at[16 * half + block],
                )
            )
    return copies


def spread_copies(table, staged, keep, send, sems, height, target_column, width):
    core = table[64]
    copies = []
    for half, target in ((0, keep), (1, send)):
        place = core if half == 0 else 1 - core
        column = pl.multiple_of(place * width, LANES)
        for block in range(BLOCKS):
            owner = table[32 + 16 * half + block]
            copies.append(
                pltpu.make_async_copy(
                    staged.at[pl.ds(pl.multiple_of(owner * height, 16), height), pl.ds(column, width)],
                    target.at[pl.ds(block * height, height), pl.ds(target_column, width)],
                    sems.at[16 * half + block],
                )
            )
    return copies


def start_all(copies):
    for copy in copies:
        copy.start()


def wait_all(copies):
    for copy in copies:
        copy.wait()


def fold(values):
    height, width = values.shape
    return jnp.sum(values.reshape(height // 8, 8, width), axis=0)


def six(column):
    return jnp.concatenate([column] * (D // LANES), axis=1)


def lane_first(height):
    return lax.broadcasted_iota(jnp.int32, (height, LANES), 1) < HEAD_DIM


def normalise(values):
    mean = jnp.mean(values, axis=1, keepdims=True)
    centred = values - mean
    spread = jnp.mean(centred * centred, axis=1, keepdims=True)
    rate = lax.rsqrt(spread + EPSILON)
    return centred * rate, rate


def norm_back(weighted, unit, rate):
    return rate * (
        weighted
        - jnp.mean(weighted, axis=1, keepdims=True)
        - unit * jnp.mean(weighted * unit, axis=1, keepdims=True)
    )


def attend_kernel(
    table, tokens, mask, mine, other, *refs
):
    x_out, qkv_out, raised_out, inverse_out, context_out, turned_out, vec_out = refs[-12:-5]
    weight, columns, vectors, sems, vec_sems = refs[-5:]

    @pl.when(pl.program_id(0) == 0)
    def _():
        copies = fetch_copies(table, mine, other, weight, sems, D // BLOCKS, 0, QKV // 2)
        height = D // BLOCKS
        for block in range(BLOCKS):
            copies.append(
                pltpu.make_async_copy(
                    mine.at[pl.ds(block * height, height), pl.ds(QKV // 2, LANES)],
                    columns.at[pl.ds(pl.multiple_of(table[block] * height, 16), height), :],
                    vec_sems.at[block],
                )
            )
        start_all(copies)
        wait_all(copies)
        vectors[...] = columns[...].astype(f32).T[:16]
        vec_out[...] = vectors[...]

    chosen = six(mask[...]) > 0
    x = jnp.where(chosen, jnp.broadcast_to(vectors[0:1, :].astype(bf16), (L, D)), tokens[...])
    x_out[...] = x
    queries = dot(x, weight[:, :D], NN) + vectors[1:2, :]
    qkv_out[:, :D] = queries.astype(bf16) * jnp.asarray(HEAD_DIM**-0.5, bf16)
    qkv_out[:, D : 2 * D] = dot(x, weight[:, D : 2 * D], NN).astype(bf16)
    qkv_out[:, 2 * D :] = (dot(x, weight[:, 2 * D :], NN) + vectors[2:3, :]).astype(bf16)
    first = lane_first(L)
    for pair in range(HEADS // 2):
        low = LANES * pair
        queries = qkv_out[:, low : low + LANES]
        keys = qkv_out[:, D + low : D + low + LANES]
        values = qkv_out[:, 2 * D + low : 2 * D + low + LANES].T
        for part in range(2):
            head = 2 * pair + part
            lanes = first if part == 0 else ~first
            scores = dot(keys, jnp.where(lanes, queries, jnp.zeros_like(queries)), NT)
            raised = jnp.exp(scores - jnp.max(scores, axis=0, keepdims=True)).astype(bf16)
            raised_out[head] = raised
            stacked = jnp.concatenate(
                [values[HEAD_DIM * part : HEAD_DIM * (part + 1)], jnp.ones((16, L), bf16)], axis=0
            )
            mixed = dot(stacked, raised, NN)
            inverse = 1.0 / mixed[HEAD_DIM : HEAD_DIM + 1]
            inverse_out[head : head + 1, :] = inverse
            turned_out[HEAD_DIM * head : HEAD_DIM * (head + 1), :] = (mixed[:HEAD_DIM] * inverse).astype(bf16)
    context_out[...] = turned_out[...].T


def attend(table, tokens, mask, mine, other, earlier, start, count):
    height = tokens.shape[0]
    total = height // L
    shapes = [
        shaped((height, D), bf16),
        shaped((height, QKV), bf16),
        shaped((total, HEADS, L, L), bf16),
        shaped((total, 16, L), f32),
        shaped((height, D), bf16),
        shaped((total, D, L), bf16),
        shaped((16, D), f32),
    ]
    passed = list(earlier[:6]) if earlier else []
    return pl.pallas_call(
        attend_kernel,
        name="attend",
        grid=(count,),
        in_specs=[SMEM, rows(L, D, start), rows(L, LANES, start), ANY, ANY] + [ANY] * len(passed),
        out_specs=[
            rows(L, D, start),
            rows(L, QKV, start),
            pl.BlockSpec((None, HEADS, L, L), lambda i: (i + start, 0, 0, 0)),
            pl.BlockSpec((None, 16, L), lambda i: (i + start, 0, 0)),
            rows(L, D, start),
            pl.BlockSpec((None, D, L), lambda i: (i + start, 0, 0)),
            whole((16, D)),
        ],
        out_shape=shapes,
        scratch_shapes=[
            pltpu.VMEM((D, QKV), bf16),
            pltpu.VMEM((D, LANES), bf16),
            pltpu.VMEM((16, D), f32),
            pltpu.SemaphoreType.DMA((32,)),
            pltpu.SemaphoreType.DMA((16,)),
        ],
        input_output_aliases={5 + i: i for i in range(len(passed))},
        compiler_params=params(),
        cost_estimate=pl.CostEstimate(
            flops=count * (2 * L * D * QKV + 16 * L * L * D), bytes_accessed=count * 14_000_000, transcendentals=0
        ),
    )(table, tokens, mask, mine, other, *passed)


def expand_kernel(table, context, x, vec, bias, mine, other, *refs):
    unit_out, rate_out, low_out, active_out, slope_out = refs[-9:-4]
    out_weight, weight, sems, more_sems = refs[-4:]

    @pl.when(pl.program_id(0) == 0)
    def _():
        copies = fetch_copies(table, mine, other, out_weight, sems, D // BLOCKS, 0, D // 2)
        copies += fetch_copies(table, mine, other, weight, more_sems, D // BLOCKS, D // 2, FF // 2)
        start_all(copies)
        wait_all(copies)

    first_sum = x[...].astype(f32) + (dot(context[...], out_weight[...], NN) + vec[3:4, :])
    unit, rate = normalise(first_sum)
    unit_out[...] = unit
    rate_out[...] = jnp.broadcast_to(rate, rate_out.shape)
    low = (unit * vec[4:5, :] + vec[5:6, :]).astype(bf16)
    low_out[...] = low
    step = 512
    for part in range(FF // step):
        span = slice(step * part, step * (part + 1))
        hidden = dot(low, weight[:, span], NN) + bias[0:1, span]
        share = 0.5 * (1.0 + lax.erf(hidden * (2.0**-0.5)))
        density = jnp.exp(-0.5 * hidden * hidden) * ((2.0 * np.pi) ** -0.5)
        active_out[:, span] = (hidden * share).astype(bf16)
        slope_out[:, span] = (share + hidden * density).astype(bf16)


def expand(table, context, x, vec, bias, mine, other, earlier, start, count, size):
    height = x.shape[0]
    shapes = [
        shaped((height, D), f32),
        shaped((height, LANES), f32),
        shaped((height, D), bf16),
        shaped((height, FF), bf16),
        shaped((height, FF), bf16),
    ]
    passed = list(earlier) if earlier else []
    return pl.pallas_call(
        expand_kernel,
        name="expand",
        grid=(count,),
        in_specs=[SMEM, rows(size, D, start), rows(size, D, start), whole((16, D)), whole((1, FF)), ANY, ANY]
        + [ANY] * len(passed),
        out_specs=[
            rows(size, D, start),
            rows(size, LANES, start),
            rows(size, D, start),
            rows(size, FF, start),
            rows(size, FF, start),
        ],
        out_shape=shapes,
        scratch_shapes=[
            pltpu.VMEM((D, D), bf16),
            pltpu.VMEM((D, FF), bf16),
            pltpu.SemaphoreType.DMA((32,)),
            pltpu.SemaphoreType.DMA((32,)),
        ],
        input_output_aliases={7 + i: i for i in range(len(passed))},
        compiler_params=params(),
        cost_estimate=pl.CostEstimate(
            flops=count * size * 2 * D * (D + FF), bytes_accessed=count * size * 20_000, transcendentals=0
        ),
    )(table, context, x, vec, bias, mine, other, *passed)


def reduce_kernel(
    table, active, slope, unit_in, cotangent, mask, vec, mine, other,
    outputs, outer_out, hidden_out, sums, bias_sums, keep, send,
    weight, total, staged, sems, out_sems,
):
    step = pl.program_id(0)

    @pl.when(step == 0)
    def _():
        copies = fetch_copies(table, mine, other, weight, sems, FF // BLOCKS, 0, D // 2)
        start_all(copies)
        sums[...] = jnp.zeros_like(sums)
        bias_sums[...] = jnp.zeros_like(bias_sums)
        total[...] = jnp.zeros_like(total)
        wait_all(copies)

    height = active.shape[0]
    parts = 2
    share = height // parts
    lows = []
    for part in range(parts):
        span = slice(share * part, share * (part + 1))
        normed = unit_in[span, :] * vec[4:5, :] + vec[5:6, :]
        second = normed + (dot(active[span, :], weight[...], NN) + vec[10:11, :])
        unit, rate = normalise(second)
        outputs[span, :] = (unit * vec[11:12, :] + vec[12:13, :]).astype(bf16)
        upstream = jnp.where(six(mask[span, :]) > 0, cotangent[span, :].astype(f32), 0.0)
        outer = norm_back(upstream * vec[11:12, :], unit, rate)
        outer_out[span, :] = outer
        low = outer.astype(bf16)
        sums[0:8, :] += fold(upstream * unit)
        sums[8:16, :] += fold(upstream)
        sums[16:24, :] += fold(low.astype(f32))
        width = 512
        for piece in range(FF // width):
            units = slice(width * piece, width * (piece + 1))
            grad = dot(low, weight[units, :], NT) * slope[span, units].astype(f32)
            grad_low = grad.astype(bf16)
            hidden_out[span, units] = grad_low
            bias_sums[:, units] += fold(grad_low.astype(f32))
        lows.append(low)
    low = jnp.concatenate(lows, axis=0)
    for piece in range(FF // D):
        units = slice(D * piece, D * (piece + 1))
        total[units, :] += dot(active[:, units], low, TN)

    @pl.when(step == pl.num_programs(0) - 1)
    def _():
        staged[...] = total[...].astype(bf16)
        copies = spread_copies(table, staged, keep, send, out_sems, FF // BLOCKS, 0, D // 2)
        start_all(copies)
        wait_all(copies)


def reduce(table, active, slope, unit, cotangent, mask, vec, mine, other, size):
    height = active.shape[0]
    return pl.pallas_call(
        reduce_kernel,
        name="reduce",
        grid=(height // size,),
        in_specs=[
            SMEM,
            rows(size, FF),
            rows(size, FF),
            rows(size, D),
            rows(size, D),
            rows(size, LANES),
            whole((16, D)),
            ANY,
            ANY,
        ],
        out_specs=[rows(size, D), rows(size, D), rows(size, FF), whole((24, D)), whole((8, FF)), ANY, ANY],
        out_shape=[
            shaped((height, D), bf16),
            shaped((height, D), f32),
            shaped((height, FF), bf16),
            shaped((24, D), f32),
            shaped((8, FF), f32),
            shaped((FF, D // 2), bf16),
            shaped((FF, D // 2), bf16),
        ],
        scratch_shapes=[
            pltpu.VMEM((FF, D), bf16),
            pltpu.VMEM((FF, D), f32),
            pltpu.VMEM((FF, D), bf16),
            pltpu.SemaphoreType.DMA((32,)),
            pltpu.SemaphoreType.DMA((32,)),
        ],
        compiler_params=params(),
        cost_estimate=pl.CostEstimate(flops=height * 6 * D * FF, bytes_accessed=height * 30_000, transcendentals=0),
    )(table, active, slope, unit, cotangent, mask, vec, mine, other)


def inner_kernel(
    table, hidden, outer, unit_in, rate_in, low_in, context, mask, vec, mine, other,
    inner_out, context_out, sums, keep, send,
    out_weight, weight, out_total, total, out_staged, staged, sems, more_sems, out_sems, more_out_sems,
):
    step = pl.program_id(0)

    @pl.when(step == 0)
    def _():
        copies = fetch_copies(table, mine, other, out_weight, sems, D // BLOCKS, 0, D // 2)
        copies += fetch_copies(table, mine, other, weight, more_sems, D // BLOCKS, D // 2, FF // 2)
        start_all(copies)
        sums[...] = jnp.zeros_like(sums)
        out_total[...] = jnp.zeros_like(out_total)
        total[...] = jnp.zeros_like(total)
        wait_all(copies)

    grad_normed = outer[...] + dot(hidden[...], weight[...], NT)
    low = low_in[...]
    for piece in range(FF // D):
        units = slice(D * piece, D * (piece + 1))
        total[:, units] += dot(low, hidden[:, units], TN)
    unit = unit_in[...]
    sums[0:8, :] += fold(grad_normed * unit)
    sums[8:16, :] += fold(grad_normed)
    inner = norm_back(grad_normed * vec[4:5, :], unit, six(rate_in[...]))
    inner_out[...] = inner
    branch = inner.astype(bf16)
    sums[16:24, :] += fold(branch.astype(f32))
    sums[24:32, :] += fold(jnp.where(six(mask[...]) > 0, inner, 0.0))
    context_out[...] = dot(branch, out_weight[...], NT).astype(bf16)
    out_total[...] += dot(context[...], branch, TN)

    @pl.when(step == pl.num_programs(0) - 1)
    def _():
        out_staged[...] = out_total[...].astype(bf16)
        staged[...] = total[...].astype(bf16)
        copies = spread_copies(table, out_staged, keep, send, out_sems, D // BLOCKS, 0, D // 2)
        copies += spread_copies(table, staged, keep, send, more_out_sems, D // BLOCKS, D // 2, FF // 2)
        start_all(copies)
        wait_all(copies)


def inner_pass(table, hidden, outer, unit, rate, low, context, mask, vec, mine, other, size):
    height = hidden.shape[0]
    return pl.pallas_call(
        inner_kernel,
        name="inner",
        grid=(height // size,),
        in_specs=[
            SMEM,
            rows(size, FF),
            rows(size, D),
            rows(size, D),
            rows(size, LANES),
            rows(size, D),
            rows(size, D),
            rows(size, LANES),
            whole((16, D)),
            ANY,
            ANY,
        ],
        out_specs=[rows(size, D), rows(size, D), whole((32, D)), ANY, ANY],
        out_shape=[
            shaped((height, D), f32),
            shaped((height, D), bf16),
            shaped((32, D), f32),
            shaped((D, (D + FF) // 2), bf16),
            shaped((D, (D + FF) // 2), bf16),
        ],
        scratch_shapes=[
            pltpu.VMEM((D, D), bf16),
            pltpu.VMEM((D, FF), bf16),
            pltpu.VMEM((D, D), f32),
            pltpu.VMEM((D, FF), f32),
            pltpu.VMEM((D, D), bf16),
            pltpu.VMEM((D, FF), bf16),
            pltpu.SemaphoreType.DMA((32,)),
            pltpu.SemaphoreType.DMA((32,)),
            pltpu.SemaphoreType.DMA((32,)),
            pltpu.SemaphoreType.DMA((32,)),
        ],
        compiler_params=params(),
        cost_estimate=pl.CostEstimate(
            flops=height * 4 * D * (D + FF), bytes_accessed=height * 20_000, transcendentals=0
        ),
    )(table, hidden, outer, unit, rate, low, context, mask, vec, mine, other)


def attend_back_kernel(qkv, raised_in, inverse_in, turned, grad_context, *refs):
    mixed_out, turned_grad = refs[-2:]
    first = lane_first(L)
    blank = jnp.zeros((HEAD_DIM, L), bf16)
    for pair in range(HEADS // 2):
        low = LANES * pair
        queries = qkv[:, low : low + LANES]
        keys = qkv[:, D + low : D + low + LANES]
        values = qkv[:, 2 * D + low : 2 * D + low + LANES]
        grads = grad_context[:, low : low + LANES].T.astype(f32)
        turned_keys = keys.T
        grad_values = None
        grad_keys = None
        for part in range(2):
            head = 2 * pair + part
            span = slice(HEAD_DIM * part, HEAD_DIM * (part + 1))
            outer_span = slice(HEAD_DIM * head, HEAD_DIM * (head + 1))
            grad = grads[span] * inverse_in[head : head + 1, :]
            level = jnp.sum(grad * turned[outer_span, :].astype(f32), axis=0, keepdims=True)
            grad_low = grad.astype(bf16)
            padded = jnp.concatenate([grad_low, blank] if part == 0 else [blank, grad_low], axis=0)
            raised = raised_in[head]
            grad_scores = (raised.astype(f32) * (dot(values, padded, NN) - level)).astype(bf16)
            lanes = first if part == 0 else ~first
            chosen = jnp.where(lanes, queries, jnp.zeros_like(queries))
            value_term = dot(raised, padded, NT)
            key_term = dot(grad_scores, chosen, NN)
            grad_values = value_term if part == 0 else grad_values + value_term
            grad_keys = key_term if part == 0 else grad_keys + key_term
            turned_grad[outer_span, :] = dot(turned_keys[span], grad_scores, NN) * HEAD_DIM**-0.5
        mixed_out[:, low : low + LANES] = turned_grad[low : low + LANES, :].T.astype(bf16)
        mixed_out[:, D + low : D + low + LANES] = grad_keys.astype(bf16)
        mixed_out[:, 2 * D + low : 2 * D + low + LANES] = grad_values.astype(bf16)


def attend_back(qkv, raised, inverse, turned, grad_context, earlier, start, count):
    height = qkv.shape[0]
    passed = [earlier] if earlier is not None else []
    return pl.pallas_call(
        attend_back_kernel,
        name="attend_back",
        grid=(count,),
        in_specs=[
            rows(L, QKV, start),
            pl.BlockSpec((None, HEADS, L, L), lambda i: (i + start, 0, 0, 0)),
            pl.BlockSpec((None, 16, L), lambda i: (i + start, 0, 0)),
            pl.BlockSpec((None, D, L), lambda i: (i + start, 0, 0)),
            rows(L, D, start),
        ]
        + [ANY] * len(passed),
        out_specs=rows(L, QKV, start),
        out_shape=shaped((height, QKV), bf16),
        scratch_shapes=[pltpu.VMEM((D, L), f32)],
        input_output_aliases={5: 0} if passed else {},
        compiler_params=params(),
        cost_estimate=pl.CostEstimate(flops=count * 32 * L * L * D, bytes_accessed=count * 14_000_000, transcendentals=0),
    )(qkv, raised, inverse, turned, grad_context, *passed)


def heads_kernel(
    table, x, marks, mixed, second_sums, inner_sums, bias_rows, mine, other,
    keep, send,
    total, staged, columns, weight, sems, out_sems, vec_sems,
):
    step = pl.program_id(0)

    @pl.when(step == 0)
    def _():
        start_all(fetch_copies(table, mine, other, weight, sems, D // BLOCKS, 0, QKV // 2))
        total[...] = jnp.zeros_like(total)

    turned = jnp.concatenate([x[...].T, marks[...]], axis=0)
    for piece in range(3):
        span = slice(D * piece, D * (piece + 1))
        total[:, span] += dot(turned, mixed[:, span], NN)

    @pl.when(step == pl.num_programs(0) - 1)
    def _():
        wait_all(fetch_copies(table, mine, other, weight, sems, D // BLOCKS, 0, QKV // 2))
        staged[...] = total[:D, :].astype(bf16)
        copies = spread_copies(table, staged, keep, send, out_sems, D // BLOCKS, 0, QKV // 2)
        start_all(copies)
        whole_sums = total[D : D + 1, :]
        masked_sums = total[D + 1 : D + 2, :]
        high = masked_sums.astype(bf16)
        low = (masked_sums - high.astype(f32)).astype(bf16)
        split = jnp.concatenate([high, low, jnp.zeros((14, QKV), bf16)], axis=0)
        reached = jnp.sum(dot(split, weight[...], NT), axis=0, keepdims=True)

        def line(ref, group):
            return jnp.sum(ref[8 * group : 8 * (group + 1), :], axis=0, keepdims=True)

        lines = [
            reached + line(inner_sums, 3),
            whole_sums[:, :D],
            whole_sums[:, 2 * D :],
            line(inner_sums, 2),
            line(inner_sums, 0),
            line(inner_sums, 1),
            bias_rows[...],
            line(second_sums, 2),
            line(second_sums, 0),
            line(second_sums, 1),
            jnp.zeros((LANES - VECTORS, D), f32),
        ]
        columns[...] = jnp.concatenate(lines, axis=0).T.astype(bf16)
        height = D // BLOCKS
        more = []
        for half, target in ((0, keep), (1, send)):
            for block in range(BLOCKS):
                owner = table[32 + 16 * half + block]
                more.append(
                    pltpu.make_async_copy(
                        columns.at[pl.ds(pl.multiple_of(owner * height, 16), height), :],
                        target.at[pl.ds(block * height, height), pl.ds(QKV // 2, LANES)],
                        vec_sems.at[16 * half + block],
                    )
                )
        start_all(more)
        wait_all(copies + more)


def heads_grad(table, x, marks, mixed, second_sums, inner_sums, bias_rows, mine, other, size):
    height = x.shape[0]
    wide = QKV // 2 + LANES
    return pl.pallas_call(
        heads_kernel,
        name="heads_grad",
        grid=(height // size,),
        in_specs=[
            SMEM,
            rows(size, D),
            pl.BlockSpec((16, size), lambda i: (0, i)),
            rows(size, QKV),
            whole((24, D)),
            whole((32, D)),
            whole((4, D)),
            ANY,
            ANY,
        ],
        out_specs=[ANY, ANY],
        out_shape=[shaped((D, wide), bf16), shaped((D, wide), bf16)],
        scratch_shapes=[
            pltpu.VMEM((D + 16, QKV), f32),
            pltpu.VMEM((D, QKV), bf16),
            pltpu.VMEM((D, LANES), bf16),
            pltpu.VMEM((D, QKV), bf16),
            pltpu.SemaphoreType.DMA((32,)),
            pltpu.SemaphoreType.DMA((32,)),
            pltpu.SemaphoreType.DMA((32,)),
        ],
        compiler_params=params(),
        cost_estimate=pl.CostEstimate(flops=height * 2 * D * QKV, bytes_accessed=height * 10_000, transcendentals=0),
    )(table, x, marks, mixed, second_sums, inner_sums, bias_rows, mine, other)


def rows_kernel(table, mixed, inner, mask, mine, other, grad_out, weight, sems):
    @pl.when(pl.program_id(0) == 0)
    def _():
        copies = fetch_copies(table, mine, other, weight, sems, D // BLOCKS, 0, QKV // 2)
        start_all(copies)
        wait_all(copies)

    grad = inner[...] + dot(mixed[...], weight[...], NT)
    grad_out[...] = jnp.where(six(mask[...]) > 0, 0.0, grad).astype(bf16)


def rows_grad(table, mixed, inner, mask, mine, other, size):
    height = mixed.shape[0]
    return pl.pallas_call(
        rows_kernel,
        name="rows_grad",
        grid=(height // size,),
        in_specs=[SMEM, rows(size, QKV), rows(size, D), rows(size, LANES), ANY, ANY],
        out_specs=rows(size, D),
        out_shape=shaped((height, D), bf16),
        scratch_shapes=[pltpu.VMEM((D, QKV), bf16), pltpu.SemaphoreType.DMA((32,))],
        compiler_params=params(),
        cost_estimate=pl.CostEstimate(flops=height * 2 * D * QKV, bytes_accessed=height * 10_000, transcendentals=0),
    )(table, mixed, inner, mask, mine, other)


def around_z(hops):
    return [(i, (i + 8 * hops) % 32) for i in range(32)]


def across(turn):
    return [(i, i ^ (2 if (i & 1) == turn else 4)) for i in range(32)]


def between_cores():
    return [(i, i ^ 1) for i in range(32)]


def make_table():
    table = np.zeros((32, 65), np.int32)
    for device in range(32):
        core, x, y, z = device & 1, (device >> 1) & 1, (device >> 2) & 1, device >> 3
        table[device, 64] = core
        for half in range(2):
            turn = core ^ half
            for block in range(16):
                hops, near, far = block & 3, (block >> 2) & 1, block >> 3
                there_x, there_y = (x ^ near, y ^ far) if turn == 0 else (x ^ far, y ^ near)
                table[device, 16 * half + block] = ((z - hops) % 4) * 4 + there_y * 2 + there_x
                near, far = far, near
                there_x, there_y = (x ^ near, y ^ far) if turn == 0 else (x ^ far, y ^ near)
                table[device, 32 + 16 * half + block] = ((z + hops) % 4) * 4 + there_y * 2 + there_x
    return table


def gather_blocks(block):
    parts = [block] + [lax.ppermute(block, ALL, around_z(hops)) for hops in (1, 2, 3)]
    held = jnp.concatenate(parts, axis=0)
    held = jnp.concatenate([held, lax.ppermute(held, ALL, across(0))], axis=0)
    held = jnp.concatenate([held, lax.ppermute(held, ALL, across(1))], axis=0)
    return held, lax.ppermute(held, ALL, between_cores())


def add_low(*terms):
    total = terms[0].astype(f32)
    for term in terms[1:]:
        total = total + term.astype(f32)
    return total


def scatter_blocks(keep, send):
    height = keep.shape[0]
    arrived = lax.ppermute(send, ALL, between_cores())
    for turn in (0, 1):
        half = height // 2
        kept = add_low(keep[:half], arrived[:half]).astype(bf16)
        sent = add_low(keep[half:], arrived[half:]).astype(bf16)
        keep, arrived = kept, lax.ppermute(sent, ALL, across(turn))
        height = half
    quarter = height // 4
    pieces = [
        add_low(keep[quarter * hops : quarter * (hops + 1)], arrived[quarter * hops : quarter * (hops + 1)])
        for hops in range(4)
    ]
    moved = [lax.ppermute(pieces[hops].astype(bf16), ALL, around_z(hops)) for hops in (1, 2, 3)]
    return add_low(pieces[0], *moved)


def gather_plain(mine, other):
    return (
        lax.all_gather(mine, "fsdp", axis=0, tiled=True),
        lax.all_gather(other, "fsdp", axis=0, tiled=True),
    )


def scatter_plain(keep, send):
    both = add_low(keep, lax.ppermute(send, "rep", [(0, 1), (1, 0)]))
    return lax.psum_scatter(both, "fsdp", scatter_dimension=0, tiled=True)


def join(core, mine):
    other = lax.ppermute(mine, "rep", [(0, 1), (1, 0)])
    low = jnp.where(core == 0, mine, other)
    high = jnp.where(core == 0, other, mine)
    return jnp.concatenate([low, high], axis=1)


def half_of(weight, place):
    width = weight.shape[1] // 2
    return lax.dynamic_slice_in_dim(weight, place * width, width, axis=1)


def local(
    chips,
    tokens,
    masked,
    cotangent,
    mask_vector,
    heads_weight,
    query_bias,
    value_bias,
    output_weight,
    output_bias,
    first_gain,
    first_shift,
    expand_weight,
    expand_bias,
    reduce_weight,
    reduce_bias,
    second_gain,
    second_shift,
):
    core = lax.axis_index("rep")
    layout = tokens.shape
    height = layout[0] * layout[1] * layout[2]
    share = mask_vector.shape[0]
    by_hops = chips == BLOCKS
    if by_hops:
        table = lax.dynamic_index_in_dim(
            jnp.asarray(make_table()), lax.axis_index("fsdp") * 2 + core, axis=0, keepdims=False
        )
    else:
        table = jnp.concatenate([jnp.tile(jnp.arange(BLOCKS, dtype=jnp.int32), 4), core[None].astype(jnp.int32)])

    vector_rows = jnp.concatenate(
        [
            mask_vector[None],
            query_bias[None],
            value_bias[None],
            output_bias[None],
            first_gain[None],
            first_shift[None],
            expand_bias.reshape(4, share),
            reduce_bias[None],
            second_gain[None],
            second_shift[None],
        ],
        axis=0,
    )
    vector_columns = jnp.pad(vector_rows.T, ((0, 0), (0, LANES - VECTORS)))

    def payloads(place):
        return (
            jnp.concatenate([half_of(heads_weight, place), vector_columns], axis=1),
            jnp.concatenate([half_of(output_weight, place), half_of(expand_weight, place)], axis=1),
            half_of(reduce_weight, place),
        )

    if by_hops:
        gathered = [gather_blocks(payload) for payload in payloads(core)]
    else:
        gathered = [gather_plain(a, b) for a, b in zip(payloads(core), payloads(1 - core))]
    heads, middle, last = gathered
    scatter = scatter_blocks if by_hops else scatter_plain

    flat_tokens = tokens.reshape(height, D)
    flat_cotangent = cotangent.reshape(height, D)
    flags = masked.reshape(height).astype(bf16)
    mask = jnp.broadcast_to(flags[:, None], (height, LANES))
    marks = jnp.concatenate([jnp.ones((1, height), bf16), flags[None], jnp.zeros((14, height), bf16)], axis=0)

    sequences = height // L
    half = sequences // 2
    done = attend(table, flat_tokens, mask, *heads, None, 0, half)
    vec = done[6]
    done = attend(table, flat_tokens, mask, *heads, done, half, sequences - half)
    x, qkv, raised, inverse, context, turned = done[:6]
    bias = vec[6:10].reshape(4, D // share, share).transpose(1, 0, 2).reshape(1, FF)

    size = 512
    steps = height // size
    early = steps // 2
    opened = expand(table, context, x, vec, bias, *middle, None, 0, early, size)
    opened = expand(table, context, x, vec, bias, *middle, opened, early, steps - early, size)
    unit, rate, low, active, slope = opened

    outputs, outer, hidden, second_sums, bias_sums, keep, send = reduce(
        table, active, slope, unit, flat_cotangent, mask, vec, *last, size
    )
    last_grad = scatter(keep, send)
    bias_rows = jnp.sum(bias_sums, axis=0).reshape(D // share, 4, share).transpose(1, 0, 2).reshape(4, D)

    inner, grad_context, inner_sums, keep, send = inner_pass(
        table, hidden, outer, unit, rate, low, context, mask, vec, *middle, size
    )
    middle_grad = scatter(keep, send)

    mixed = attend_back(qkv, raised, inverse, turned, grad_context, None, 0, half)
    mixed = attend_back(qkv, raised, inverse, turned, grad_context, mixed, half, sequences - half)

    keep, send = heads_grad(table, x, marks, mixed, second_sums, inner_sums, bias_rows, *heads, size)
    heads_share = scatter(keep, send)
    grad_tokens = rows_grad(table, mixed, inner, mask, *heads, size)

    vector_grads = heads_share[:, QKV // 2 :]

    def vector(index):
        return vector_grads[:, index]

    return (
        outputs.reshape(layout),
        grad_tokens.reshape(layout),
        vector(0),
        join(core, heads_share[:, : QKV // 2]),
        vector(1),
        vector(2),
        join(core, middle_grad[:, : D // 2]),
        vector(3),
        vector(4),
        vector(5),
        join(core, middle_grad[:, D // 2 :]),
        vector_grads[:, 6:10].T.reshape(-1),
        join(core, last_grad),
        vector(10),
        vector(11),
        vector(12),
    )


def solution(mesh):
    in_specs = (
        P(None, ("fsdp", "rep"), None, None),
        P(None, ("fsdp", "rep"), None),
        P(None, ("fsdp", "rep"), None, None),
        P("fsdp"),
        P("fsdp", None),
        P("fsdp"),
        P("fsdp"),
        P("fsdp", None),
        P("fsdp"),
        P("fsdp"),
        P("fsdp"),
        P("fsdp", None),
        P("fsdp"),
        P("fsdp", None),
        P("fsdp"),
        P("fsdp"),
        P("fsdp"),
    )
    out_specs = (
        P(None, ("fsdp", "rep"), None, None),
        P(None, ("fsdp", "rep"), None, None),
        P("fsdp"),
        P("fsdp", None),
        P("fsdp"),
        P("fsdp"),
        P("fsdp", None),
        P("fsdp"),
        P("fsdp"),
        P("fsdp"),
        P("fsdp", None),
        P("fsdp"),
        P("fsdp", None),
        P("fsdp"),
        P("fsdp"),
        P("fsdp"),
    )
    return jax.shard_map(
        functools.partial(local, mesh.shape["fsdp"]),
        mesh=mesh,
        in_specs=in_specs,
        out_specs=out_specs,
        check_vma=False,
    )
```

time: 1220 us -> 455 us (0.37)
  waiting for transfers between devices: 478 us -> 105 us
  matrix products: 350 us -> 0 us
  Pallas kernels: 0 us -> 245 us
  blocking collectives: 157 us -> 0 us
  other arithmetic: 102 us -> 20.1 us
  local copies, waits for them, and re-layouts: 102 us -> 25.7 us
  starting transfers between devices: 0.36 us -> 49.5 us
  between operations: 18.2 us -> 1.3 us
    reduce_scatter x4 -> x0, waiting for transfers between devices: 437 us -> none  [the longest x1 175 us: local(): lax.psum_scatter(totals[10], 'fsdp', scatter_dimension=0, tiled=True)]
    dot_general x52 -> x0, matrix products: 350 us -> none  [the longest x2 71.6 us: forward_pass(): jnp.dot(normed_low, expand_weight, preferred_element_type=jnp.float32)]
    pallas_call x0 -> x10, Pallas kernels: none -> 245 us  [the longest x1 53.7 us: reduce(): pl.pallas_call(reduce_kernel, name='reduce', grid=(height // size,), in_s...]
    unnamed x2 -> x0, blocking collectives: 154 us -> none
    ppermute x0 -> x40, waiting for transfers between devices: none -> 105 us  [the longest x9 34.3 us: scatter_blocks(): lax.ppermute(pieces[hops].astype(bf16), ALL, around_z(hops))]
    ppermute x0 -> x40, starting transfers between devices: none -> 49.5 us  [the longest x9 16.3 us: gather_blocks(): lax.ppermute(block, ALL, around_z(hops))]
    convert_element_type x32 -> x10, other arithmetic: 53.2 us -> 12.8 us  [the longest x6 12.5 us: scatter_blocks(): kept = add_low(keep[:half], arrived[:half]).astype(bf16)]
    all_gather x4 -> x0, waiting for transfers between devices: 38 us -> none  [the longest x1 32.3 us: local(): lax.all_gather(expand_weight, 'fsdp', axis=0, tiled=True)]
  transfers between devices with their start and end apart: 9 -> 40, of which waited for: 5 -> 20; matrix products, arithmetic and copies ran while one was open for 35% -> 9% of each run, Pallas kernels for 0% -> 22%
where the time goes in v1:
time: 455 us; the launch traced here: 447 us
  Pallas kernels  245 us (54%)
  waiting for transfers between devices  105 us (23%)
  starting transfers between devices  49.5 us (11%)
  local copies, waits for them, and re-layouts  25.7 us (6%)
  other arithmetic  20.1 us (4%)
    pallas_call x1, Pallas kernels, reduce(): pl.pallas_call(reduce_kernel, name='reduce', grid=(height // size,), in_s...  53.7 us
    pallas_call x2, Pallas kernels, attend(): pl.pallas_call(attend_kernel, name='attend', grid=(count,), in_specs=[SME...  44.2 us
    pallas_call x1, Pallas kernels, inner_pass(): pl.pallas_call(inner_kernel, name='inner', grid=(height // size,), in_spe...  40.8 us
    pallas_call x2, Pallas kernels, expand(): pl.pallas_call(expand_kernel, name='expand', grid=(count,), in_specs=[SME...  38.2 us
    pallas_call x2, Pallas kernels, attend_back(): pl.pallas_call(attend_back_kernel, name='attend_back', grid=(count,), in_...  37.8 us
    ppermute x9, waiting for transfers between devices, scatter_blocks(): lax.ppermute(pieces[hops].astype(bf16), ALL, around_z(hops))  34.3 us
    ppermute x3, waiting for transfers between devices, gather_blocks(): held = jnp.concatenate([held, lax.ppermute(held, ALL, across(0))], axis=0)  19 us
    ppermute x9, waiting for transfers between devices, gather_blocks(): lax.ppermute(block, ALL, around_z(hops))  16.8 us
  transfers between devices with their start and end apart: 40, of which 20 were waited for; matrix products, arithmetic and copies ran while one was open for 9% of the time, Pallas kernels for 22%

profile of v1, /device:TPU:0, one launch (start us, length us, event | category | flops | bytes accessed | tf_op | source)
XLA Modules:
  0.0 446.7 jit_solution(6281317835891472341)
XLA Ops:
  1.5 1.6 concatenate.57
  4.8 3.0 collective-permute-start
  7.8 2.6 collective-permute-start.1
  10.4 1.3 collective-permute-start.2
  14.4 2.2 collective-permute-start.8
  16.6 9.4 %collective-permute-done.1 = bf16[48,1280]{1,0:T(8,128)(2,1)} collective-permute-done((bf16[48,1280]{1,0:T(8,128)(2,1)}, bf16[48,1280]{1,0:T(8,128)(2,1)}, u32[]{:S(2)}, u32[]{:S(2)}) %collective-permute-start.1) | collective-permute-done | bytes 122912 | tf_op jit(solution)/shard_map/ppermute | solution.py:684
  26.0 1.1 pad_maximum_fusion.4
  27.1 1.3 collective-permute-start.3
  28.4 1.6 constant_dynamic-update-slice_fusion.3
  30.0 1.6 constant_dynamic-update-slice_fusion.2
  31.6 1.6 constant_dynamic-update-slice_fusion.1
  33.3 1.6 collective-permute-start.9
  34.9 1.1 collective-permute-done.3
  36.8 1.3 collective-permute-start.4
  38.2 13.4 %collective-permute-done.9 = bf16[192,1920]{1,0:T(8,128)(2,1)S(1)} collective-permute-done((bf16[192,1920]{1,0:T(8,128)(2,1)S(1)}, bf16[192,1920]{1,0:T(8,128)(2,1)S(1)}, u32[]{:S(2)}, u32[]{:S(2)}) %collective-permute-start.9) | collective-permute-done | bytes 737312 | tf_op jit(solution)/shard_map/ppermute | solution.py:686
  51.8 2.6 collective-permute-start.10
  55.1 3.4 collective-permute-start.12
  58.5 2.7 collective-permute-start.13
  61.2 2.7 collective-permute-done.12
  63.8 3.2 collective-permute-done.13
  67.9 1.5 collective-permute-start.15
  69.4 1.0 constant_dynamic-update-slice_fusion.5.mine
  73.3 4.5 %collective-permute-done.15 = bf16[768,384]{1,0:T(8,128)(2,1)S(1)} collective-permute-done((bf16[768,384]{1,0:T(8,128)(2,1)S(1)}, bf16[768,384]{1,0:T(8,128)(2,1)S(1)}, u32[]{:S(2)}, u32[]{:S(2)}) %collective-permute-start.15) | collective-permute-done | bytes 589856 | tf_op jit(solution)/shard_map/ppermute | solution.py:686
  77.9 1.1 constant_dynamic-update-slice_fusion.22
  79.0 1.2 collective-permute-start.16
  80.6 1.2 fusion.table
  82.6 13.0 %collective-permute-done.16 = bf16[1536,384]{1,0:T(8,128)(2,1)} collective-permute-done((bf16[1536,384]{1,0:T(8,128)(2,1)}, bf16[1536,384]{1,0:T(8,128)(2,1)}, u32[]{:S(2)}, u32[]{:S(2)}) %collective-permute-start.16) | collective-permute-done | bytes 1179680 | tf_op jit(solution)/shard_map/ppermute | solution.py:687
  95.5 2.4 constant_dynamic-update-slice_fusion.27.mine
  97.9 1.1 broadcast_in_dim.40.mask
  99.1 21.9 %attend.2 = (bf16[2048,768]{1,0:T(8,128)(2,1)}, bf16[2048,2304]{1,0:T(8,128)(2,1)}, bf16[4,12,512,512]{3,2,1,0:T(8,128)(2,1)}, f32[4,16,512]{2,1,0:T(8,128)}, bf...) custom-call(s32[65]{0:T(128)} %fusion.table, bf16[2048,768]{1,0:T(8,128)(2,1)} %bitcast.26, ...), custom_call_target="tpu_custom_call" | custom-call | flops 10066329600 | bytes 28000000 | tf_op jit(solution)/shard_map/attend/pallas_call | solution.py:195
  122.6 22.3 %attend.3 = (bf16[2048,768]{1,0:T(8,128)(2,1)}, bf16[2048,2304]{1,0:T(8,128)(2,1)}, bf16[4,12,512,512]{3,2,1,0:T(8,128)(2,1)}, f32[4,16,512]{2,1,0:T(8,128)}, bf...) custom-call(s32[65]{0:T(128)} %fusion.table, ...), custom_call_target="tpu_custom_call", output_to_operand_aliasing={{0}: (5, {}), {1}: (6, {}), {2}: (7, {}), {3}: (8, {}), {4}... | custom-call | flops 10066329600 | bytes 28000000 | tf_op jit(solution)/shard_map/attend/pallas_call | solution.py:195
  145.0 19.3 %expand.2 = (f32[2048,768]{1,0:T(8,128)}, f32[2048,128]{1,0:T(8,128)}, bf16[2048,768]{1,0:T(8,128)(2,1)}, bf16[2048,3072]{1,0:T(8,128)(2,1)}, bf16[2048,3072]{1,0:T(8,128)(2,1)}) custom-call(s32[65]{0:T(128)} %fusion.table, bf16[2048,768]{1,0:T(8,128)(2,1)} %get-tuple-element.59.context, bf16[2048,768]{1,0:T(8,128)(2,1)} %get-tuple-element.60.x, ...), custom_call_target="tpu_custom_call" | custom-call | flops 6039797760 | bytes 20480000 | tf_op jit(solution)/shard_map/expand/pallas_call | solution.py:262
  164.2 19.0 %expand.3 = (f32[2048,768]{1,0:T(8,128)}, f32[2048,128]{1,0:T(8,128)}, bf16[2048,768]{1,0:T(8,128)(2,1)}, bf16[2048,3072]{1,0:T(8,128)(2,1)}, bf16[2048,3072]{1,0:T(8,128)(2,1)}) custom-call(s32[65]{0:T(128)} %fusion.table, ...), custom_call_target="tpu_custom_call", output_to_operand_aliasing={{0}: (7, {}), {1}: (8, {}), {2}: (9, {}), {3}: (10, {}), {4... | custom-call | flops 6039797760 | bytes 20480000 | tf_op jit(solution)/shard_map/expand/pallas_call | solution.py:262
  183.2 53.7 %reduce.19 = (bf16[2048,768]{1,0:T(8,128)(2,1)}, f32[2048,768]{1,0:T(8,128)}, bf16[2048,3072]{1,0:T(8,128)(2,1)}, f32[24,768]{1,0:T(8,128)}, f32[8,3072]{1,0:T(8...) custom-call(s32[65]{0:T(128)} %fusion.table, bf16[2048,3072]{1,0:T(8,128)(2,1)} %get-tuple-element.67.active, ...), custom_call_target="tpu_custom_call" | custom-call | flops 28991029248 | bytes 61440000 | tf_op jit(solution)/shard_map/reduce/pallas_call | solution.py:346
  237.0 40.8 %inner.1 = (f32[2048,768]{1,0:T(8,128)}, bf16[2048,768]{1,0:T(8,128)(2,1)}, f32[32,768]{1,0:T(8,128)}, bf16[768,1920]{1,0:T(8,128)(2,1)}, bf16[768,1920]{1,0:T(8,128)(2,1)}) custom-call(s32[65]{0:T(128)} %fusion.table, bf16[2048,3072]{1,0:T(8,128)(2,1)} %get-tuple-element.75.hidden, f32[2048,768]{1,0:T(8,128)} %get-tuple-element.76.outer, ...), custom_call_target="tpu_custom_call" | custom-call | flops 24159191040 | bytes 40960000 | tf_op jit(solution)/shard_map/inner/pallas_call | solution.py:428
  277.8 19.0 %attend_back.2.refs_0_ = bf16[2048,2304]{1,0:T(8,128)(2,1)} custom-call(bf16[2048,2304]{1,0:T(8,128)(2,1)} %get-tuple-element.71.qkv, bf16[4,12,512,512]{3,2,1,0:T(8,128)(2,1)} %get-tuple-element.72.raised_in, f32[4,16,512]{2,1,0:T(8,128)} %get-tuple-element.73.inverse_in, bf16[4,768,512]{2,1,0:T(8,128)(2,1)} %get-tuple-element.74.turned, ...), custom_call_target="tpu_custom_call" | custom-call | flops 12884901888 | bytes 28000000 | tf_op jit(solution)/shard_map/attend_back/pallas_call | solution.py:510
  296.8 18.7 %attend_back.3.mixed = bf16[2048,2304]{1,0:T(8,128)(2,1)} custom-call(bf16[2048,2304]{1,0:T(8,128)(2,1)} %get-tuple-element.71.qkv, bf16[4,12,512,512]{3,2,1,0:T(8,128)(2,1)} %get-tuple-element.72.raised_in, f32[4,16,512]{2,1,0:T(8,128)} %get-tuple-element.73.inverse_in, ...), custom_call_target="tpu_custom_call", output_to_operand_aliasing={{}: (5, {})} | custom-call | flops 12884901888 | bytes 28000000 | tf_op jit(solution)/shard_map/attend_back/pallas_call | solution.py:510
  316.4 15.5 %heads_grad.1 = (bf16[768,1280]{1,0:T(8,128)(2,1)}, bf16[768,1280]{1,0:T(8,128)(2,1)}) custom-call(s32[65]{0:T(128)} %fusion.table, bf16[2048,768]{1,0:T(8,128)(2,1)} %get-tuple-element.60.x, bf16[16,2048]{1,0:T(8,128)(2,1)} %maximum_maximum_fusion.marks, bf16[2048,2304]{1,0:T(8,128)(2,1)} %attend_back.3.mixed, f32[24,768]{1,0:T(8,128)} %get-tuple-element.81.second_sums, ...), custom_call_target="tpu_custom_call" | custom-call | flops 7247757312 | bytes 20480000 | tf_op jit(solution)/shard_map/heads_grad/pallas_call | solution.py:597
  333.0 5.3 %collective-permute-done.18 = bf16[768,1280]{1,0:T(8,128)(2,1)S(1)} collective-permute-done((bf16[768,1280]{1,0:T(8,128)(2,1)}, bf16[768,1280]{1,0:T(8,128)(2,1)S(1)}, u32[]{:S(2)}, u32[]{:S(2)}) %collective-permute-start.18) | collective-permute-done | bytes 1966112 | tf_op jit(solution)/shard_map/ppermute | solution.py:700
  338.3 2.9 add_convert_fusion.5
  341.2 1.5 collective-permute-start.19
  342.7 14.5 %rows_grad.1 = bf16[2048,768]{1,0:T(8,128)(2,1)} custom-call(s32[65]{0:T(128)} %fusion.table, bf16[2048,2304]{1,0:T(8,128)(2,1)} %attend_back.3.mixed, f32[2048,768]{1,0:T(8,128)} %get-tuple-element.80.inner, bf16[2048,128]{1,0:T(8,128)(2,1)} %broadcast_in_dim.40.mask, bf16[768,1280]{1,0:T(8,128)(2,1)} %constant_dynamic-update-slice_fusion.5.mine, ...), custom_call_target="tpu_custom_call" | custom-call | flops 7247757312 | bytes 20480000 | tf_op jit(solution)/shard_map/rows_grad/pallas_call | solution.py:641
  357.2 2.2 add_convert_fusion.3
  360.1 1.6 add_convert_fusion.11
  361.7 1.2 collective-permute-start.20
  363.0 3.7 add_convert_fusion.1
  366.7 1.2 collective-permute-start.26
  367.9 8.1 %collective-permute-done.20 = bf16[192,1280]{1,0:T(8,128)(2,1)S(1)} collective-permute-done((bf16[192,1280]{1,0:T(8,128)(2,1)S(1)}, bf16[192,1280]{1,0:T(8,128)(2,1)S(1)}, u32[]{:S(2)}, u32[]{:S(2)}) %collective-permute-start.20) | collective-permute-done | bytes 491552 | tf_op jit(solution)/shard_map/ppermute | solution.py:705
  376.0 5.0 %collective-permute-start.23 = (bf16[48,1280]{1,0:T(8,128)(2,1)S(1)}, bf16[48,1280]{1,0:T(8,128)(2,1)S(1)}, u32[]{:S(2)}, u32[]{:S(2)}) collective-permute-start(bf16[48,1280]{1,0:T(8,128)(2,1)S(1)} %get-tuple-element.120), channel_id=1, source_target_pairs={{0,24},{1,25},{2,26},{3,27},{4,28},{5,29},{6,30},{7,31},{8,0},{9,1... | collective-permute-start | bytes 368648 | tf_op jit(solution)/shard_map/ppermute | solution.py:712
  382.1 1.5 collective-permute-start.35
  383.6 1.3 collective-permute-done.23
  384.9 6.7 %collective-permute-done.22 = bf16[48,1280]{1,0:T(8,128)(2,1)S(1)} collective-permute-done((bf16[48,1280]{1,0:T(8,128)(2,1)S(1)}, bf16[48,1280]{1,0:T(8,128)(2,1)S(1)}, u32[]{:S(2)}, u32[]{:S(2)}) %collective-permute-start.22) | collective-permute-done | bytes 122912 | tf_op jit(solution)/shard_map/ppermute | solution.py:712
  394.1 1.0 broadcast_select_fusion.5
  395.1 8.1 %collective-permute-done.26 = bf16[384,1920]{1,0:T(8,128)(2,1)} collective-permute-done((bf16[384,1920]{1,0:T(8,128)(2,1)}, bf16[384,1920]{1,0:T(8,128)(2,1)}, u32[]{:S(2)}, u32[]{:S(2)}) %collective-permute-start.26) | collective-permute-done | bytes 1474592 | tf_op jit(solution)/shard_map/ppermute | solution.py:705
  403.2 1.7 add_convert_fusion.7
  404.9 1.2 collective-permute-start.27
  406.3 4.6 %collective-permute-start.38 = (bf16[192,384]{1,0:T(8,128)(2,1)S(1)}, bf16[192,384]{1,0:T(8,128)(2,1)S(1)}, u32[]{:S(2)}, u32[]{:S(2)}) collective-permute-start(bf16[192,384]{1,0:T(8,128)(2,1)S(1)} %get-tuple-element.117), channel_id=1, source_target_pairs={{0,24},{1,25},{2,26},{3,27},{4,28},{5,29},{6,30},{7,31},{8,0},{9,1... | collective-permute-start | bytes 442376 | tf_op jit(solution)/shard_map/ppermute | solution.py:712
  410.9 1.3 collective-permute-start.37
  413.0 2.2 collective-permute-done.38
  415.2 9.1 %collective-permute-done.37 = bf16[192,384]{1,0:T(8,128)(2,1)S(1)} collective-permute-done((bf16[192,384]{1,0:T(8,128)(2,1)S(1)}, bf16[192,384]{1,0:T(8,128)(2,1)S(1)}, u32[]{:S(2)}, u32[]{:S(2)}) %collective-permute-start.37) | collective-permute-done | bytes 147488 | tf_op jit(solution)/shard_map/ppermute | solution.py:712
  424.7 1.0 collective-permute-start.29
  425.6 1.9 collective-permute-start.28
  427.6 5.3 %collective-permute-done.30 = bf16[48,1920]{1,0:T(8,128)(2,1)S(1)} collective-permute-done((bf16[48,1920]{1,0:T(8,128)(2,1)S(1)}, bf16[48,1920]{1,0:T(8,128)(2,1)S(1)}, u32[]{:S(2)}, u32[]{:S(2)}) %collective-permute-start.30) | collective-permute-done | bytes 184352 | tf_op jit(solution)/shard_map/ppermute | solution.py:712
  433.0 9.7 %collective-permute-done.29 = bf16[48,1920]{1,0:T(8,128)(2,1)S(1)} collective-permute-done((bf16[48,1920]{1,0:T(8,128)(2,1)S(1)}, bf16[48,1920]{1,0:T(8,128)(2,1)S(1)}, u32[]{:S(2)}, u32[]{:S(2)}) %collective-permute-start.29) | collective-permute-done | bytes 184352 | tf_op jit(solution)/shard_map/ppermute | solution.py:712
  (118 shorter events, 24.8 us)
Async XLA Ops:
  0.6 11.1 %copy-start = (bf16[48,3072]{1,0:T(8,128)(2,1)S(1)}, bf16[48,3072]{1,0:T(8,128)(2,1)}, u32[]{:S(2)}) copy-start(bf16[48,3072]{1,0:T(8,128)(2,1)} %param.29) | copy-start | bytes 884740
  4.8 9.6 %collective-permute-start = (bf16[48,1280]{1,0:T(8,128)(2,1)}, bf16[48,1280]{1,0:T(8,128)(2,1)}, u32[]{:S(2)}, u32[]{:S(2)}) collective-permute-start(bf16[48,1280]{1,0:T(8,128)(2,1)} %get-tuple-element.159), channel_id=1, source_target_pairs={{0,8},{1,9},{2,10},{3,11},{4,12},{5,13},{6,14},{7,15},{8,16},{9,17... | collective-permute-start | bytes 368648 | tf_op jit(solution)/shard_map/ppermute | solution.py:684
  7.8 18.2 %collective-permute-start.1 = (bf16[48,1280]{1,0:T(8,128)(2,1)}, bf16[48,1280]{1,0:T(8,128)(2,1)}, u32[]{:S(2)}, u32[]{:S(2)}) collective-permute-start(bf16[48,1280]{1,0:T(8,128)(2,1)} %get-tuple-element.159), channel_id=1, source_target_pairs={{0,16},{1,17},{2,18},{3,19},{4,20},{5,21},{6,22},{7,23},{8,24},{9,... | collective-permute-start | bytes 368648 | tf_op jit(solution)/shard_map/ppermute | solution.py:684
  10.4 15.6 %collective-permute-start.2 = (bf16[48,1280]{1,0:T(8,128)(2,1)}, bf16[48,1280]{1,0:T(8,128)(2,1)}, u32[]{:S(2)}, u32[]{:S(2)}) collective-permute-start(bf16[48,1280]{1,0:T(8,128)(2,1)} %get-tuple-element.159), channel_id=1, source_target_pairs={{0,24},{1,25},{2,26},{3,27},{4,28},{5,29},{6,30},{7,31},{8,0},{9,1... | collective-permute-start | bytes 368648 | tf_op jit(solution)/shard_map/ppermute | solution.py:684
  12.6 20.6 %collective-permute-start.6 = (bf16[48,1920]{1,0:T(8,128)(2,1)S(1)}, bf16[48,1920]{1,0:T(8,128)(2,1)S(1)}, u32[]{:S(2)}, u32[]{:S(2)}) collective-permute-start(bf16[48,1920]{1,0:T(8,128)(2,1)S(1)} %get-tuple-element.144), channel_id=1, source_target_pairs={{0,8},{1,9},{2,10},{3,11},{4,12},{5,13},{6,14},{7,15},{8,16},{9,17... | collective-permute-start | bytes 552968 | tf_op jit(solution)/shard_map/ppermute | solution.py:684
  13.3 19.9 %collective-permute-start.7 = (bf16[48,1920]{1,0:T(8,128)(2,1)S(1)}, bf16[48,1920]{1,0:T(8,128)(2,1)S(1)}, u32[]{:S(2)}, u32[]{:S(2)}) collective-permute-start(bf16[48,1920]{1,0:T(8,128)(2,1)S(1)} %get-tuple-element.144), channel_id=1, source_target_pairs={{0,16},{1,17},{2,18},{3,19},{4,20},{5,21},{6,22},{7,23},{8,24},{9,... | collective-permute-start | bytes 552968 | tf_op jit(solution)/shard_map/ppermute | solution.py:684
  14.4 18.9 %collective-permute-start.8 = (bf16[48,1920]{1,0:T(8,128)(2,1)S(1)}, bf16[48,1920]{1,0:T(8,128)(2,1)S(1)}, u32[]{:S(2)}, u32[]{:S(2)}) collective-permute-start(bf16[48,1920]{1,0:T(8,128)(2,1)S(1)} %get-tuple-element.144), channel_id=1, source_target_pairs={{0,24},{1,25},{2,26},{3,27},{4,28},{5,29},{6,30},{7,31},{8,0},{9,1... | collective-permute-start | bytes 552968 | tf_op jit(solution)/shard_map/ppermute | solution.py:684
  27.1 8.9 %collective-permute-start.3 = (bf16[192,1280]{1,0:T(8,128)(2,1)S(1)}, bf16[192,1280]{1,0:T(8,128)(2,1)S(1)}, u32[]{:S(2)}, u32[]{:S(2)}) collective-permute-start(bf16[192,1280]{1,0:T(8,128)(2,1)S(1)} %pad_maximum_fusion.4), channel_id=1, source_target_pairs={{0,2},{1,5},{2,0},{3,7},{4,6},{5,1},{6,4},{7,3},{8,10},{9,13},{10,... | collective-permute-start | bytes 1474568 | tf_op jit(solution)/shard_map/ppermute | solution.py:686
  33.2 2.8 copy-start.8
  33.3 18.3 %collective-permute-start.9 = (bf16[192,1920]{1,0:T(8,128)(2,1)S(1)}, bf16[192,1920]{1,0:T(8,128)(2,1)S(1)}, u32[]{:S(2)}, u32[]{:S(2)}) collective-permute-start(bf16[192,1920]{1,0:T(8,128)(2,1)S(1)} %pad_maximum_fusion), channel_id=1, source_target_pairs={{0,2},{1,5},{2,0},{3,7},{4,6},{5,1},{6,4},{7,3},{8,10},{9,13},{10,... | collective-permute-start | bytes 2211848 | tf_op jit(solution)/shard_map/ppermute | solution.py:686
  36.8 17.6 %copy-start.6 = (bf16[192,768]{1,0:T(8,128)(2,1)S(1)}, bf16[192,768]{1,0:T(8,128)(2,1)}, u32[]{:S(2)}) copy-start(bf16[192,768]{1,0:T(8,128)(2,1)} %param.31) | copy-start | bytes 884740
  36.8 32.6 %collective-permute-start.4 = (bf16[384,1280]{1,0:T(8,128)(2,1)S(1)}, bf16[384,1280]{1,0:T(8,128)(2,1)S(1)}, u32[]{:S(2)}, u32[]{:S(2)}) collective-permute-start(bf16[384,1280]{1,0:T(8,128)(2,1)S(1)} %get-tuple-element.130), channel_id=1, source_target_pairs={{0,4},{1,3},{2,6},{3,1},{4,0},{5,7},{6,2},{7,5},{8,12},{9,11},{10,... | collective-permute-start | bytes 2949128 | tf_op jit(solution)/shard_map/ppermute | solution.py:687
  51.8 28.3 %collective-permute-start.10 = (bf16[384,1920]{1,0:T(8,128)(2,1)S(1)}, bf16[384,1920]{1,0:T(8,128)(2,1)S(1)}, u32[]{:S(2)}, u32[]{:S(2)}) collective-permute-start(bf16[384,1920]{1,0:T(8,128)(2,1)S(1)} %get-tuple-element.122), channel_id=1, source_target_pairs={{0,4},{1,3},{2,6},{3,1},{4,0},{5,7},{6,2},{7,5},{8,12},{9,11},{10,... | collective-permute-start | bytes 4423688 | tf_op jit(solution)/shard_map/ppermute | solution.py:687
  55.1 8.7 %collective-permute-start.12 = (bf16[192,384]{1,0:T(8,128)(2,1)S(1)}, bf16[192,384]{1,0:T(8,128)(2,1)S(1)}, u32[]{:S(2)}, u32[]{:S(2)}) collective-permute-start(bf16[192,384]{1,0:T(8,128)(2,1)S(1)} %get-tuple-element.100), channel_id=1, source_target_pairs={{0,8},{1,9},{2,10},{3,11},{4,12},{5,13},{6,14},{7,15},{8,16},{9,17... | collective-permute-start | bytes 442376 | tf_op jit(solution)/shard_map/ppermute | solution.py:684
  58.5 8.5 %collective-permute-start.13 = (bf16[192,384]{1,0:T(8,128)(2,1)S(1)}, bf16[192,384]{1,0:T(8,128)(2,1)S(1)}, u32[]{:S(2)}, u32[]{:S(2)}) collective-permute-start(bf16[192,384]{1,0:T(8,128)(2,1)S(1)} %get-tuple-element.100), channel_id=1, source_target_pairs={{0,16},{1,17},{2,18},{3,19},{4,20},{5,21},{6,22},{7,23},{8,24},{9,... | collective-permute-start | bytes 442376 | tf_op jit(solution)/shard_map/ppermute | solution.py:684
  61.2 6.7 %collective-permute-start.14 = (bf16[192,384]{1,0:T(8,128)(2,1)S(1)}, bf16[192,384]{1,0:T(8,128)(2,1)S(1)}, u32[]{:S(2)}, u32[]{:S(2)}) collective-permute-start(bf16[192,384]{1,0:T(8,128)(2,1)S(1)} %get-tuple-element.100), channel_id=1, source_target_pairs={{0,24},{1,25},{2,26},{3,27},{4,28},{5,29},{6,30},{7,31},{8,0},{9,1... | collective-permute-start | bytes 442376 | tf_op jit(solution)/shard_map/ppermute | solution.py:684
  67.9 9.9 %collective-permute-start.15 = (bf16[768,384]{1,0:T(8,128)(2,1)S(1)}, bf16[768,384]{1,0:T(8,128)(2,1)S(1)}, u32[]{:S(2)}, u32[]{:S(2)}) collective-permute-start(bf16[768,384]{1,0:T(8,128)(2,1)S(1)} %pad_maximum_fusion.1), channel_id=1, source_target_pairs={{0,2},{1,5},{2,0},{3,7},{4,6},{5,1},{6,4},{7,3},{8,10},{9,13},{10,... | collective-permute-start | bytes 1769480 | tf_op jit(solution)/shard_map/ppermute | solution.py:686
  70.5 27.5 %collective-permute-start.5 = (bf16[768,1280]{1,0:T(8,128)(2,1)}, bf16[768,1280]{1,0:T(8,128)(2,1)}, u32[]{:S(2)}, u32[]{:S(2)}) collective-permute-start(bf16[768,1280]{1,0:T(8,128)(2,1)} %constant_dynamic-update-slice_fusion.5.mine), channel_id=1, source_target_pairs={{0,1},{1,0},{2,3},{3,2},{4,5},{5,4},{6,7},{7,6},{8,9},{9,8},{10,11... | collective-permute-start | bytes 5898248 | tf_op jit(solution)/shard_map/ppermute | solution.py:688
  77.9 2.6 copy-start.7
  79.0 16.5 %collective-permute-start.16 = (bf16[1536,384]{1,0:T(8,128)(2,1)}, bf16[1536,384]{1,0:T(8,128)(2,1)}, u32[]{:S(2)}, u32[]{:S(2)}) collective-permute-start(bf16[1536,384]{1,0:T(8,128)(2,1)} %get-tuple-element.128), channel_id=1, source_target_pairs={{0,4},{1,3},{2,6},{3,1},{4,0},{5,7},{6,2},{7,5},{8,12},{9,11},{10,... | collective-permute-start | bytes 3538952 | tf_op jit(solution)/shard_map/ppermute | solution.py:687
  80.4 40.7 %copy-start.2 = (bf16[768,1920]{1,0:T(8,128)(2,1)}, bf16[768,1920]{1,0:T(8,128)(2,1)S(1)}, u32[]{:S(2)}) copy-start(bf16[768,1920]{1,0:T(8,128)(2,1)S(1)} %constant_dynamic-update-slice_fusion.16.mine) | copy-start | bytes 8847364
  80.4 64.6 %collective-permute-start.11 = (bf16[768,1920]{1,0:T(8,128)(2,1)S(1)}, bf16[768,1920]{1,0:T(8,128)(2,1)}, u32[]{:S(2)}, u32[]{:S(2)}) collective-permute-start(bf16[768,1920]{1,0:T(8,128)(2,1)S(1)} %constant_dynamic-update-slice_fusion.16.mine), channel_id=1, source_target_pairs={{0,1},{1,0},{2,3},{3,2},{4,5},{5,4},{6,7},{7,6},{8,9},{9,8},{10,11... | collective-permute-start | bytes 8847368 | tf_op jit(solution)/shard_map/ppermute | solution.py:688
  97.9 85.3 %collective-permute-start.17 = (bf16[3072,384]{1,0:T(8,128)(2,1)}, bf16[3072,384]{1,0:T(8,128)(2,1)}, u32[]{:S(2)}, u32[]{:S(2)}) collective-permute-start(bf16[3072,384]{1,0:T(8,128)(2,1)} %constant_dynamic-update-slice_fusion.27.mine), channel_id=1, source_target_pairs={{0,1},{1,0},{2,3},{3,2},{4,5},{5,4},{6,7},{7,6},{8,9},{9,8},{10,11... | collective-permute-start | bytes 7077896 | tf_op jit(solution)/shard_map/ppermute | solution.py:688
  296.8 18.8 %copy-start.5 = (f32[8,3072]{1,0:T(8,128)S(1)}, f32[8,3072]{1,0:T(8,128)}, u32[]{:S(2)}) copy-start(f32[8,3072]{1,0:T(8,128)} %get-tuple-element.83) | copy-start | bytes 294916
  331.9 6.4 %collective-permute-start.18 = (bf16[768,1280]{1,0:T(8,128)(2,1)}, bf16[768,1280]{1,0:T(8,128)(2,1)S(1)}, u32[]{:S(2)}, u32[]{:S(2)}) collective-permute-start(bf16[768,1280]{1,0:T(8,128)(2,1)} %get-tuple-element.85), channel_id=1, source_target_pairs={{0,1},{1,0},{2,3},{3,2},{4,5},{5,4},{6,7},{7,6},{8,9},{9,8},{10,11... | collective-permute-start | bytes 5898248 | tf_op jit(solution)/shard_map/ppermute | solution.py:700
  332.5 24.8 %collective-permute-start.33 = (bf16[3072,384]{1,0:T(8,128)(2,1)}, bf16[3072,384]{1,0:T(8,128)(2,1)}, u32[]{:S(2)}, u32[]{:S(2)}) collective-permute-start(bf16[3072,384]{1,0:T(8,128)(2,1)} %get-tuple-element.89), channel_id=1, source_target_pairs={{0,1},{1,0},{2,3},{3,2},{4,5},{5,4},{6,7},{7,6},{8,9},{9,8},{10,11... | collective-permute-start | bytes 7077896 | tf_op jit(solution)/shard_map/ppermute | solution.py:700
  332.5 30.5 %collective-permute-start.25 = (bf16[768,1920]{1,0:T(8,128)(2,1)}, bf16[768,1920]{1,0:T(8,128)(2,1)}, u32[]{:S(2)}, u32[]{:S(2)}) collective-permute-start(bf16[768,1920]{1,0:T(8,128)(2,1)} %get-tuple-element.87), channel_id=1, source_target_pairs={{0,1},{1,0},{2,3},{3,2},{4,5},{5,4},{6,7},{7,6},{8,9},{9,8},{10,11... | collective-permute-start | bytes 8847368 | tf_op jit(solution)/shard_map/ppermute | solution.py:700
  341.2 18.9 %collective-permute-start.19 = (bf16[384,1280]{1,0:T(8,128)(2,1)}, bf16[384,1280]{1,0:T(8,128)(2,1)}, u32[]{:S(2)}, u32[]{:S(2)}) collective-permute-start(bf16[384,1280]{1,0:T(8,128)(2,1)} %get-tuple-element.106), channel_id=1, source_target_pairs={{0,2},{1,5},{2,0},{3,7},{4,6},{5,1},{6,4},{7,3},{8,10},{9,13},{10,... | collective-permute-start | bytes 2949128 | tf_op jit(solution)/shard_map/ppermute | solution.py:705
  342.7 14.5 %copy-start.4 = (bf16[3072,384]{1,0:T(8,128)(2,1)S(1)}, bf16[3072,384]{1,0:T(8,128)(2,1)}, u32[]{:S(2)}) copy-start(bf16[3072,384]{1,0:T(8,128)(2,1)} %get-tuple-element.88) | copy-start | bytes 7077892
  359.4 3.5 copy-start.3
  359.5 22.3 %collective-permute-start.34 = (bf16[1536,384]{1,0:T(8,128)(2,1)S(1)}, bf16[1536,384]{1,0:T(8,128)(2,1)S(1)}, u32[]{:S(2)}, u32[]{:S(2)}) collective-permute-start(bf16[1536,384]{1,0:T(8,128)(2,1)S(1)} %get-tuple-element.104), channel_id=1, source_target_pairs={{0,2},{1,5},{2,0},{3,7},{4,6},{5,1},{6,4},{7,3},{8,10},{9,13},{10,... | collective-permute-start | bytes 3538952 | tf_op jit(solution)/shard_map/ppermute | solution.py:705
  361.7 14.2 %collective-permute-start.20 = (bf16[192,1280]{1,0:T(8,128)(2,1)S(1)}, bf16[192,1280]{1,0:T(8,128)(2,1)S(1)}, u32[]{:S(2)}, u32[]{:S(2)}) collective-permute-start(bf16[192,1280]{1,0:T(8,128)(2,1)S(1)} %get-tuple-element.112), channel_id=1, source_target_pairs={{0,4},{1,3},{2,6},{3,1},{4,0},{5,7},{6,2},{7,5},{8,12},{9,11},{10,... | collective-permute-start | bytes 1474568 | tf_op jit(solution)/shard_map/ppermute | solution.py:705
  366.7 36.5 %collective-permute-start.26 = (bf16[384,1920]{1,0:T(8,128)(2,1)}, bf16[384,1920]{1,0:T(8,128)(2,1)}, u32[]{:S(2)}, u32[]{:S(2)}) collective-permute-start(bf16[384,1920]{1,0:T(8,128)(2,1)} %get-tuple-element.102), channel_id=1, source_target_pairs={{0,2},{1,5},{2,0},{3,7},{4,6},{5,1},{6,4},{7,3},{8,10},{9,13},{10,... | collective-permute-start | bytes 4423688 | tf_op jit(solution)/shard_map/ppermute | solution.py:705
  376.0 8.8 %collective-permute-start.23 = (bf16[48,1280]{1,0:T(8,128)(2,1)S(1)}, bf16[48,1280]{1,0:T(8,128)(2,1)S(1)}, u32[]{:S(2)}, u32[]{:S(2)}) collective-permute-start(bf16[48,1280]{1,0:T(8,128)(2,1)S(1)} %get-tuple-element.120), channel_id=1, source_target_pairs={{0,24},{1,25},{2,26},{3,27},{4,28},{5,29},{6,30},{7,31},{8,0},{9,1... | collective-permute-start | bytes 368648 | tf_op jit(solution)/shard_map/ppermute | solution.py:712
  381.1 10.4 %collective-permute-start.22 = (bf16[48,1280]{1,0:T(8,128)(2,1)S(1)}, bf16[48,1280]{1,0:T(8,128)(2,1)S(1)}, u32[]{:S(2)}, u32[]{:S(2)}) collective-permute-start(bf16[48,1280]{1,0:T(8,128)(2,1)S(1)} %get-tuple-element.121), channel_id=1, source_target_pairs={{0,16},{1,17},{2,18},{3,19},{4,20},{5,21},{6,22},{7,23},{8,24},{9,... | collective-permute-start | bytes 368648 | tf_op jit(solution)/shard_map/ppermute | solution.py:712
  381.6 9.9 %collective-permute-start.21 = (bf16[48,1280]{1,0:T(8,128)(2,1)S(1)}, bf16[48,1280]{1,0:T(8,128)(2,1)S(1)}, u32[]{:S(2)}, u32[]{:S(2)}) collective-permute-start(bf16[48,1280]{1,0:T(8,128)(2,1)S(1)} %get-tuple-element.119), channel_id=1, source_target_pairs={{0,8},{1,9},{2,10},{3,11},{4,12},{5,13},{6,14},{7,15},{8,16},{9,17... | collective-permute-start | bytes 368648 | tf_op jit(solution)/shard_map/ppermute | solution.py:712
  382.1 24.1 %collective-permute-start.35 = (bf16[768,384]{1,0:T(8,128)(2,1)S(1)}, bf16[768,384]{1,0:T(8,128)(2,1)S(1)}, u32[]{:S(2)}, u32[]{:S(2)}) collective-permute-start(bf16[768,384]{1,0:T(8,128)(2,1)S(1)} %get-tuple-element.110), channel_id=1, source_target_pairs={{0,4},{1,3},{2,6},{3,1},{4,0},{5,7},{6,2},{7,5},{8,12},{9,11},{10,... | collective-permute-start | bytes 1769480 | tf_op jit(solution)/shard_map/ppermute | solution.py:705
  392.3 1.8 collective-permute-start.24
  404.9 19.5 %collective-permute-start.27 = (bf16[192,1920]{1,0:T(8,128)(2,1)S(1)}, bf16[192,1920]{1,0:T(8,128)(2,1)S(1)}, u32[]{:S(2)}, u32[]{:S(2)}) collective-permute-start(bf16[192,1920]{1,0:T(8,128)(2,1)S(1)} %get-tuple-element.108), channel_id=1, source_target_pairs={{0,4},{1,3},{2,6},{3,1},{4,0},{5,7},{6,2},{7,5},{8,12},{9,11},{10,... | collective-permute-start | bytes 2211848 | tf_op jit(solution)/shard_map/ppermute | solution.py:705
  406.3 8.9 %collective-permute-start.38 = (bf16[192,384]{1,0:T(8,128)(2,1)S(1)}, bf16[192,384]{1,0:T(8,128)(2,1)S(1)}, u32[]{:S(2)}, u32[]{:S(2)}) collective-permute-start(bf16[192,384]{1,0:T(8,128)(2,1)S(1)} %get-tuple-element.117), channel_id=1, source_target_pairs={{0,24},{1,25},{2,26},{3,27},{4,28},{5,29},{6,30},{7,31},{8,0},{9,1... | collective-permute-start | bytes 442376 | tf_op jit(solution)/shard_map/ppermute | solution.py:712
  410.9 13.4 %collective-permute-start.37 = (bf16[192,384]{1,0:T(8,128)(2,1)S(1)}, bf16[192,384]{1,0:T(8,128)(2,1)S(1)}, u32[]{:S(2)}, u32[]{:S(2)}) collective-permute-start(bf16[192,384]{1,0:T(8,128)(2,1)S(1)} %get-tuple-element.118), channel_id=1, source_target_pairs={{0,16},{1,17},{2,18},{3,19},{4,20},{5,21},{6,22},{7,23},{8,24},{9,... | collective-permute-start | bytes 442376 | tf_op jit(solution)/shard_map/ppermute | solution.py:712
  412.2 12.1 %collective-permute-start.36 = (bf16[192,384]{1,0:T(8,128)(2,1)S(1)}, bf16[192,384]{1,0:T(8,128)(2,1)S(1)}, u32[]{:S(2)}, u32[]{:S(2)}) collective-permute-start(bf16[192,384]{1,0:T(8,128)(2,1)S(1)} %get-tuple-element.116), channel_id=1, source_target_pairs={{0,8},{1,9},{2,10},{3,11},{4,12},{5,13},{6,14},{7,15},{8,16},{9,17... | collective-permute-start | bytes 442376 | tf_op jit(solution)/shard_map/ppermute | solution.py:712
  424.3 3.2 collective-permute-start.39
  424.6 8.4 %collective-permute-start.30 = (bf16[48,1920]{1,0:T(8,128)(2,1)S(1)}, bf16[48,1920]{1,0:T(8,128)(2,1)S(1)}, u32[]{:S(2)}, u32[]{:S(2)}) collective-permute-start(bf16[48,1920]{1,0:T(8,128)(2,1)S(1)} %get-tuple-element.114), channel_id=1, source_target_pairs={{0,24},{1,25},{2,26},{3,27},{4,28},{5,29},{6,30},{7,31},{8,0},{9,1... | collective-permute-start | bytes 552968 | tf_op jit(solution)/shard_map/ppermute | solution.py:712
  424.7 18.0 %collective-permute-start.29 = (bf16[48,1920]{1,0:T(8,128)(2,1)S(1)}, bf16[48,1920]{1,0:T(8,128)(2,1)S(1)}, u32[]{:S(2)}, u32[]{:S(2)}) collective-permute-start(bf16[48,1920]{1,0:T(8,128)(2,1)S(1)} %get-tuple-element.115), channel_id=1, source_target_pairs={{0,16},{1,17},{2,18},{3,19},{4,20},{5,21},{6,22},{7,23},{8,24},{9,... | collective-permute-start | bytes 552968 | tf_op jit(solution)/shard_map/ppermute | solution.py:712
  425.6 17.1 %collective-permute-start.28 = (bf16[48,1920]{1,0:T(8,128)(2,1)S(1)}, bf16[48,1920]{1,0:T(8,128)(2,1)S(1)}, u32[]{:S(2)}, u32[]{:S(2)}) collective-permute-start(bf16[48,1920]{1,0:T(8,128)(2,1)S(1)} %get-tuple-element.113), channel_id=1, source_target_pairs={{0,8},{1,9},{2,10},{3,11},{4,12},{5,13},{6,14},{7,15},{8,16},{9,17... | collective-permute-start | bytes 552968 | tf_op jit(solution)/shard_map/ppermute | solution.py:712
  442.8 1.5 collective-permute-start.31
  442.9 3.6 copy-start.1
  443.8 1.8 collective-permute-start.32

commit v2 on v1

v2 whole, which is shorter than its diff:
```python
import functools

import jax
import jax.numpy as jnp
import numpy as np
from jax import lax
from jax.experimental import pallas as pl
from jax.experimental.pallas import tpu as pltpu
from jax.sharding import PartitionSpec as P

D = 768
HEADS = 12
HEAD_DIM = 64
FF = 3072
L = 512
QKV = 3 * D
LANES = 128
BLOCKS = 16
EPSILON = 1e-06
ALL = ("fsdp", "rep")
VECTORS = 13

bf16 = jnp.bfloat16
f32 = jnp.float32

NN = ((1,), (0,))
NT = ((1,), (1,))
TN = ((0,), (0,))


def dot(left, right, dims):
    return lax.dot_general(left, right, (dims, ((), ())), preferred_element_type=f32)


def params():
    return pltpu.CompilerParams(vmem_limit_bytes=60 << 20)


def shaped(shape, dtype):
    return jax.ShapeDtypeStruct(shape, dtype)


def rows(size, width, shift=0):
    return pl.BlockSpec((size, width), lambda i: (i + shift, 0))


def whole(shape):
    return pl.BlockSpec(shape, lambda i: (0,) * len(shape), pipeline_mode=pl.Buffered(1))


SMEM = pl.BlockSpec(memory_space=pltpu.SMEM)
ANY = pl.BlockSpec(memory_space=pl.ANY)


def fetch_copies(table, pieces, target, sems, height, source_column, width):
    core = table[64]
    copies = []
    for half in range(2):
        place = core if half == 0 else 1 - core
        column = pl.multiple_of(place * width, LANES)
        for block in range(BLOCKS):
            owner = table[16 * half + block]
            source = pieces[2 * half + block // 8]
            copies.append(
                pltpu.make_async_copy(
                    source.at[pl.ds(block % 8 * height, height), pl.ds(source_column, width)],
                    target.at[pl.ds(pl.multiple_of(owner * height, 16), height), pl.ds(column, width)],
                    sems.at[16 * half + block],
                )
            )
    return copies


def spread_copies(table, staged, keep, send, sems, height, target_column, width):
    core = table[64]
    copies = []
    for half, target in ((0, keep), (1, send)):
        place = core if half == 0 else 1 - core
        column = pl.multiple_of(place * width, LANES)
        for block in range(BLOCKS):
            owner = table[32 + 16 * half + block]
            copies.append(
                pltpu.make_async_copy(
                    staged.at[pl.ds(pl.multiple_of(owner * height, 16), height), pl.ds(column, width)],
                    target.at[pl.ds(block * height, height), pl.ds(target_column, width)],
                    sems.at[16 * half + block],
                )
            )
    return copies


def start_all(copies):
    for copy in copies:
        copy.start()


def wait_all(copies):
    for copy in copies:
        copy.wait()


def fold(values):
    height, width = values.shape
    return jnp.sum(values.reshape(height // 8, 8, width), axis=0)


def six(column):
    return jnp.concatenate([column] * (D // LANES), axis=1)


def lane_first(height):
    return lax.broadcasted_iota(jnp.int32, (height, LANES), 1) < HEAD_DIM


def normalise(values):
    mean = jnp.mean(values, axis=1, keepdims=True)
    centred = values - mean
    spread = jnp.mean(centred * centred, axis=1, keepdims=True)
    rate = lax.rsqrt(spread + EPSILON)
    return centred * rate, rate


def norm_back(weighted, unit, rate):
    return rate * (
        weighted
        - jnp.mean(weighted, axis=1, keepdims=True)
        - unit * jnp.mean(weighted * unit, axis=1, keepdims=True)
    )


def attend_kernel(table, tokens, mask, *refs):
    pieces = refs[:4]
    x_out, qkv_out, raised_out, inverse_out, context_out, turned_out, vec_out, weight_out = refs[-14:-6]
    weight, columns, vectors, sems, vec_sems, out_sem = refs[-6:]

    @pl.when(pl.program_id(0) == 0)
    def _():
        copies = fetch_copies(table, pieces, weight, sems, D // BLOCKS, 0, QKV // 2)
        height = D // BLOCKS
        for block in range(BLOCKS):
            copies.append(
                pltpu.make_async_copy(
                    pieces[block // 8].at[pl.ds(block % 8 * height, height), pl.ds(QKV // 2, LANES)],
                    columns.at[pl.ds(pl.multiple_of(table[block] * height, 16), height), :],
                    vec_sems.at[block],
                )
            )
        start_all(copies)
        wait_all(copies)
        vectors[...] = columns[...].astype(f32).T[:16]
        vec_out[...] = vectors[...]
        pltpu.make_async_copy(weight, weight_out, out_sem).start()

    @pl.when(pl.program_id(0) == pl.num_programs(0) - 1)
    def _():
        pltpu.make_async_copy(weight, weight_out, out_sem).wait()

    chosen = six(mask[...]) > 0
    x = jnp.where(chosen, jnp.broadcast_to(vectors[0:1, :].astype(bf16), (L, D)), tokens[...])
    x_out[...] = x
    queries = dot(x, weight[:, :D], NN) + vectors[1:2, :]
    qkv_out[:, :D] = queries.astype(bf16) * jnp.asarray(HEAD_DIM**-0.5, bf16)
    qkv_out[:, D : 2 * D] = dot(x, weight[:, D : 2 * D], NN).astype(bf16)
    qkv_out[:, 2 * D :] = (dot(x, weight[:, 2 * D :], NN) + vectors[2:3, :]).astype(bf16)
    first = lane_first(L)
    scores = {}
    raised = {}

    def score(head):
        low = LANES * (head // 2)
        queries = qkv_out[:, low : low + LANES]
        lanes = first if head % 2 == 0 else ~first
        keys = qkv_out[:, D + low : D + low + LANES]
        scores[head] = dot(keys, jnp.where(lanes, queries, jnp.zeros_like(queries)), NT)

    def raise_scores(head):
        own = scores.pop(head)
        raised[head] = jnp.exp(own - jnp.max(own, axis=0, keepdims=True)).astype(bf16)
        raised_out[head] = raised[head]

    def mix(head, values):
        part = head % 2
        stacked = jnp.concatenate(
            [values[HEAD_DIM * part : HEAD_DIM * (part + 1)], jnp.ones((16, L), bf16)], axis=0
        )
        mixed = dot(stacked, raised.pop(head), NN)
        inverse = 1.0 / mixed[HEAD_DIM : HEAD_DIM + 1]
        inverse_out[head : head + 1, :] = inverse
        turned_out[HEAD_DIM * head : HEAD_DIM * (head + 1), :] = (mixed[:HEAD_DIM] * inverse).astype(bf16)

    score(0)
    score(1)
    for pair in range(HEADS // 2):
        for head in (2 * pair, 2 * pair + 1):
            raise_scores(head)
            if head + 2 < HEADS:
                score(head + 2)
        low = 2 * D + LANES * pair
        values = qkv_out[:, low : low + LANES].T
        mix(2 * pair, values)
        mix(2 * pair + 1, values)
    context_out[...] = turned_out[...].T


def attend(table, tokens, mask, pieces, earlier, start, count, after=()):
    height = tokens.shape[0]
    total = height // L
    passed = list(earlier[:6]) if earlier else []
    return pl.pallas_call(
        attend_kernel,
        name="attend",
        grid=(count,),
        in_specs=[SMEM, rows(L, D, start), rows(L, LANES, start)] + [ANY] * (4 + len(passed) + len(after)),
        out_specs=[
            rows(L, D, start),
            rows(L, QKV, start),
            pl.BlockSpec((None, HEADS, L, L), lambda i: (i + start, 0, 0, 0)),
            pl.BlockSpec((None, 16, L), lambda i: (i + start, 0, 0)),
            rows(L, D, start),
            pl.BlockSpec((None, D, L), lambda i: (i + start, 0, 0)),
            whole((16, D)),
            ANY,
        ],
        out_shape=[
            shaped((height, D), bf16),
            shaped((height, QKV), bf16),
            shaped((total, HEADS, L, L), bf16),
            shaped((total, 16, L), f32),
            shaped((height, D), bf16),
            shaped((total, D, L), bf16),
            shaped((16, D), f32),
            shaped((D, QKV), bf16),
        ],
        scratch_shapes=[
            pltpu.VMEM((D, QKV), bf16),
            pltpu.VMEM((D, LANES), bf16),
            pltpu.VMEM((16, D), f32),
            pltpu.SemaphoreType.DMA((32,)),
            pltpu.SemaphoreType.DMA((16,)),
            pltpu.SemaphoreType.DMA,
        ],
        input_output_aliases={7 + i: i for i in range(len(passed))},
        compiler_params=params(),
        cost_estimate=pl.CostEstimate(
            flops=10 * count * (2 * L * D * QKV + 16 * L * L * D), bytes_accessed=count * 14_000_000, transcendentals=0
        ),
    )(table, tokens, mask, *pieces, *passed, *after)


def expand_kernel(table, context, x, vec, bias, *refs):
    pieces = refs[:4]
    unit_out, rate_out, low_out, active_out, slope_out, out_weight_out, weight_out = refs[-13:-6]
    out_weight, weight, sems, more_sems, out_sem, more_out_sem = refs[-6:]
    step = pl.program_id(0)

    @pl.when(step == 0)
    def _():
        copies = fetch_copies(table, pieces, out_weight, sems, D // BLOCKS, 0, D // 2)
        start_all(copies)
        start_all(fetch_copies(table, pieces, weight, more_sems, D // BLOCKS, D // 2, FF // 2))
        wait_all(copies)

    first_sum = x[...].astype(f32) + (dot(context[...], out_weight[...], NN) + vec[3:4, :])
    unit, rate = normalise(first_sum)
    unit_out[...] = unit
    rate_out[...] = jnp.broadcast_to(rate, rate_out.shape)
    low = (unit * vec[4:5, :] + vec[5:6, :]).astype(bf16)
    low_out[...] = low

    @pl.when(step == 0)
    def _():
        wait_all(fetch_copies(table, pieces, weight, more_sems, D // BLOCKS, D // 2, FF // 2))
        pltpu.make_async_copy(out_weight, out_weight_out, out_sem).start()
        pltpu.make_async_copy(weight, weight_out, more_out_sem).start()

    @pl.when(step == 1)
    def _():
        pltpu.make_async_copy(out_weight, out_weight_out, out_sem).wait()
        pltpu.make_async_copy(weight, weight_out, more_out_sem).wait()

    width = 1024
    for part in range(FF // width):
        span = slice(width * part, width * (part + 1))
        hidden = dot(low, weight[:, span], NN) + bias[0:1, span]
        scaled = hidden * 2.0**-0.5
        share = 0.5 * lax.erf(scaled) + 0.5
        active_out[:, span] = (hidden * share).astype(bf16)
        slope_out[:, span] = (share + scaled * jnp.exp(-(scaled * scaled)) * np.pi**-0.5).astype(bf16)


def expand(table, context, x, vec, bias, pieces, size, after=()):
    height = x.shape[0]
    return pl.pallas_call(
        expand_kernel,
        name="expand",
        grid=(height // size,),
        in_specs=[SMEM, rows(size, D), rows(size, D), whole((16, D)), whole((1, FF))] + [ANY] * (4 + len(after)),
        out_specs=[rows(size, D), rows(size, LANES), rows(size, D), rows(size, FF), rows(size, FF), ANY, ANY],
        out_shape=[
            shaped((height, D), f32),
            shaped((height, LANES), f32),
            shaped((height, D), bf16),
            shaped((height, FF), bf16),
            shaped((height, FF), bf16),
            shaped((D, D), bf16),
            shaped((D, FF), bf16),
        ],
        scratch_shapes=[
            pltpu.VMEM((D, D), bf16),
            pltpu.VMEM((D, FF), bf16),
            pltpu.SemaphoreType.DMA((32,)),
            pltpu.SemaphoreType.DMA((32,)),
            pltpu.SemaphoreType.DMA,
            pltpu.SemaphoreType.DMA,
        ],
        compiler_params=params(),
        cost_estimate=pl.CostEstimate(
            flops=10 * height * 2 * D * (D + FF), bytes_accessed=height * 20_000, transcendentals=0
        ),
    )(table, context, x, vec, bias, *pieces, *after)


def reduce_kernel(table, active, slope, unit_in, low_in, cotangent, mask, vec, *refs):
    pieces = refs[:4]
    outputs, outer_out, hidden_out, sums, bias_sums, keep, send = refs[-13:-6]
    weight, total, expand_total, expand_staged, sems, out_sems = refs[-6:]
    staged = weight
    step = pl.program_id(0)

    @pl.when(step == 0)
    def _():
        copies = fetch_copies(table, pieces, weight, sems, FF // BLOCKS, 0, D // 2)
        start_all(copies)
        sums[...] = jnp.zeros_like(sums)
        bias_sums[...] = jnp.zeros_like(bias_sums)
        total[...] = jnp.zeros_like(total)
        expand_total[...] = jnp.zeros_like(expand_total)
        wait_all(copies)

    height = active.shape[0]
    parts = 2
    share = height // parts
    lows = []
    for part in range(parts):
        span = slice(share * part, share * (part + 1))
        normed = unit_in[span, :] * vec[4:5, :] + vec[5:6, :]
        second = normed + (dot(active[span, :], weight[...], NN) + vec[10:11, :])
        unit, rate = normalise(second)
        outputs[span, :] = (unit * vec[11:12, :] + vec[12:13, :]).astype(bf16)
        upstream = jnp.where(six(mask[span, :]) > 0, cotangent[span, :].astype(f32), 0.0)
        outer = norm_back(upstream * vec[11:12, :], unit, rate)
        outer_out[span, :] = outer
        low = outer.astype(bf16)
        sums[0:8, :] += fold(upstream * unit)
        sums[8:16, :] += fold(upstream)
        sums[16:24, :] += fold(low.astype(f32))
        lows.append(low)
    low = jnp.concatenate(lows, axis=0)
    groups = FF // D
    for group in range(groups):
        units = slice(D * group, D * (group + 1))
        total[units, :] += dot(active[:, units], low, TN)
        for part in range(parts):
            span = slice(share * part, share * (part + 1))
            grad = dot(lows[part], weight[units, :], NT) * slope[span, units].astype(f32)
            grad_low = grad.astype(bf16)
            hidden_out[span, units] = grad_low
            bias_sums[:, units] += fold(grad_low.astype(f32))
        if group:
            before = slice(D * (group - 1), D * group)
            expand_total[:, before] += dot(low_in[...], hidden_out[:, before], TN)
    before = slice(D * (groups - 1), D * groups)
    expand_total[:, before] += dot(low_in[...], hidden_out[:, before], TN)

    @pl.when(step == pl.num_programs(0) - 1)
    def _():
        staged[...] = total[...].astype(bf16)
        expand_staged[...] = expand_total[...].astype(bf16)
        core = table[64]
        height = D // BLOCKS
        copies = spread_copies(table, expand_staged, keep, send, out_sems, height, FF // 2, FF // 2)
        for half, target in ((0, keep), (1, send)):
            column = pl.multiple_of((core if half == 0 else 1 - core) * (D // 2), LANES)
            for block in range(BLOCKS):
                owner = table[32 + 16 * half + block]
                for group in range(groups):
                    row = pl.multiple_of((owner * groups + group) * height, 16)
                    copies.append(
                        pltpu.make_async_copy(
                            staged.at[pl.ds(row, height), pl.ds(column, D // 2)],
                            target.at[pl.ds(block * height, height), pl.ds(D // 2 * group, D // 2)],
                            out_sems.at[32 + (16 * half + block) * groups + group],
                        )
                    )
        start_all(copies)
        wait_all(copies)


def reduce(table, active, slope, unit, low, cotangent, mask, vec, pieces, size, after=()):
    height = active.shape[0]
    return pl.pallas_call(
        reduce_kernel,
        name="reduce",
        grid=(height // size,),
        in_specs=[
            SMEM,
            rows(size, FF),
            rows(size, FF),
            rows(size, D),
            rows(size, D),
            rows(size, D),
            rows(size, LANES),
            whole((16, D)),
        ]
        + [ANY] * (4 + len(after)),
        out_specs=[rows(size, D), rows(size, D), rows(size, FF), whole((24, D)), whole((8, FF)), ANY, ANY],
        out_shape=[
            shaped((height, D), bf16),
            shaped((height, D), f32),
            shaped((height, FF), bf16),
            shaped((24, D), f32),
            shaped((8, FF), f32),
            shaped((D, FF), bf16),
            shaped((D, FF), bf16),
        ],
        scratch_shapes=[
            pltpu.VMEM((FF, D), bf16),
            pltpu.VMEM((FF, D), f32),
            pltpu.VMEM((D, FF), f32),
            pltpu.VMEM((D, FF), bf16),
            pltpu.SemaphoreType.DMA((32,)),
            pltpu.SemaphoreType.DMA((160,)),
        ],
        compiler_params=params(),
        cost_estimate=pl.CostEstimate(
            flops=10 * height * 8 * D * FF, bytes_accessed=height * 30_000, transcendentals=0
        ),
    )(table, active, slope, unit, low, cotangent, mask, vec, *pieces, *after)


def inner_kernel(hidden, outer, unit_in, rate_in, context, mask, vec, out_weight, weight, *refs):
    inner_out, context_out, sums, grad_out, total = refs[-5:]
    step = pl.program_id(0)

    @pl.when(step == 0)
    def _():
        sums[...] = jnp.zeros_like(sums)
        total[...] = jnp.zeros_like(total)

    height = hidden.shape[0]
    parts = 2
    share = height // parts
    spans = [slice(share * part, share * (part + 1)) for part in range(parts)]
    raw = {0: dot(hidden[spans[0], :], weight[...], NT)}
    for part in range(parts):
        span = spans[part]
        if part + 1 < parts:
            raw[part + 1] = dot(hidden[spans[part + 1], :], weight[...], NT)
        grad_normed = outer[span, :] + raw[part]
        unit = unit_in[span, :]
        sums[0:8, :] += fold(grad_normed * unit)
        sums[8:16, :] += fold(grad_normed)
        inner = norm_back(grad_normed * vec[4:5, :], unit, six(rate_in[span, :]))
        inner_out[span, :] = inner
        branch = inner.astype(bf16)
        sums[16:24, :] += fold(branch.astype(f32))
        sums[24:32, :] += fold(jnp.where(six(mask[span, :]) > 0, inner, 0.0))
        context_out[span, :] = dot(branch, out_weight[...], NT).astype(bf16)
        total[...] += dot(context[span, :], branch, TN)

    @pl.when(step == pl.num_programs(0) - 1)
    def _():
        grad_out[...] = total[...].astype(bf16)


def inner_pass(hidden, outer, unit, rate, context, mask, vec, weights, size, after=()):
    height = hidden.shape[0]
    return pl.pallas_call(
        inner_kernel,
        name="inner",
        grid=(height // size,),
        in_specs=[
            rows(size, FF),
            rows(size, D),
            rows(size, D),
            rows(size, LANES),
            rows(size, D),
            rows(size, LANES),
            whole((16, D)),
            whole((D, D)),
            whole((D, FF)),
        ]
        + [ANY] * len(after),
        out_specs=[rows(size, D), rows(size, D), whole((32, D)), whole((D, D))],
        out_shape=[
            shaped((height, D), f32),
            shaped((height, D), bf16),
            shaped((32, D), f32),
            shaped((D, D), bf16),
        ],
        scratch_shapes=[pltpu.VMEM((D, D), f32)],
        compiler_params=params(),
        cost_estimate=pl.CostEstimate(
            flops=10 * height * 2 * D * (2 * D + FF), bytes_accessed=height * 20_000, transcendentals=0
        ),
    )(hidden, outer, unit, rate, context, mask, vec, *weights, *after)


def attend_back_kernel(qkv, raised_in, inverse_in, turned, grad_context, *refs):
    mixed_out, turned_grad = refs[-2:]
    first = lane_first(L)
    blank = jnp.zeros((HEAD_DIM, L), bf16)
    pairs = {}
    padded = {}
    levels = {}
    probs_grads = {}
    score_grads = {}
    value_terms = {}
    key_terms = {}

    def open_head(head):
        pair, part = divmod(head, 2)
        low = LANES * pair
        if part == 0:
            pairs[pair] = (grad_context[:, low : low + LANES].T.astype(f32), qkv[:, D + low : D + low + LANES].T)
        grads = pairs[pair][0]
        grad = grads[HEAD_DIM * part : HEAD_DIM * (part + 1)] * inverse_in[head : head + 1, :]
        context = turned[HEAD_DIM * head : HEAD_DIM * (head + 1), :].astype(f32)
        levels[head] = jnp.sum(grad * context, axis=0, keepdims=True)
        grad_low = grad.astype(bf16)
        padded[head] = jnp.concatenate([grad_low, blank] if part == 0 else [blank, grad_low], axis=0)
        probs_grads[head] = dot(qkv[:, 2 * D + low : 2 * D + low + LANES], padded[head], NN)

    def scale_head(head):
        score_grads[head] = (raised_in[head].astype(f32) * (probs_grads.pop(head) - levels[head])).astype(bf16)

    def close_head(head):
        pair, part = divmod(head, 2)
        low = LANES * pair
        value_terms[head] = dot(raised_in[head], padded.pop(head), NT)
        queries = qkv[:, low : low + LANES]
        lanes = first if part == 0 else ~first
        grads = score_grads.pop(head)
        key_terms[head] = dot(grads, jnp.where(lanes, queries, jnp.zeros_like(queries)), NN)
        keys = pairs[pair][1][HEAD_DIM * part : HEAD_DIM * (part + 1)]
        turned_grad[HEAD_DIM * head : HEAD_DIM * (head + 1), :] = dot(keys, grads, NN) * HEAD_DIM**-0.5
        if part:
            span = slice(low, low + LANES)
            mixed_out[:, span] = turned_grad[span, :].T.astype(bf16)
            mixed_out[:, D + low : D + low + LANES] = (key_terms.pop(head - 1) + key_terms.pop(head)).astype(bf16)
            mixed_out[:, 2 * D + low : 2 * D + low + LANES] = (
                value_terms.pop(head - 1) + value_terms.pop(head)
            ).astype(bf16)

    open_head(0)
    open_head(1)
    scale_head(0)
    for head in range(HEADS):
        if head + 2 < HEADS:
            open_head(head + 2)
        if head + 1 < HEADS:
            scale_head(head + 1)
        close_head(head)


def attend_back(qkv, raised, inverse, turned, grad_context, after=()):
    height = qkv.shape[0]
    count = height // L
    return pl.pallas_call(
        attend_back_kernel,
        name="attend_back",
        grid=(count,),
        in_specs=[
            rows(L, QKV),
            pl.BlockSpec((None, HEADS, L, L), lambda i: (i, 0, 0, 0)),
            pl.BlockSpec((None, 16, L), lambda i: (i, 0, 0)),
            pl.BlockSpec((None, D, L), lambda i: (i, 0, 0)),
            rows(L, D),
        ]
        + [ANY] * len(after),
        out_specs=rows(L, QKV),
        out_shape=shaped((height, QKV), bf16),
        scratch_shapes=[pltpu.VMEM((D, L), f32)],
        compiler_params=params(),
        cost_estimate=pl.CostEstimate(
            flops=10 * count * 32 * L * L * D, bytes_accessed=count * 14_000_000, transcendentals=0
        ),
    )(qkv, raised, inverse, turned, grad_context, *after)


def heads_kernel(table, x, marks, mixed, second_sums, inner_sums, bias_rows, weight, out_grad, *refs):
    keep, send, total, staged, columns, out_sems, more_out_sems, vec_sems = refs[-8:]
    step = pl.program_id(0)

    @pl.when(step == 0)
    def _():
        total[...] = jnp.zeros_like(total)

    turned = jnp.concatenate([x[...].T, marks[...]], axis=0)
    for piece in range(3):
        span = slice(D * piece, D * (piece + 1))
        total[:, span] += dot(turned, mixed[:, span], NN)

    @pl.when(step == pl.num_programs(0) - 1)
    def _():
        staged[...] = total[:D, :].astype(bf16)
        copies = spread_copies(table, out_grad, keep, send, more_out_sems, D // BLOCKS, QKV // 2 + LANES, D // 2)
        copies += spread_copies(table, staged, keep, send, out_sems, D // BLOCKS, 0, QKV // 2)
        start_all(copies)
        whole_sums = total[D : D + 1, :]
        masked_sums = total[D + 1 : D + 2, :]
        high = masked_sums.astype(bf16)
        low = (masked_sums - high.astype(f32)).astype(bf16)
        split = jnp.concatenate([high, low, jnp.zeros((14, QKV), bf16)], axis=0)
        reached = jnp.sum(dot(split, weight[...], NT), axis=0, keepdims=True)

        def line(ref, group):
            return jnp.sum(ref[8 * group : 8 * (group + 1), :], axis=0, keepdims=True)

        lines = [
            reached + line(inner_sums, 3),
            whole_sums[:, :D],
            whole_sums[:, 2 * D :],
            line(inner_sums, 2),
            line(inner_sums, 0),
            line(inner_sums, 1),
            bias_rows[...],
            line(second_sums, 2),
            line(second_sums, 0),
            line(second_sums, 1),
            jnp.zeros((LANES - VECTORS, D), f32),
        ]
        columns[...] = jnp.concatenate(lines, axis=0).T.astype(bf16)
        height = D // BLOCKS
        more = []
        for half, target in ((0, keep), (1, send)):
            for block in range(BLOCKS):
                owner = table[32 + 16 * half + block]
                more.append(
                    pltpu.make_async_copy(
                        columns.at[pl.ds(pl.multiple_of(owner * height, 16), height), :],
                        target.at[pl.ds(block * height, height), pl.ds(QKV // 2, LANES)],
                        vec_sems.at[16 * half + block],
                    )
                )
        start_all(more)
        wait_all(copies + more)


def heads_grad(table, x, marks, mixed, second_sums, inner_sums, bias_rows, weight, out_grad, size, after=()):
    height = x.shape[0]
    wide = QKV // 2 + LANES + D // 2
    return pl.pallas_call(
        heads_kernel,
        name="heads_grad",
        grid=(height // size,),
        in_specs=[
            SMEM,
            rows(size, D),
            pl.BlockSpec((16, size), lambda i: (0, i)),
            rows(size, QKV),
            whole((24, D)),
            whole((32, D)),
            whole((4, D)),
            whole((D, QKV)),
            whole((D, D)),
        ]
        + [ANY] * len(after),
        out_specs=[ANY, ANY],
        out_shape=[shaped((D, wide), bf16), shaped((D, wide), bf16)],
        scratch_shapes=[
            pltpu.VMEM((D + 16, QKV), f32),
            pltpu.VMEM((D, QKV), bf16),
            pltpu.VMEM((D, LANES), bf16),
            pltpu.SemaphoreType.DMA((32,)),
            pltpu.SemaphoreType.DMA((32,)),
            pltpu.SemaphoreType.DMA((32,)),
        ],
        compiler_params=params(),
        cost_estimate=pl.CostEstimate(flops=10 * height * 2 * D * QKV, bytes_accessed=height * 10_000, transcendentals=0),
    )(table, x, marks, mixed, second_sums, inner_sums, bias_rows, weight, out_grad, *after)


def rows_kernel(mixed, inner, mask, weight, *refs):
    grad = inner[...] + dot(mixed[...], weight[...], NT)
    refs[-1][...] = jnp.where(six(mask[...]) > 0, 0.0, grad).astype(bf16)


def rows_grad(mixed, inner, mask, weight, size, after=()):
    height = mixed.shape[0]
    return pl.pallas_call(
        rows_kernel,
        name="rows_grad",
        grid=(height // size,),
        in_specs=[rows(size, QKV), rows(size, D), rows(size, LANES), whole((D, QKV))] + [ANY] * len(after),
        out_specs=rows(size, D),
        out_shape=shaped((height, D), bf16),
        compiler_params=params(),
        cost_estimate=pl.CostEstimate(
            flops=10 * height * 2 * D * QKV, bytes_accessed=height * 10_000, transcendentals=0
        ),
    )(mixed, inner, mask, weight, *after)


def pile_kernel(*refs):
    height = refs[0].shape[0]
    for index, piece in enumerate(refs[:-1]):
        refs[-1][height * index : height * (index + 1), :] = piece[...]


def pile(pieces):
    height, width = pieces[0].shape
    return pl.pallas_call(
        pile_kernel,
        name="pile",
        out_shape=shaped((height * len(pieces), width), bf16),
        compiler_params=pltpu.CompilerParams(vmem_limit_bytes=16 << 20),
        cost_estimate=pl.CostEstimate(flops=0, bytes_accessed=2_000_000, transcendentals=0),
    )(*pieces)


def around_z(hops):
    return [(i, (i + 8 * hops) % 32) for i in range(32)]


def across(turn):
    return [(i, i ^ (2 if (i & 1) == turn else 4)) for i in range(32)]


def between_cores():
    return [(i, i ^ 1) for i in range(32)]


def make_table():
    table = np.zeros((32, 65), np.int32)
    for device in range(32):
        core, x, y, z = device & 1, (device >> 1) & 1, (device >> 2) & 1, device >> 3
        table[device, 64] = core
        for half in range(2):
            turn = core ^ half
            for block in range(16):
                hops, near, far = block & 3, (block >> 2) & 1, block >> 3
                there_x, there_y = (x ^ near, y ^ far) if turn == 0 else (x ^ far, y ^ near)
                table[device, 16 * half + block] = ((z - hops) % 4) * 4 + there_y * 2 + there_x
                near, far = far, near
                there_x, there_y = (x ^ near, y ^ far) if turn == 0 else (x ^ far, y ^ near)
                table[device, 32 + 16 * half + block] = ((z + hops) % 4) * 4 + there_y * 2 + there_x
    return table


def hop_parts(block):
    return [block] + [lax.ppermute(block, ALL, around_z(hops)) for hops in (1, 2, 3)]


def hop_across(held, turn):
    return lax.ppermute(held, ALL, across(turn))


def hop_core(held):
    return lax.ppermute(held, ALL, between_cores())


def follow(value, earlier):
    return lax.optimization_barrier((value, earlier))[0]


def add_low(*terms):
    total = terms[0].astype(f32)
    for term in terms[1:]:
        total = total + term.astype(f32)
    return total


def add_halves(keep, arrived):
    half = keep.shape[0] // 2
    sent = add_low(keep[half:], arrived[half:]).astype(bf16)
    return add_low(keep[:half], arrived[:half]).astype(bf16), sent


def add_quarters(keep, arrived):
    quarter = keep.shape[0] // 4
    pieces = []
    for hops in range(4):
        span = slice(quarter * hops, quarter * (hops + 1))
        piece = add_low(keep[span], arrived[span])
        pieces.append(piece.astype(bf16) if hops else piece)
    return pieces


def hop_quarters(pieces):
    return [lax.ppermute(pieces[hops], ALL, around_z(hops)) for hops in (1, 2, 3)]


def gather_plain(mine, other):
    pieces = []
    for block in (mine, other):
        full = lax.all_gather(block, "fsdp", axis=0, tiled=True)
        half = full.shape[0] // 2
        pieces += [full[:half], full[half:]]
    return pieces


def scatter_plain(keep, send):
    both = add_low(keep, lax.ppermute(send, "rep", [(0, 1), (1, 0)]))
    return lax.psum_scatter(both, "fsdp", scatter_dimension=0, tiled=True)


def join(core, mine):
    other = lax.ppermute(mine, "rep", [(0, 1), (1, 0)])
    low = jnp.where(core == 0, mine, other)
    high = jnp.where(core == 0, other, mine)
    return jnp.concatenate([low, high], axis=1)


def half_of(weight, place):
    width = weight.shape[1] // 2
    return lax.dynamic_slice_in_dim(weight, place * width, width, axis=1)


def local(
    chips,
    tokens,
    masked,
    cotangent,
    mask_vector,
    heads_weight,
    query_bias,
    value_bias,
    output_weight,
    output_bias,
    first_gain,
    first_shift,
    expand_weight,
    expand_bias,
    reduce_weight,
    reduce_bias,
    second_gain,
    second_shift,
):
    core = lax.axis_index("rep")
    layout = tokens.shape
    height = layout[0] * layout[1] * layout[2]
    share = mask_vector.shape[0]
    by_hops = chips == BLOCKS
    if by_hops:
        table = lax.dynamic_index_in_dim(
            jnp.asarray(make_table()), lax.axis_index("fsdp") * 2 + core, axis=0, keepdims=False
        )
    else:
        table = jnp.concatenate([jnp.tile(jnp.arange(BLOCKS, dtype=jnp.int32), 4), core[None].astype(jnp.int32)])

    vector_rows = jnp.concatenate(
        [
            mask_vector[None],
            query_bias[None],
            value_bias[None],
            output_bias[None],
            first_gain[None],
            first_shift[None],
            *[expand_bias[None, share * group : share * (group + 1)] for group in range(4)],
            reduce_bias[None],
            second_gain[None],
            second_shift[None],
        ],
        axis=0,
    )
    vector_columns = jnp.pad(vector_rows.T, ((0, 0), (0, LANES - VECTORS)))

    def payloads(place):
        return (
            jnp.concatenate([half_of(heads_weight, place), vector_columns], axis=1),
            jnp.concatenate([half_of(output_weight, place), half_of(expand_weight, place)], axis=1),
            half_of(reduce_weight, place),
        )

    flat_tokens = tokens.reshape(height, D)
    flat_cotangent = cotangent.reshape(height, D)
    flags = masked.reshape(height).astype(bf16)
    mask = jnp.broadcast_to(flags[:, None], (height, LANES))
    marks = jnp.concatenate([jnp.ones((1, height), bf16), flags[None], jnp.zeros((14, height), bf16)], axis=0)
    size = 512
    sequences = height // L
    half = sequences // 2

    if by_hops:
        first_load, middle_load, last_load = payloads(core)
        held = pile(hop_parts(first_load))
        middle_parts = hop_parts(follow(middle_load, held))
        near = pile([held, follow(hop_across(held, 0), middle_parts[1])])
        far = hop_across(near, 1)
        middle_held = pile(middle_parts)
        heads = (near, far, hop_core(near), hop_core(follow(far, middle_parts)))
        middle_near = pile([middle_held, hop_across(middle_held, 0)])
        done = attend(table, flat_tokens, mask, heads, None, 0, half, after=(middle_near,))
        vec = done[6]
        last_held = pile(follow(hop_parts(follow(last_load, middle_held)), vec))
        middle_far = hop_across(middle_near, 1)
        middle_near_other = hop_core(middle_near)
        middle_far_other = hop_core(follow(middle_far, vec))
        done = attend(
            table, flat_tokens, mask, heads, done, half, sequences - half, after=(middle_far, middle_near_other, last_held)
        )
        last_near = pile([last_held, hop_across(last_held, 0)])
        middle = (middle_near, middle_far, middle_near_other, middle_far_other)
        after = (last_near,)
    else:
        heads, middle, last = [gather_plain(a, b) for a, b in zip(payloads(core), payloads(1 - core))]
        done = attend(table, flat_tokens, mask, heads, None, 0, sequences)
        vec = done[6]
        after = ()
    x, qkv, raised, inverse, context, turned, _, heads_whole = done
    bias = vec[6:10].reshape(4, D // share, share).transpose(1, 0, 2).reshape(1, FF)
    unit, rate, low, active, slope, *middle_whole = expand(table, context, x, vec, bias, middle, size, after=after)
    if by_hops:
        last_far = hop_across(last_near, 1)
        last = (last_near, last_far, hop_core(last_near), hop_core(follow(last_far, unit)))

    outputs, outer, hidden, second_sums, bias_sums, keep, send = reduce(
        table, active, slope, unit, low, flat_cotangent, mask, vec, last, size
    )
    bias_rows = jnp.sum(bias_sums, axis=0).reshape(D // share, 4, share).transpose(1, 0, 2).reshape(4, D)

    def inner_call(after=()):
        return inner_pass(hidden, outer, unit, rate, context, mask, vec, middle_whole, size, after=after)

    def back_call(after=()):
        return attend_back(qkv, raised, inverse, turned, grad_context, after=after)

    def heads_call(after=()):
        return heads_grad(
            table, x, marks, mixed, second_sums, inner_sums, bias_rows, heads_whole, out_grad, size, after=after
        )

    def rows_call(after=()):
        return rows_grad(mixed, inner, mask, heads_whole, size, after=after)

    if by_hops:
        arrived = hop_core(send)
        inner, grad_context, inner_sums, out_grad = inner_call()
        rest_keep, sent = add_halves(keep, arrived)
        arrived = hop_across(sent, 0)
        mixed = back_call(after=(rest_keep, sent))
        rest_keep, sent = add_halves(rest_keep, arrived)
        arrived = hop_across(sent, 1)
        keep, send = heads_call(after=(rest_keep, sent))
        send = follow(send, arrived)
        rest_pieces = add_quarters(rest_keep, arrived)
        arrived = hop_core(send)
        keep, sent = add_halves(keep, arrived)
        arrived = hop_across(sent, 0)
        grad_tokens = rows_call(after=(sent, *rest_pieces))
        rest_moved = follow(hop_quarters(rest_pieces), grad_tokens)
        keep, sent = add_halves(follow(keep, grad_tokens), arrived)
        arrived = hop_across(sent, 1)
        rest_share = add_low(rest_pieces[0], *rest_moved)
        pieces = add_quarters(keep, arrived)
        heads_share = add_low(pieces[0], *hop_quarters(pieces))
    else:
        rest_share = scatter_plain(keep, send)
        inner, grad_context, inner_sums, out_grad = inner_call()
        mixed = back_call()
        heads_share = scatter_plain(*heads_call())
        grad_tokens = rows_call()

    last_share = jnp.concatenate([rest_share[:, D // 2 * group : D // 2 * (group + 1)] for group in range(4)], axis=0)
    vector_grads = heads_share[:, QKV // 2 : QKV // 2 + LANES]

    def vector(index):
        return vector_grads[:, index]

    return (
        outputs.reshape(layout),
        grad_tokens.reshape(layout),
        vector(0),
        join(core, heads_share[:, : QKV // 2]),
        vector(1),
        vector(2),
        join(core, heads_share[:, QKV // 2 + LANES :]),
        vector(3),
        vector(4),
        vector(5),
        join(core, rest_share[:, FF // 2 :]),
        vector_grads[:, 6:10].T.reshape(-1),
        join(core, last_share),
        vector(10),
        vector(11),
        vector(12),
    )


def solution(mesh):
    in_specs = (
        P(None, ("fsdp", "rep"), None, None),
        P(None, ("fsdp", "rep"), None),
        P(None, ("fsdp", "rep"), None, None),
        P("fsdp"),
        P("fsdp", None),
        P("fsdp"),
        P("fsdp"),
        P("fsdp", None),
        P("fsdp"),
        P("fsdp"),
        P("fsdp"),
        P("fsdp", None),
        P("fsdp"),
        P("fsdp", None),
        P("fsdp"),
        P("fsdp"),
        P("fsdp"),
    )
    out_specs = (
        P(None, ("fsdp", "rep"), None, None),
        P(None, ("fsdp", "rep"), None, None),
        P("fsdp"),
        P("fsdp", None),
        P("fsdp"),
        P("fsdp"),
        P("fsdp", None),
        P("fsdp"),
        P("fsdp"),
        P("fsdp"),
        P("fsdp", None),
        P("fsdp"),
        P("fsdp", None),
        P("fsdp"),
        P("fsdp"),
        P("fsdp"),
    )
    return jax.shard_map(
        functools.partial(local, mesh.shape["fsdp"]),
        mesh=mesh,
        in_specs=in_specs,
        out_specs=out_specs,
        check_vma=False,
    )
```

time: 455 us -> 358 us (0.79); the launches traced: 447 us -> 360 us
  waiting for transfers between devices: 105 us -> 45.2 us
  Pallas kernels: 245 us -> 231 us
  local copies, waits for them, and re-layouts: 25.7 us -> 14.2 us
    ppermute x36 -> x33, waiting for transfers between devices: 105 us -> 45.2 us  [the longest x9 19.6 us: hop_parts(): lax.ppermute(block, ALL, around_z(hops))]
    pallas_call x1, Pallas kernels: 40.8 us -> 24.5 us  [inner_pass(): pl.pallas_call(inner_kernel, name='inner', grid=(height // size,), in_spe...]
    pallas_call x1, Pallas kernels: 53.7 us -> 61.9 us  [reduce(): pl.pallas_call(reduce_kernel, name='reduce', grid=(height // size,), in_s...]
    pallas_call x2 -> x1, Pallas kernels: 37.8 us -> 29.7 us  [attend_back(): pl.pallas_call(attend_back_kernel, name='attend_back', grid=(count,), in_...]
    pallas_call x2, Pallas kernels: 44.2 us -> 52 us  [attend(): pl.pallas_call(attend_kernel, name='attend', grid=(count,), in_specs=[SME...]
    concatenate x6 -> x0, local copies, waits for them, and re-layouts: 5.82 us -> none  [the longest x3 3.65 us: gather_blocks(): held = jnp.concatenate([held, lax.ppermute(held, ALL, across(1))], axis=0)]
    pallas_call x2 -> x7, Pallas kernels: 38.2 us -> 32.5 us  [the longest x1 32.1 us: expand(): pl.pallas_call(expand_kernel, name='expand', grid=(height // size,), in_s...]
    unnamed x30 -> x43, local copies, waits for them, and re-layouts: 8.51 us -> 3.48 us
  transfers between devices with their start and end apart: 40 -> 37, of which waited for: 20 -> 12; matrix products, arithmetic and copies ran while one was open for 9% -> 5% of each run, Pallas kernels for 22% -> 47%
where the time goes in v2:
time: 358 us; the launch traced here: 360 us
  Pallas kernels  231 us (65%)
  starting transfers between devices  47.7 us (13%)
  waiting for transfers between devices  45.2 us (13%)
  other arithmetic  21.4 us (6%)
  local copies, waits for them, and re-layouts  14.2 us (4%)
    pallas_call x1, Pallas kernels, reduce(): pl.pallas_call(reduce_kernel, name='reduce', grid=(height // size,), in_s...  61.9 us
    pallas_call x2, Pallas kernels, attend(): pl.pallas_call(attend_kernel, name='attend', grid=(count,), in_specs=[SME...  52 us
    pallas_call x1, Pallas kernels, expand(): pl.pallas_call(expand_kernel, name='expand', grid=(height // size,), in_s...  32.1 us
    pallas_call x1, Pallas kernels, attend_back(): pl.pallas_call(attend_back_kernel, name='attend_back', grid=(count,), in_...  29.7 us
    pallas_call x1, Pallas kernels, inner_pass(): pl.pallas_call(inner_kernel, name='inner', grid=(height // size,), in_spe...  24.5 us
    ppermute x9, starting transfers between devices, hop_parts(): lax.ppermute(block, ALL, around_z(hops))  21 us
    ppermute x9, waiting for transfers between devices, hop_parts(): lax.ppermute(block, ALL, around_z(hops))  19.6 us
    pallas_call x1, Pallas kernels, heads_grad(): pl.pallas_call(heads_kernel, name='heads_grad', grid=(height // size,), i...  16.7 us
  transfers between devices with their start and end apart: 37, of which 12 were waited for; matrix products, arithmetic and copies ran while one was open for 5% of the time, Pallas kernels for 47%

profile of v2, /device:TPU:0, one launch (start us, length us, event | category | flops | bytes accessed | tf_op | source)
XLA Modules:
  0.0 360.4 jit_solution(4559786581170805226)
XLA Ops:
  0.7 0.9 slice_bitcast_fusion.1
  1.5 1.5 concatenate.27
  3.1 0.9 constant_dynamic-slice_fusion.3
  4.1 3.1 collective-permute-start
  7.1 2.6 collective-permute-start.1
  9.7 1.3 collective-permute-start.2
  11.1 2.3 collective-permute-done.refs_1_
  13.4 4.4 %collective-permute-done.1.refs_2_ = bf16[48,1280]{1,0:T(8,128)(2,1)S(1)} collective-permute-done((bf16[48,1280]{1,0:T(8,128)(2,1)S(1)}, bf16[48,1280]{1,0:T(8,128)(2,1)S(1)}, u32[]{:S(2)}, u32[]{:S(2)}) %collective-permute-start.1) | collective-permute-done | bytes 122912 | tf_op jit(solution)/shard_map/ppermute | solution.py:752
  17.9 1.6 collective-permute-start.3
  19.4 0.8 constant_dynamic-slice_fusion.2
  20.2 3.2 collective-permute-start.4
  23.4 4.9 %collective-permute-done.4.refs_1_ = bf16[48,1920]{1,0:T(8,128)(2,1)S(1)} collective-permute-done((bf16[48,1920]{1,0:T(8,128)(2,1)S(1)}, bf16[48,1920]{1,0:T(8,128)(2,1)S(1)}, u32[]{:S(2)}, u32[]{:S(2)}) %collective-permute-start.4) | collective-permute-done | bytes 184352 | tf_op jit(solution)/shard_map/ppermute | solution.py:752
  28.4 1.3 collective-permute-start.5
  29.6 0.9 collective-permute-start.7
  30.5 3.4 collective-permute-start.8
  33.9 8.0 %collective-permute-done.7.refs_2_ = bf16[48,1920]{1,0:T(8,128)(2,1)S(1)} collective-permute-done((bf16[48,1920]{1,0:T(8,128)(2,1)S(1)}, bf16[48,1920]{1,0:T(8,128)(2,1)S(1)}, u32[]{:S(2)}, u32[]{:S(2)}) %collective-permute-start.7) | collective-permute-done | bytes 184352 | tf_op jit(solution)/shard_map/ppermute | solution.py:752
  41.9 0.7 collective-permute-done.5.refs_1_
  42.7 1.6 collective-permute-start.10
  44.3 1.2 fusion.2.table
  45.5 1.6 collective-permute-start.13
  47.1 1.6 collective-permute-start.14
  48.8 5.5 %collective-permute-done.10.refs_1_ = bf16[192,1920]{1,0:T(8,128)(2,1)S(1)} collective-permute-done((bf16[192,1920]{1,0:T(8,128)(2,1)S(1)}, bf16[192,1920]{1,0:T(8,128)(2,1)S(1)}, u32[]{:S(2)}, u32[]{:S(2)}) %collective-permute-start.10) | collective-permute-done | bytes 737312 | tf_op jit(solution)/shard_map/ppermute | solution.py:756
  54.2 0.9 copy-done.7
  55.1 3.3 collective-permute-start.15
  58.5 1.1 copy-done.8
  59.7 1.2 collective-permute-start.11
  60.9 1.1 broadcast_in_dim.52.mask
  62.1 19.7 %attend.2 = (bf16[2048,768]{1,0:T(8,128)(2,1)}, bf16[2048,2304]{1,0:T(8,128)(2,1)}, bf16[4,12,512,512]{3,2,1,0:T(8,128)(2,1)}, f32[4,16,512]{2,1,0:T(8,128)}, bf...) custom-call(s32[65]{0:T(128)} %fusion.2.table, ...), custom_call_target="tpu_custom_call" | custom-call | flops 100663296000 | bytes 28000000 | tf_op jit(solution)/shard_map/attend/pallas_call | solution.py:209
  81.9 1.2 collective-permute-start.17
  83.2 32.3 %attend.3 = (bf16[2048,768]{1,0:T(8,128)(2,1)}, bf16[2048,2304]{1,0:T(8,128)(2,1)}, bf16[4,12,512,512]{3,2,1,0:T(8,128)(2,1)}, f32[4,16,512]{2,1,0:T(8,128)}, bf...) custom-call(s32[65]{0:T(128)} %fusion.2.table, ...), custom_call_target="tpu_custom_call", output_to_operand_aliasing={{0}: (7, {}), {1}: (8, {}), {2}: (9, {}), {3}: (10, {}), {4... | custom-call | flops 100663296000 | bytes 28000000 | tf_op jit(solution)/shard_map/attend/pallas_call | solution.py:209
  115.4 0.8 slice.177
  116.3 0.7 reshape.79.bias
  117.0 1.1 copy-done.3
  118.2 1.1 collective-permute-start.18
  119.4 32.1 %expand.1 = (f32[2048,768]{1,0:T(8,128)}, f32[2048,128]{1,0:T(8,128)}, bf16[2048,768]{1,0:T(8,128)(2,1)}, bf16[2048,3072]{1,0:T(8,128)(2,1)}, bf16[2048,3072]{1,...) custom-call(s32[65]{0:T(128)} %fusion.2.table, bf16[2048,768]{1,0:T(8,128)(2,1)} %get-tuple-element.80.context, ...), custom_call_target="tpu_custom_call" | custom-call | flops 120795955200 | bytes 40960000 | tf_op jit(solution)/shard_map/expand/pallas_call | solution.py:293
  152.2 0.7 maximum_maximum_fusion.marks
  152.9 1.8 collective-permute-done.20.refs_3_
  154.7 61.9 %reduce.19 = (bf16[2048,768]{1,0:T(8,128)(2,1)}, f32[2048,768]{1,0:T(8,128)}, bf16[2048,3072]{1,0:T(8,128)(2,1)}, f32[24,768]{1,0:T(8,128)}, f32[8,3072]{1,0:T(8...) custom-call(s32[65]{0:T(128)} %fusion.2.table, bf16[2048,3072]{1,0:T(8,128)(2,1)} %get-tuple-element.83.active, ...), custom_call_target="tpu_custom_call" | custom-call | flops 386547056640 | bytes 61440000 | tf_op jit(solution)/shard_map/reduce/pallas_call | solution.py:401
  217.0 24.5 %inner.1 = (f32[2048,768]{1,0:T(8,128)}, bf16[2048,768]{1,0:T(8,128)(2,1)}, f32[32,768]{1,0:T(8,128)}, bf16[768,768]{1,0:T(8,128)(2,1)}) custom-call(bf16[2048,3072]{1,0:T(8,128)(2,1)} %get-tuple-element.93.hidden, f32[2048,768]{1,0:T(8,128)} %get-tuple-element.94.outer, f32[2048,768]{1,0:T(8,128)} %get-tuple-element.85.unit_in, ...), custom_call_target="tpu_custom_call" | custom-call | flops 144955146240 | bytes 40960000 | tf_op jit(solution)/shard_map/inner/pallas_call | solution.py:478
  241.6 0.7 reshape.83.bias_rows
  242.3 6.2 %add_convert_fusion = (bf16[384,3072]{1,0:T(8,128)(2,1)}, bf16[384,3072]{1,0:T(8,128)(2,1)}) fusion(bf16[768,3072]{1,0:T(8,128)(2,1)} %collective-permute-done.21, bf16[768,3072]{1,0:T(8,128)(2,1)} %get-tuple-element.99), kind=kLoop, calls=%fused_computation | loop fusion | flops 9437184 | bytes 14155776 | tf_op jit(solution)/shard_map/convert_element_type | solution.py:776
  248.6 1.1 collective-permute-start.22
  249.7 29.7 %attend_back.1.mixed = bf16[2048,2304]{1,0:T(8,128)(2,1)} custom-call(bf16[2048,2304]{1,0:T(8,128)(2,1)} %get-tuple-element.89.qkv, bf16[4,12,512,512]{3,2,1,0:T(8,128)(2,1)} %get-tuple-element.90.raised_in, f32[4,16,512]{2,1,0:T(8,128)} %get-tuple-element.91.inverse_in, bf16[4,768,512]{2,1,0:T(8,128)(2,1)} %get-tuple-element.92.turned, ...), custom_call_target="tpu_custom_call" | custom-call | flops 257698037760 | bytes 56000000 | tf_op jit(solution)/shard_map/attend_back/pallas_call | solution.py:569
  279.5 3.5 add_convert_fusion.4
  283.0 0.7 collective-permute-start.23
  284.0 16.7 %heads_grad.1 = (bf16[768,1664]{1,0:T(8,128)(2,1)}, bf16[768,1664]{1,0:T(8,128)(2,1)}) custom-call(s32[65]{0:T(128)} %fusion.2.table, bf16[2048,768]{1,0:T(8,128)(2,1)} %get-tuple-element.81.x, bf16[16,2048]{1,0:T(8,128)(2,1)} %maximum_maximum_fusion.marks, bf16[2048,2304]{1,0:T(8,128)(2,1)} %attend_back.1.mixed, f32[24,768]{1,0:T(8,128)} %get-tuple-element.103.second_sums, ...), custom_call_target="tpu_custom_call" | custom-call | flops 72477573120 | bytes 20480000 | tf_op jit(solution)/shard_map/heads_grad/pallas_call | solution.py:653
  300.9 1.2 add_convert_fusion.8
  302.6 3.3 collective-permute-start.34
  306.0 3.4 add_convert_fusion.2
  309.4 0.9 collective-permute-start.25
  310.3 13.3 %rows_grad.1 = bf16[2048,768]{1,0:T(8,128)(2,1)} custom-call(bf16[2048,2304]{1,0:T(8,128)(2,1)} %attend_back.1.mixed, f32[2048,768]{1,0:T(8,128)} %get-tuple-element.101.inner, bf16[2048,128]{1,0:T(8,128)(2,1)} %broadcast_in_dim.52.mask, bf16[768,2304]{1,0:T(8,128)(2,1)} %get-tuple-element.102.weight, bf16[384,1664]{1,0:T(8,128)(2,1)} %get-tuple-element.126.refs_0_, ...), custom_call_target="tpu_custom_call" | custom-call | flops 72477573120 | bytes 20480000 | tf_op jit(solution)/shard_map/rows_grad/pallas_call | solution.py:691
  323.5 2.1 collective-permute-done.33
  325.6 1.1 convert_add_fusion
  327.5 1.6 add_convert_fusion.7
  329.0 1.1 collective-permute-start.26
  330.2 0.9 pad_maximum_fusion
  331.0 8.5 %collective-permute-done.26 = bf16[192,1664]{1,0:T(8,128)(2,1)S(1)} collective-permute-done((bf16[192,1664]{1,0:T(8,128)(2,1)S(1)}, bf16[192,1664]{1,0:T(8,128)(2,1)S(1)}, u32[]{:S(2)}, u32[]{:S(2)}) %collective-permute-start.26) | collective-permute-done | bytes 639008 | tf_op jit(solution)/shard_map/ppermute | solution.py:756
  339.6 6.5 %collective-permute-start.27 = (bf16[48,1664]{1,0:T(8,128)(2,1)S(1)}, bf16[48,1664]{1,0:T(8,128)(2,1)S(1)}, u32[]{:S(2)}, u32[]{:S(2)}) collective-permute-start(bf16[48,1664]{1,0:T(8,128)(2,1)S(1)} %get-tuple-element.135), channel_id=1, source_target_pairs={{0,8},{1,9},{2,10},{3,11},{4,12},{5,13},{6,14},{7,15},{8,16},{9,17... | collective-permute-start | bytes 479240 | tf_op jit(solution)/shard_map/ppermute | solution.py:791
  346.5 2.1 collective-permute-start.29
  348.6 0.9 pad_maximum_fusion.1
  349.5 1.2 collective-permute-done.27
  350.7 5.7 %collective-permute-done.28 = bf16[48,1664]{1,0:T(8,128)(2,1)S(1)} collective-permute-done((bf16[48,1664]{1,0:T(8,128)(2,1)S(1)}, bf16[48,1664]{1,0:T(8,128)(2,1)S(1)}, u32[]{:S(2)}, u32[]{:S(2)}) %collective-permute-start.28) | collective-permute-done | bytes 159776 | tf_op jit(solution)/shard_map/ppermute | solution.py:791
  357.8 0.9 slice_reduce_fusion
  359.5 0.8 pad_maximum_fusion.2
  (118 shorter events, 6.5 us)
Async XLA Ops:
  0.6 10.4 %copy-start = (bf16[48,3072]{1,0:T(8,128)(2,1)S(1)}, bf16[48,3072]{1,0:T(8,128)(2,1)}, u32[]{:S(2)}) copy-start(bf16[48,3072]{1,0:T(8,128)(2,1)} %param.29) | copy-start | bytes 884740
  4.1 9.3 %collective-permute-start = (bf16[48,1280]{1,0:T(8,128)(2,1)S(1)}, bf16[48,1280]{1,0:T(8,128)(2,1)S(1)}, u32[]{:S(2)}, u32[]{:S(2)}) collective-permute-start(bf16[48,1280]{1,0:T(8,128)(2,1)S(1)} %fusion.1.refs_0_), channel_id=1, source_target_pairs={{0,8},{1,9},{2,10},{3,11},{4,12},{5,13},{6,14},{7,15},{8,16},{9,17... | collective-permute-start | bytes 368648 | tf_op jit(solution)/shard_map/ppermute | solution.py:752
  7.1 10.7 %collective-permute-start.1 = (bf16[48,1280]{1,0:T(8,128)(2,1)S(1)}, bf16[48,1280]{1,0:T(8,128)(2,1)S(1)}, u32[]{:S(2)}, u32[]{:S(2)}) collective-permute-start(bf16[48,1280]{1,0:T(8,128)(2,1)S(1)} %fusion.1.refs_0_), channel_id=1, source_target_pairs={{0,16},{1,17},{2,18},{3,19},{4,20},{5,21},{6,22},{7,23},{8,24},{9,... | collective-permute-start | bytes 368648 | tf_op jit(solution)/shard_map/ppermute | solution.py:752
  9.7 8.1 %collective-permute-start.2 = (bf16[48,1280]{1,0:T(8,128)(2,1)S(1)}, bf16[48,1280]{1,0:T(8,128)(2,1)S(1)}, u32[]{:S(2)}, u32[]{:S(2)}) collective-permute-start(bf16[48,1280]{1,0:T(8,128)(2,1)S(1)} %fusion.1.refs_0_), channel_id=1, source_target_pairs={{0,24},{1,25},{2,26},{3,27},{4,28},{5,29},{6,30},{7,31},{8,0},{9,1... | collective-permute-start | bytes 368648 | tf_op jit(solution)/shard_map/ppermute | solution.py:752
  11.1 33.2 %copy-start.17 = (s32[2,2,512]{2,1,0:T(2,128)S(1)}, s32[2,2,512]{2,1,0:T(2,128)}, u32[]{:S(2)}) copy-start(s32[2,2,512]{2,1,0:T(2,128)} %param.19) | copy-start | bytes 24580
  11.1 34.4 %copy-start.16 = (bf16[192,768]{1,0:T(8,128)(2,1)S(1)}, bf16[192,768]{1,0:T(8,128)(2,1)}, u32[]{:S(2)}) copy-start(bf16[192,768]{1,0:T(8,128)(2,1)} %param.31) | copy-start | bytes 884740
  17.9 10.4 %collective-permute-start.3 = (bf16[192,1280]{1,0:T(8,128)(2,1)S(1)}, bf16[192,1280]{1,0:T(8,128)(2,1)S(1)}, u32[]{:S(2)}, u32[]{:S(2)}) collective-permute-start(bf16[192,1280]{1,0:T(8,128)(2,1)S(1)} %pile.6.refs_0_), channel_id=1, source_target_pairs={{0,2},{1,5},{2,0},{3,7},{4,6},{5,1},{6,4},{7,3},{8,10},{9,13},{10,... | collective-permute-start | bytes 1474568 | tf_op jit(solution)/shard_map/ppermute | solution.py:756
  20.2 8.1 %collective-permute-start.4 = (bf16[48,1920]{1,0:T(8,128)(2,1)S(1)}, bf16[48,1920]{1,0:T(8,128)(2,1)S(1)}, u32[]{:S(2)}, u32[]{:S(2)}) collective-permute-start(bf16[48,1920]{1,0:T(8,128)(2,1)S(1)} %pad_maximum_fusion.4.refs_0_), channel_id=1, source_target_pairs={{0,8},{1,9},{2,10},{3,11},{4,12},{5,13},{6,14},{7,15},{8,16},{9,17... | collective-permute-start | bytes 552968 | tf_op jit(solution)/shard_map/ppermute | solution.py:752
  28.4 31.3 %copy-start.6 = (bf16[384,1280]{1,0:T(8,128)(2,1)}, bf16[384,1280]{1,0:T(8,128)(2,1)S(1)}, u32[]{:S(2)}) copy-start(bf16[384,1280]{1,0:T(8,128)(2,1)S(1)} %pile.7.refs_0_) | copy-start | bytes 2949124
  28.4 14.3 %collective-permute-start.5 = (bf16[384,1280]{1,0:T(8,128)(2,1)S(1)}, bf16[384,1280]{1,0:T(8,128)(2,1)}, u32[]{:S(2)}, u32[]{:S(2)}) collective-permute-start(bf16[384,1280]{1,0:T(8,128)(2,1)S(1)} %pile.7.refs_0_), channel_id=1, source_target_pairs={{0,4},{1,3},{2,6},{3,1},{4,0},{5,7},{6,2},{7,5},{8,12},{9,11},{10,... | collective-permute-start | bytes 2949128 | tf_op jit(solution)/shard_map/ppermute | solution.py:756
  29.6 12.3 %collective-permute-start.7 = (bf16[48,1920]{1,0:T(8,128)(2,1)S(1)}, bf16[48,1920]{1,0:T(8,128)(2,1)S(1)}, u32[]{:S(2)}, u32[]{:S(2)}) collective-permute-start(bf16[48,1920]{1,0:T(8,128)(2,1)S(1)} %pad_maximum_fusion.4.refs_0_), channel_id=1, source_target_pairs={{0,16},{1,17},{2,18},{3,19},{4,20},{5,21},{6,22},{7,23},{8,24},{9,... | collective-permute-start | bytes 552968 | tf_op jit(solution)/shard_map/ppermute | solution.py:752
  30.5 11.4 %collective-permute-start.8 = (bf16[48,1920]{1,0:T(8,128)(2,1)S(1)}, bf16[48,1920]{1,0:T(8,128)(2,1)S(1)}, u32[]{:S(2)}, u32[]{:S(2)}) collective-permute-start(bf16[48,1920]{1,0:T(8,128)(2,1)S(1)} %pad_maximum_fusion.4.refs_0_), channel_id=1, source_target_pairs={{0,24},{1,25},{2,26},{3,27},{4,28},{5,29},{6,30},{7,31},{8,0},{9,1... | collective-permute-start | bytes 552968 | tf_op jit(solution)/shard_map/ppermute | solution.py:752
  33.9 25.8 %collective-permute-start.6 = (bf16[384,1280]{1,0:T(8,128)(2,1)S(1)}, bf16[384,1280]{1,0:T(8,128)(2,1)}, u32[]{:S(2)}, u32[]{:S(2)}) collective-permute-start(bf16[384,1280]{1,0:T(8,128)(2,1)S(1)} %pile.7.refs_0_), channel_id=1, source_target_pairs={{0,1},{1,0},{2,3},{3,2},{4,5},{5,4},{6,7},{7,6},{8,9},{9,8},{10,11... | collective-permute-start | bytes 2949128 | tf_op jit(solution)/shard_map/ppermute | solution.py:760
  42.6 18.3 %collective-permute-start.9 = (bf16[384,1280]{1,0:T(8,128)(2,1)}, bf16[384,1280]{1,0:T(8,128)(2,1)}, u32[]{:S(2)}, u32[]{:S(2)}) collective-permute-start(bf16[384,1280]{1,0:T(8,128)(2,1)} %collective-permute-done.5.refs_1_), channel_id=1, source_target_pairs={{0,1},{1,0},{2,3},{3,2},{4,5},{5,4},{6,7},{7,6},{8,9},{9,8},{10,11... | collective-permute-start | bytes 2949128 | tf_op jit(solution)/shard_map/ppermute | solution.py:760
  42.7 11.5 %collective-permute-start.10 = (bf16[192,1920]{1,0:T(8,128)(2,1)S(1)}, bf16[192,1920]{1,0:T(8,128)(2,1)S(1)}, u32[]{:S(2)}, u32[]{:S(2)}) collective-permute-start(bf16[192,1920]{1,0:T(8,128)(2,1)S(1)} %pile.8.refs_0_), channel_id=1, source_target_pairs={{0,2},{1,5},{2,0},{3,7},{4,6},{5,1},{6,4},{7,3},{8,10},{9,13},{10,... | collective-permute-start | bytes 2211848 | tf_op jit(solution)/shard_map/ppermute | solution.py:756
  45.5 36.3 %collective-permute-start.13 = (bf16[192,384]{1,0:T(8,128)(2,1)S(1)}, bf16[192,384]{1,0:T(8,128)(2,1)S(1)}, u32[]{:S(2)}, u32[]{:S(2)}) collective-permute-start(bf16[192,384]{1,0:T(8,128)(2,1)S(1)} %constant_dynamic-slice_fusion.refs_0_), channel_id=1, source_target_pairs={{0,8},{1,9},{2,10},{3,11},{4,12},{5,13},{6,14},{7,15},{8,16},{9,17... | collective-permute-start | bytes 442376 | tf_op jit(solution)/shard_map/ppermute | solution.py:752
  47.1 34.7 %collective-permute-start.14 = (bf16[192,384]{1,0:T(8,128)(2,1)S(1)}, bf16[192,384]{1,0:T(8,128)(2,1)S(1)}, u32[]{:S(2)}, u32[]{:S(2)}) collective-permute-start(bf16[192,384]{1,0:T(8,128)(2,1)S(1)} %constant_dynamic-slice_fusion.refs_0_), channel_id=1, source_target_pairs={{0,16},{1,17},{2,18},{3,19},{4,20},{5,21},{6,22},{7,23},{8,24},{9,... | collective-permute-start | bytes 442376 | tf_op jit(solution)/shard_map/ppermute | solution.py:752
  54.2 0.9 copy-start.7
  55.1 26.7 %collective-permute-start.15 = (bf16[192,384]{1,0:T(8,128)(2,1)S(1)}, bf16[192,384]{1,0:T(8,128)(2,1)S(1)}, u32[]{:S(2)}, u32[]{:S(2)}) collective-permute-start(bf16[192,384]{1,0:T(8,128)(2,1)S(1)} %constant_dynamic-slice_fusion.refs_0_), channel_id=1, source_target_pairs={{0,24},{1,25},{2,26},{3,27},{4,28},{5,29},{6,30},{7,31},{8,0},{9,1... | collective-permute-start | bytes 442376 | tf_op jit(solution)/shard_map/ppermute | solution.py:752
  58.4 1.1 copy-start.8
  59.7 2.4 copy-start.4
  59.7 23.4 %collective-permute-start.11 = (bf16[384,1920]{1,0:T(8,128)(2,1)S(1)}, bf16[384,1920]{1,0:T(8,128)(2,1)}, u32[]{:S(2)}, u32[]{:S(2)}) collective-permute-start(bf16[384,1920]{1,0:T(8,128)(2,1)S(1)} %pile.9.refs_4_.refs_0_), channel_id=1, source_target_pairs={{0,4},{1,3},{2,6},{3,1},{4,0},{5,7},{6,2},{7,5},{8,12},{9,11},{10,... | collective-permute-start | bytes 4423688 | tf_op jit(solution)/shard_map/ppermute | solution.py:756
  60.9 22.2 %collective-permute-start.12 = (bf16[384,1920]{1,0:T(8,128)(2,1)S(1)}, bf16[384,1920]{1,0:T(8,128)(2,1)}, u32[]{:S(2)}, u32[]{:S(2)}) collective-permute-start(bf16[384,1920]{1,0:T(8,128)(2,1)S(1)} %pile.9.refs_4_.refs_0_), channel_id=1, source_target_pairs={{0,1},{1,0},{2,3},{3,2},{4,5},{5,4},{6,7},{7,6},{8,9},{9,8},{10,11... | collective-permute-start | bytes 4423688 | tf_op jit(solution)/shard_map/ppermute | solution.py:760
  81.9 1.2 copy-start.2
  81.9 35.1 %collective-permute-start.17 = (bf16[768,384]{1,0:T(8,128)(2,1)S(1)}, bf16[768,384]{1,0:T(8,128)(2,1)S(1)}, u32[]{:S(2)}, u32[]{:S(2)}) collective-permute-start(bf16[768,384]{1,0:T(8,128)(2,1)S(1)} %pile.10.refs_12_.refs_0_), channel_id=1, source_target_pairs={{0,2},{1,5},{2,0},{3,7},{4,6},{5,1},{6,4},{7,3},{8,10},{9,13},{10,... | collective-permute-start | bytes 1769480 | tf_op jit(solution)/shard_map/ppermute | solution.py:756
  83.1 36.2 %collective-permute-start.16 = (bf16[384,1920]{1,0:T(8,128)(2,1)}, bf16[384,1920]{1,0:T(8,128)(2,1)}, u32[]{:S(2)}, u32[]{:S(2)}) collective-permute-start(bf16[384,1920]{1,0:T(8,128)(2,1)} %collective-permute-done.11.refs_10_.refs_1_), channel_id=1, source_target_pairs={{0,1},{1,0},{2,3},{3,2},{4,5},{5,4},{6,7},{7,6},{8,9},{9,8},{10,11... | collective-permute-start | bytes 4423688 | tf_op jit(solution)/shard_map/ppermute | solution.py:760
  117.0 1.1 copy-start.3
  118.2 1.2 copy-start.5
  118.2 33.2 %collective-permute-start.18 = (bf16[1536,384]{1,0:T(8,128)(2,1)S(1)}, bf16[1536,384]{1,0:T(8,128)(2,1)S(1)}, u32[]{:S(2)}, u32[]{:S(2)}) collective-permute-start(bf16[1536,384]{1,0:T(8,128)(2,1)S(1)} %pile.11.refs_4_.refs_0_), channel_id=1, source_target_pairs={{0,4},{1,3},{2,6},{3,1},{4,0},{5,7},{6,2},{7,5},{8,12},{9,11},{10,... | collective-permute-start | bytes 3538952 | tf_op jit(solution)/shard_map/ppermute | solution.py:756
  119.4 33.5 %collective-permute-start.19 = (bf16[1536,384]{1,0:T(8,128)(2,1)S(1)}, bf16[1536,384]{1,0:T(8,128)(2,1)S(1)}, u32[]{:S(2)}, u32[]{:S(2)}) collective-permute-start(bf16[1536,384]{1,0:T(8,128)(2,1)S(1)} %pile.11.refs_4_.refs_0_), channel_id=1, source_target_pairs={{0,1},{1,0},{2,3},{3,2},{4,5},{5,4},{6,7},{7,6},{8,9},{9,8},{10,11... | collective-permute-start | bytes 3538952 | tf_op jit(solution)/shard_map/ppermute | solution.py:760
  119.4 32.7 %copy-start.18 = (s32[2,2,512]{2,1,0:T(2,128)S(1)}, s32[2,2,512]{2,1,0:T(2,128)}, u32[]{:S(2)}) copy-start(s32[2,2,512]{2,1,0:T(2,128)} %param.19) | copy-start | bytes 24580
  151.5 3.2 copy-start.19
  151.5 3.2 collective-permute-start.20
  152.9 1.8 copy-start.20
  216.6 25.8 %collective-permute-start.21 = (bf16[768,3072]{1,0:T(8,128)(2,1)}, bf16[768,3072]{1,0:T(8,128)(2,1)}, u32[]{:S(2)}, u32[]{:S(2)}) collective-permute-start(bf16[768,3072]{1,0:T(8,128)(2,1)} %get-tuple-element.100), channel_id=1, source_target_pairs={{0,1},{1,0},{2,3},{3,2},{4,5},{5,4},{6,7},{7,6},{8,9},{9,8},{10,11... | collective-permute-start | bytes 14155784 | tf_op jit(solution)/shard_map/ppermute | solution.py:760
  217.0 24.5 %copy-start.15 = (f32[8,3072]{1,0:T(8,128)S(1)}, f32[8,3072]{1,0:T(8,128)}, u32[]{:S(2)}) copy-start(f32[8,3072]{1,0:T(8,128)} %get-tuple-element.105) | copy-start | bytes 294916
  248.6 30.9 %collective-permute-start.22 = (bf16[384,3072]{1,0:T(8,128)(2,1)}, bf16[384,3072]{1,0:T(8,128)(2,1)}, u32[]{:S(2)}, u32[]{:S(2)}) collective-permute-start(bf16[384,3072]{1,0:T(8,128)(2,1)} %get-tuple-element.123.refs_1_), channel_id=1, source_target_pairs={{0,2},{1,5},{2,0},{3,7},{4,6},{5,1},{6,4},{7,3},{8,10},{9,13},{10,... | collective-permute-start | bytes 7077896 | tf_op jit(solution)/shard_map/ppermute | solution.py:756
  249.7 29.7 %copy-start.9 = (bf16[384,3072]{1,0:T(8,128)(2,1)S(1)}, bf16[384,3072]{1,0:T(8,128)(2,1)}, u32[]{:S(2)}) copy-start(bf16[384,3072]{1,0:T(8,128)(2,1)} %get-tuple-element.124.refs_0_) | copy-start | bytes 7077892
  283.0 1.0 copy-start.13
  283.0 17.7 %collective-permute-start.23 = (bf16[192,3072]{1,0:T(8,128)(2,1)S(1)}, bf16[192,3072]{1,0:T(8,128)(2,1)S(1)}, u32[]{:S(2)}, u32[]{:S(2)}) collective-permute-start(bf16[192,3072]{1,0:T(8,128)(2,1)S(1)} %get-tuple-element.127.refs_1_), channel_id=1, source_target_pairs={{0,4},{1,3},{2,6},{3,1},{4,0},{5,7},{6,2},{7,5},{8,12},{9,11},{10,... | collective-permute-start | bytes 3538952 | tf_op jit(solution)/shard_map/ppermute | solution.py:756
  284.0 16.8 %copy-start.10 = (bf16[192,3072]{1,0:T(8,128)(2,1)S(1)}, bf16[192,3072]{1,0:T(8,128)(2,1)}, u32[]{:S(2)}) copy-start(bf16[192,3072]{1,0:T(8,128)(2,1)} %get-tuple-element.128.refs_0_) | copy-start | bytes 3538948
  300.7 5.2 %copy-start.12 = (bf16[192,3072]{1,0:T(8,128)(2,1)}, bf16[192,3072]{1,0:T(8,128)(2,1)S(1)}, u32[]{:S(2)}) copy-start(bf16[192,3072]{1,0:T(8,128)(2,1)S(1)} %collective-permute-done.23) | copy-start | bytes 3538948
  300.8 5.2 %collective-permute-start.24 = (bf16[768,1664]{1,0:T(8,128)(2,1)}, bf16[768,1664]{1,0:T(8,128)(2,1)}, u32[]{:S(2)}, u32[]{:S(2)}) collective-permute-start(bf16[768,1664]{1,0:T(8,128)(2,1)} %get-tuple-element.109), channel_id=1, source_target_pairs={{0,1},{1,0},{2,3},{3,2},{4,5},{5,4},{6,7},{7,6},{8,9},{9,8},{10,11... | collective-permute-start | bytes 7667720 | tf_op jit(solution)/shard_map/ppermute | solution.py:760
  300.9 5.1 %copy-start.11 = (bf16[768,1664]{1,0:T(8,128)(2,1)S(1)}, bf16[768,1664]{1,0:T(8,128)(2,1)}, u32[]{:S(2)}) copy-start(bf16[768,1664]{1,0:T(8,128)(2,1)} %get-tuple-element.107) | copy-start | bytes 7667716
  302.0 7.3 %copy-start.14 = (bf16[48,3072]{1,0:T(8,128)(2,1)}, bf16[48,3072]{1,0:T(8,128)(2,1)S(1)}, u32[]{:S(2)}) copy-start(bf16[48,3072]{1,0:T(8,128)(2,1)S(1)} %get-tuple-element.131.refs_4_) | copy-start | bytes 884740
  302.0 21.5 %collective-permute-start.32 = (bf16[48,3072]{1,0:T(8,128)(2,1)}, bf16[48,3072]{1,0:T(8,128)(2,1)S(1)}, u32[]{:S(2)}, u32[]{:S(2)}) collective-permute-start(bf16[48,3072]{1,0:T(8,128)(2,1)} %get-tuple-element.133.refs_2_), channel_id=1, source_target_pairs={{0,8},{1,9},{2,10},{3,11},{4,12},{5,13},{6,14},{7,15},{8,16},{9,17... | collective-permute-start | bytes 884744 | tf_op jit(solution)/shard_map/ppermute | solution.py:791
  302.0 23.6 %collective-permute-start.33 = (bf16[48,3072]{1,0:T(8,128)(2,1)}, bf16[48,3072]{1,0:T(8,128)(2,1)S(1)}, u32[]{:S(2)}, u32[]{:S(2)}) collective-permute-start(bf16[48,3072]{1,0:T(8,128)(2,1)} %get-tuple-element.132.refs_3_), channel_id=1, source_target_pairs={{0,16},{1,17},{2,18},{3,19},{4,20},{5,21},{6,22},{7,23},{8,24},{9,... | collective-permute-start | bytes 884744 | tf_op jit(solution)/shard_map/ppermute | solution.py:791
  302.6 23.0 %collective-permute-start.34 = (bf16[48,3072]{1,0:T(8,128)(2,1)S(1)}, bf16[48,3072]{1,0:T(8,128)(2,1)S(1)}, u32[]{:S(2)}, u32[]{:S(2)}) collective-permute-start(bf16[48,3072]{1,0:T(8,128)(2,1)S(1)} %get-tuple-element.131.refs_4_), channel_id=1, source_target_pairs={{0,24},{1,25},{2,26},{3,27},{4,28},{5,29},{6,30},{7,31},{8,0},{9,1... | collective-permute-start | bytes 884744 | tf_op jit(solution)/shard_map/ppermute | solution.py:791
  309.4 18.1 %collective-permute-start.25 = (bf16[384,1664]{1,0:T(8,128)(2,1)}, bf16[384,1664]{1,0:T(8,128)(2,1)}, u32[]{:S(2)}, u32[]{:S(2)}) collective-permute-start(bf16[384,1664]{1,0:T(8,128)(2,1)} %get-tuple-element.126.refs_0_), channel_id=1, source_target_pairs={{0,2},{1,5},{2,0},{3,7},{4,6},{5,1},{6,4},{7,3},{8,10},{9,13},{10,... | collective-permute-start | bytes 3833864 | tf_op jit(solution)/shard_map/ppermute | solution.py:756
  326.9 21.7 %collective-permute-start.36 = (f32[192,384]{1,0:T(8,128)S(1)}, f32[192,384]{1,0:T(8,128)S(1)}, u32[]{:S(2)}, u32[]{:S(2)}) collective-permute-start(f32[192,384]{1,0:T(8,128)S(1)} %pad_maximum_fusion.3), channel_id=1, source_target_pairs={{0,1},{1,0},{2,3},{3,2},{4,5},{5,4},{6,7},{7,6},{8,9},{9,8},{10,11... | collective-permute-start | bytes 884744 | tf_op jit(solution)/shard_map/ppermute | solution.py:809
  327.0 3.1 collective-permute-start.35
  329.0 10.5 %collective-permute-start.26 = (bf16[192,1664]{1,0:T(8,128)(2,1)S(1)}, bf16[192,1664]{1,0:T(8,128)(2,1)S(1)}, u32[]{:S(2)}, u32[]{:S(2)}) collective-permute-start(bf16[192,1664]{1,0:T(8,128)(2,1)S(1)} %get-tuple-element.130), channel_id=1, source_target_pairs={{0,4},{1,3},{2,6},{3,1},{4,0},{5,7},{6,2},{7,5},{8,12},{9,11},{10,... | collective-permute-start | bytes 1916936 | tf_op jit(solution)/shard_map/ppermute | solution.py:756
  339.6 11.1 %collective-permute-start.27 = (bf16[48,1664]{1,0:T(8,128)(2,1)S(1)}, bf16[48,1664]{1,0:T(8,128)(2,1)S(1)}, u32[]{:S(2)}, u32[]{:S(2)}) collective-permute-start(bf16[48,1664]{1,0:T(8,128)(2,1)S(1)} %get-tuple-element.135), channel_id=1, source_target_pairs={{0,8},{1,9},{2,10},{3,11},{4,12},{5,13},{6,14},{7,15},{8,16},{9,17... | collective-permute-start | bytes 479240 | tf_op jit(solution)/shard_map/ppermute | solution.py:791
  346.1 10.2 %collective-permute-start.28 = (bf16[48,1664]{1,0:T(8,128)(2,1)S(1)}, bf16[48,1664]{1,0:T(8,128)(2,1)S(1)}, u32[]{:S(2)}, u32[]{:S(2)}) collective-permute-start(bf16[48,1664]{1,0:T(8,128)(2,1)S(1)} %get-tuple-element.137), channel_id=1, source_target_pairs={{0,16},{1,17},{2,18},{3,19},{4,20},{5,21},{6,22},{7,23},{8,24},{9,... | collective-permute-start | bytes 479240 | tf_op jit(solution)/shard_map/ppermute | solution.py:791
  346.5 9.9 %collective-permute-start.29 = (bf16[48,1664]{1,0:T(8,128)(2,1)S(1)}, bf16[48,1664]{1,0:T(8,128)(2,1)S(1)}, u32[]{:S(2)}, u32[]{:S(2)}) collective-permute-start(bf16[48,1664]{1,0:T(8,128)(2,1)S(1)} %get-tuple-element.136), channel_id=1, source_target_pairs={{0,24},{1,25},{2,26},{3,27},{4,28},{5,29},{6,30},{7,31},{8,0},{9,1... | collective-permute-start | bytes 479240 | tf_op jit(solution)/shard_map/ppermute | solution.py:791
  348.6 11.6 %copy-start.1 = (bf16[48,3072]{1,0:T(8,128)(2,1)S(1)}, bf16[48,3072]{1,0:T(8,128)(2,1)}, u32[]{:S(2)}) copy-start(bf16[48,3072]{1,0:T(8,128)(2,1)} %param.29) | copy-start | bytes 884740
  356.6 2.1 collective-permute-start.31
  356.6 2.8 collective-permute-start.30
